TPU v7x, 32 devices: a whole 2x2x4 slice. The times are simulated.
32 devices in a mesh: shot: 2 (over y), row: 4 (over x, core), freq: 4 (over z).
Axes of the slice: x: 2, y: 2, z: 4, core: 2. Of those that a mesh axis runs over, the one named last changes fastest.
Arguments:
- source_field: float32 [2, 8, 1024, 1024], P(None, ('shot', 'freq'), 'row'), parts along dimension 1, may hold values from -6 to 6
- receiver_field: float32 [2, 8, 1024, 1024], P(None, ('shot', 'freq'), 'row'), parts along dimension 1, may hold values from -6 to 6
- slowness: float32 [4, 1024, 1024], P('freq', 'row'), may hold values from 0.22 to 0.67
- owner: int32 [4], replicated, may hold values from 0 to 3, each once
- freq_index: int32 [8], P(('shot', 'freq')), parts along dimension 0, may hold values from 0 to 3, each once
Outputs:
- source_out: float32 [2, 8, 1024, 1024], P(None, ('shot', 'freq'), 'row'), parts along dimension 1
- receiver_out: float32 [2, 8, 1024, 1024], P(None, ('shot', 'freq'), 'row'), parts along dimension 1
- image: float32 [4, 1024, 1024], P('shot', 'row', 'freq'), parts along dimension 0
There are 2 independent parts, one for each index of `shot`. A program takes and returns all parts, laid end to end along the dimension named above; an argument that names none is the same for every part. Nothing has to cross between parts.
All inputs are finite; a program needn't handle non-finite values.
Results may differ from a plain program's by a relative error of at most 0.00022.
Values sent between devices are 32-bit elements; how exact they have to be, the bound alone decides.
No kernel may reach another device: no remote copies, remote signals or barrier semaphores. Data moves between devices by JAX's collectives and lax.ppermute only.
A program may use at most 128 MiB of HBM per device.

v0:
```python
import math

import jax
import jax.numpy as jnp
from jax import lax
from jax.sharding import PartitionSpec as P

NZ = 2


dz_km = 0.01
dx_km = 0.0125
ref_slow = 0.5
base_hertz = 3.0
step_hertz = 4.0
taper = 0.5


def spread(value, axis, source):
    kept = jnp.where(lax.axis_index(axis) == source, value, 0).astype(value.dtype)
    return lax.psum(kept, axis)


def split_length(length):
    return length // 128


def angle_table(count_a, count_b, modulus, sign):
    left = jnp.arange(count_a, dtype=jnp.int32)[:, None]
    right = jnp.arange(count_b, dtype=jnp.int32)[None, :]
    turns = (left * right % modulus).astype(jnp.float32) * (2.0 * math.pi / modulus)
    return (jnp.cos(turns), sign * jnp.sin(turns))


def contract(form, left, right):
    return jnp.einsum(form, left, right, precision=lax.Precision.HIGHEST)


def transform_pair(real_part, imag_part, sign, last):
    length = real_part.shape[2] if last else real_part.shape[1]
    first = split_length(length)
    second = length // first
    cos_a, sin_a = angle_table(first, first, first, sign)
    cos_b, sin_b = angle_table(second, second, second, sign)
    twist_c, twist_s = angle_table(first, second, length, sign)
    if last:
        shape = (real_part.shape[0], real_part.shape[1], first, second)
        form_one = "fajb,jk->fakb"
        form_two = "fakb,bm->famk"
    else:
        shape = (real_part.shape[0], first, second, real_part.shape[2])
        form_one = "fjbq,jk->fkbq"
        form_two = "fkbq,bm->fmkq"
        twist_c = twist_c[:, :, None]
        twist_s = twist_s[:, :, None]
    x_re = real_part.reshape(shape)
    x_im = imag_part.reshape(shape)
    y_re = contract(form_one, x_re, cos_a) - contract(form_one, x_im, sin_a)
    y_im = contract(form_one, x_im, cos_a) + contract(form_one, x_re, sin_a)
    z_re = y_re * twist_c - y_im * twist_s
    z_im = y_im * twist_c + y_re * twist_s
    out_re = contract(form_two, z_re, cos_b) - contract(form_two, z_im, sin_b)
    out_im = contract(form_two, z_im, cos_b) + contract(form_two, z_re, sin_b)
    return (out_re.reshape(real_part.shape), out_im.reshape(real_part.shape))


def transform(block, sign, last):
    count = block.shape[0]
    freqs = block.shape[2]
    plane = block.shape[3:]
    real_part = block[:, 0].reshape((count * freqs,) + plane)
    imag_part = block[:, 1].reshape((count * freqs,) + plane)
    out_re, out_im = transform_pair(real_part, imag_part, sign, last)
    shape = (count, freqs) + plane
    return jnp.stack([out_re.reshape(shape), out_im.reshape(shape)], axis=1)


def wavenumbers(length, start, count):
    index = start + jnp.arange(count, dtype=jnp.int32)
    signed = jnp.where(index * 2 < length, index, index - length)
    return signed.astype(jnp.float32) * (2.0 * math.pi / (length * dx_km))


def rotate(block, cos_v, sin_v):
    real_part = block[:, 0]
    imag_part = block[:, 1]
    return jnp.stack(
        [real_part * cos_v - imag_part * sin_v, imag_part * cos_v + real_part * sin_v], axis=1
    )


def shift_phase(block, omega, kx_part, ky_part, total):
    square = kx_part[:, None] ** 2 + ky_part[None, :] ** 2
    kmax = math.pi / dx_km
    damp = jnp.exp(-taper * square / (kmax * kmax)) / total
    ws0 = omega[:, None, None] * ref_slow
    vertical = ws0 - 0.5 * square[None] / ws0
    cos_v = jnp.cos(dz_km * vertical) * damp
    sin_v = jnp.sin(dz_km * vertical) * damp
    return rotate(block, cos_v, sin_v)


def correct(block, slab, omega):
    theta = omega[:, None, None] * (slab[None] - ref_slow) * dz_km
    return rotate(block, jnp.cos(theta), jnp.sin(theta))


def image_term(block):
    return jnp.sum(block[0, 0] * block[1, 0] - block[0, 1] * block[1, 1], axis=0)


def body(source_field, receiver_field, slowness, owner, freq_index):
    rows = source_field.shape[2]
    width = source_field.shape[3]
    row_count = lax.axis_size("row")
    height = rows * row_count
    cols = width // row_count
    place = lax.axis_index("row")
    omega = 2.0 * math.pi * (base_hertz + step_hertz * freq_index.astype(jnp.float32))
    mirrored = jnp.stack([receiver_field[0], -receiver_field[1]])
    fields = jnp.stack([source_field, mirrored])
    kx_all = wavenumbers(height, 0, height)
    ky_own = wavenumbers(width, place * cols, cols)
    total = float(height * width)
    slab_dev = slowness.shape[0]
    images = []
    for depth in range(NZ):
        chosen = owner[depth]
        held = spread(slowness, "freq", chosen // slab_dev)
        slab = lax.dynamic_index_in_dim(held, chosen % slab_dev, 0, keepdims=False)
        fields = transform(fields, -1.0, True)
        fields = lax.all_to_all(fields, "row", split_axis=4, concat_axis=3, tiled=True)
        items = fields
        items = transform(items, -1.0, False)
        items = shift_phase(items, omega, kx_all, ky_own, total)
        fields = transform(items, 1.0, False)
        fields = lax.all_to_all(fields, "row", split_axis=3, concat_axis=4, tiled=True)
        fields = transform(fields, 1.0, True)
        fields = correct(fields, slab, omega)
        images.append(image_term(fields))
    parts = [lax.psum_scatter(term, "freq", scatter_dimension=1, tiled=True) for term in images]
    image = jnp.stack(parts)
    source_out = fields[0]
    receiver_out = jnp.stack([fields[1, 0], -fields[1, 1]])
    return (source_out, receiver_out, image)


def solution(mesh):
    in_specs = (
        P(None, ("shot", "freq"), "row", None),
        P(None, ("shot", "freq"), "row", None),
        P("freq", "row", None),
        P(),
        P(("shot", "freq")),
    )
    out_specs = (
        P(None, ("shot", "freq"), "row", None),
        P(None, ("shot", "freq"), "row", None),
        P("shot", "row", "freq"),
    )
    return jax.shard_map(body, mesh=mesh, in_specs=in_specs, out_specs=out_specs, check_vma=False)
```

profile of v0, /device:TPU:0, one launch (start us, length us, event | category | flops | bytes accessed | tf_op | source)
XLA Modules:
  0.0 596.2 jit_solution(643073891319918496)
XLA Ops:
  20.3 2.7 fusion.112
  32.7 5.4 copy.346
  38.1 4.9 all-to-all-start
  44.0 4.0 fusion.186
  48.1 43.7 %all-to-all-done = f32[2,2,1,256,1024]{3,0,2,1,4:T(2,128)} async-done(((f32[2,2,1,256,1024]{3,0,2,1,4:T(2,128)}), f32[2,2,1,256,1024]{3,0,2,1,4:T(2,128)}, u32[]{:S(2)}, u32[]{:S(2)}) %all-to-all-start) | async-done | bytes 4194336 | tf_op jit(solution)/shard_map/all_to_all | solution.py:132
  91.8 5.0 copy.347
  96.7 5.4 copy.348
  104.7 2.9 fusion.104
  107.6 2.9 fusion.102
  110.5 2.9 fusion.118
  113.4 3.8 subtract_bitcast_fusion.13
  122.4 2.6 subtract_bitcast_fusion.12
  126.3 2.6 add_bitcast_fusion.12
  131.0 2.9 fusion.88
  133.9 2.9 fusion.86
  136.8 3.0 fusion.124
  139.8 3.9 subtract_bitcast_fusion.11
  143.7 2.6 fusion.80
  148.9 2.6 subtract_bitcast_fusion.10
  152.8 2.8 add_bitcast_fusion.10
  157.1 5.2 copy.372
  162.4 5.0 all-to-all-start.1
  171.0 90.0 %all-reduce.3.cloned.1.call-done = (f32[1,256,1024]{2,1,0:T(8,128)}, f32[1,256,1024]{2,1,0:T(8,128)}) async-done(((f32[1,256,1024]{2,1,0:T(8,128)}, f32[1,256,1024]{2,1,0:T(8,128)}), (f32[1,256,1024]{2,1,0:T(8,128)}, f32[1,256,1024]{2,1,0:T(8,128)})) %all-reduce.3.cloned.1.call-update) | async-done | bytes 2097168 | tf_op jit(solution)/shard_map/psum | solution.py:21
  260.9 4.7 fusion.192
  268.6 5.0 copy.373
  273.6 5.3 copy.374
  278.9 4.6 fusion.663
  285.6 3.2 fusion.318
  301.9 2.8 subtract_bitcast_fusion.8
  312.5 2.9 copy.386
  315.4 4.8 fusion.314
  320.2 3.1 copy.385
  323.3 3.6 fusion.316
  343.5 3.2 copy.395
  346.8 50.7 %all_to_all.72 = f32[2,2,1,256,1024]{3,0,2,1,4:T(2,128)S(1)} all-to-all(f32[2,2,1,256,1024]{3,0,2,1,4:T(2,128)S(1)} %copy.395), channel_id=1, replica_groups=mesh['shot'=2,'row'=4,'freq'=4] {'row'}, dimensions={4} | all-to-all | bytes 8388608 | tf_op jit(solution)/shard_map/all_to_all | solution.py:132
  397.5 2.7 copy.396
  400.3 5.7 copy.397
  408.5 2.9 fusion.56
  411.4 2.9 fusion.54
  414.3 2.9 fusion.130
  417.2 3.6 subtract_bitcast_fusion.5
  426.0 2.6 subtract_bitcast_fusion.4
  429.8 2.6 add_bitcast_fusion.4
  434.6 2.9 fusion.40
  437.5 2.9 fusion.38
  440.3 3.0 fusion.136
  443.4 4.0 subtract_bitcast_fusion.3
  447.4 2.6 fusion.32
  452.5 2.6 subtract_bitcast_fusion.2
  456.4 2.8 add_bitcast_fusion.2
  460.8 5.2 copy.418
  466.0 4.9 all-to-all-start.3
  471.0 2.6 copy.436
  474.9 5.7 cosine_bitcast_fusion
  484.7 4.7 fusion.10
  490.7 28.5 %all-to-all-done.3 = f32[2,2,1,1024,256]{4,0,2,1,3:T(2,128)} async-done(((f32[2,2,1,1024,256]{4,0,2,1,3:T(2,128)}), f32[2,2,1,1024,256]{4,0,2,1,3:T(2,128)}, u32[]{:S(2)}, u32[]{:S(2)}) %all-to-all-start.3) | async-done | bytes 4194336 | tf_op jit(solution)/shard_map/all_to_all | solution.py:137
  519.2 5.0 copy.419
  524.2 5.3 copy.420
  529.4 4.6 fusion.661
  536.1 3.2 fusion.306
  562.1 3.0 pad_maximum_fusion.6
  565.1 3.0 copy.444
  568.1 4.3 fusion.14
  574.3 13.1 %reduce-scatter.5.cloned.1.call-done = f32[256,256]{0,1:T(8,128)} async-done(((f32[256,1024]{0,1:T(8,128)}), f32[256,256]{0,1:T(8,128)}) %reduce-scatter.5.cloned.1.call-update) | async-done | bytes 262160 | tf_op jit(solution)/shard_map/reduce_scatter | solution.py:141
  (137 shorter events, 135.5 us)
Async XLA Ops:
  8.9 1.6 copy-start.19
  38.1 53.7 %all-to-all-start = ((f32[2,2,1,256,1024]{3,0,2,1,4:T(2,128)}), f32[2,2,1,256,1024]{3,0,2,1,4:T(2,128)}, u32[]{:S(2)}, u32[]{:S(2)}) async-start(f32[2,2,1,256,1024]{3,0,2,1,4:T(2,128)} %copy.346), calls=%async_computation | async-start | bytes 8388608 | tf_op jit(solution)/shard_map/all_to_all | solution.py:132
  48.1 82.2 %copy-start.8 = (f32[8,128,256]{2,1,0:T(8,128)}, f32[8,128,256]{2,1,0:T(8,128)S(1)}, u32[]{:S(2)}) copy-start(f32[8,128,256]{2,1,0:T(8,128)S(1)} %get-tuple-element.67) | copy-start | bytes 3145732
  162.4 5.1 copy-start.21
  162.4 7.0 %copy-start.20 = (f32[1,256,1024]{2,1,0:T(8,128)S(1)}, f32[1,256,1024]{2,1,0:T(8,128)}, u32[]{:S(2)}) copy-start(f32[1,256,1024]{2,1,0:T(8,128)} %param.7) | copy-start | bytes 3145732
  162.4 106.2 %all-to-all-start.1 = ((f32[2,2,1,1024,256]{4,0,2,1,3:T(2,128)}), f32[2,2,1,1024,256]{4,0,2,1,3:T(2,128)}, u32[]{:S(2)}, u32[]{:S(2)}) async-start(f32[2,2,1,1024,256]{4,0,2,1,3:T(2,128)} %copy.372), calls=%async_computation.1 | async-start | bytes 8388608 | tf_op jit(solution)/shard_map/all_to_all | solution.py:137
  167.4 93.5 %all-reduce.3.cloned.1.call-start = ((), (), s32[]{:S(2)}) async-start(), calls=%async_computation.8 | async-start | bytes 4194304 | tf_op jit(solution)/shard_map/psum | solution.py:21
  265.7 2.9 copy-start.11
  265.7 2.9 copy-start.13
  285.6 3.2 copy-start.6
  291.1 1.9 copy-start.14
  293.0 2.0 copy-start.7
  307.1 1.3 copy-start.1
  308.4 1.2 copy-start.17
  308.4 1.5 copy-start.18
  323.2 3.6 copy-start.2
  323.3 3.6 copy-start.15
  326.9 2.0 copy-start.5
  432.6 1.2 copy-start.9
  466.0 53.1 %all-to-all-start.3 = ((f32[2,2,1,1024,256]{4,0,2,1,3:T(2,128)}), f32[2,2,1,1024,256]{4,0,2,1,3:T(2,128)}, u32[]{:S(2)}, u32[]{:S(2)}) async-start(f32[2,2,1,1024,256]{4,0,2,1,3:T(2,128)} %copy.418), calls=%async_computation.3 | async-start | bytes 8388608 | tf_op jit(solution)/shard_map/all_to_all | solution.py:137
  470.9 2.7 copy-start.12
  470.9 103.4 %reduce-scatter.3.cloned.1.call-start = ((), (), s32[]{:S(2)}) async-start(), calls=%async_computation.6 | async-start | bytes 1310720 | tf_op jit(solution)/shard_map/reduce_scatter | solution.py:141
  490.7 96.8 %reduce-scatter.5.cloned.1.call-start = ((), (), s32[]{:S(2)}) async-start(), calls=%async_computation.7 | async-start | bytes 1310720 | tf_op jit(solution)/shard_map/reduce_scatter | solution.py:141
  536.1 3.2 copy-start.3
  541.8 1.9 copy-start.16
  543.7 2.0 copy-start.4
  555.2 2.3 copy-start.10
  557.5 2.5 copy-start
Sparse Core Ops, SparseCore 0:
  171.2 89.6 all-reduce.2
  490.8 26.5 reduce-scatter.2
  562.2 25.1 reduce-scatter.4
where the time goes:
time: 606 us; the launch traced here: 596 us
  waiting for transfers between devices  175 us (29%)
  matrix products  170 us (28%)
  local copies, waits for them, and re-layouts  125 us (21%)
  blocking collectives  50.7 us (8%)
  other arithmetic  42.9 us (7%)
  between operations  17.4 us (3%)
  starting transfers between devices  14.9 us (2%)
    dot_general x64, matrix products, contract(): return jnp.einsum(form, left, right, precision=lax.Precision.HIGHEST)  170 us
    psum x1, waiting for transfers between devices, spread(): return lax.psum(kept, axis)  90 us
    all_to_all x1, blocking collectives, body(): lax.all_to_all(fields, 'row', split_axis=4, concat_axis=3, tiled=True)  50.7 us
    all_to_all x1, waiting for transfers between devices, body(): lax.all_to_all(fields, 'row', split_axis=4, concat_axis=3, tiled=True)  43.7 us
    all_to_all x2, waiting for transfers between devices, body(): lax.all_to_all(fields, 'row', split_axis=3, concat_axis=4, tiled=True)  28.5 us
    all_to_all x4, local copies, waits for them, and re-layouts, body(): lax.all_to_all(fields, 'row', split_axis=3, concat_axis=4, tiled=True)  20.5 us
    another operation x4, local copies, waits for them, and re-layouts, transform(): return jnp.stack([out_re.reshape(shape), out_im.reshape(shape)], axis=1)  19.1 us
    all_to_all x4, local copies, waits for them, and re-layouts, body(): lax.all_to_all(fields, 'row', split_axis=4, concat_axis=3, tiled=True)  18.9 us
  transfers between devices with their start and end apart: 6, of which 4 were waited for; matrix products, arithmetic and copies ran while one was open for 15% of the time, Pallas kernels for 0%

commit v1 on v0

v1 whole, which is shorter than its diff:
```python
import math

import jax
import jax.numpy as jnp
import numpy as np
from jax import lax
from jax.experimental import pallas as pl
from jax.experimental.pallas import tpu as pltpu
from jax.sharding import PartitionSpec as P

NZ = 2

dz_km = 0.01
dx_km = 0.0125
ref_slow = 0.5
base_hertz = 3.0
step_hertz = 4.0
taper = 0.5

RADIX = 4
LIMIT = 48 * 1024 * 1024
F32 = jnp.float32
BF16 = jnp.bfloat16


def params():
    return pltpu.CompilerParams(vmem_limit_bytes=LIMIT)


def whole(shape):
    return pl.BlockSpec(shape, lambda *_: (0,) * len(shape))


def omega_of(slot):
    return 2.0 * math.pi * (base_hertz + step_hertz * slot.astype(F32))


def add(a, b):
    return (a[0] + b[0], a[1] + b[1])


def sub(a, b):
    return (a[0] - b[0], a[1] - b[1])


def add_i(a, b):
    return (a[0] - b[1], a[1] + b[0])


def sub_i(a, b):
    return (a[0] + b[1], a[1] - b[0])


def spread_blocks(x):
    even, odd = add(x[0], x[2]), add(x[1], x[3])
    plus, minus = sub(x[0], x[2]), sub(x[1], x[3])
    return [add(even, odd), sub_i(plus, minus), sub(even, odd), add_i(plus, minus)]


def join_blocks(y):
    even, odd = add(y[0], y[2]), add(y[1], y[3])
    plus, minus = sub(y[0], y[2]), sub(y[1], y[3])
    return [add(even, odd), add_i(plus, minus), sub(even, odd), sub_i(plus, minus)]


def halves(x):
    high = x.astype(BF16)
    return high, (x - high.astype(F32)).astype(BF16)


def dot(a, b):
    return jnp.dot(a, b, preferred_element_type=F32)


def times_right(x, high, low):
    xr, xi = halves(x[0]), halves(x[1])
    out = []
    for left, right, sign in ((xr, xi, -1), (xi, xr, 1)):
        a = jnp.concatenate([left[0], right[0] * sign], axis=1)
        b = jnp.concatenate([left[1], right[1] * sign], axis=1)
        out.append(dot(a, high) + dot(a, low) + dot(b, high))
    return tuple(out)


def times_left(x, high, low):
    xr, xi = halves(x[0]), halves(x[1])
    size = high.shape[1]
    lead_h = jnp.concatenate([high[:size], high[size:]], axis=1)
    lead_l = jnp.concatenate([low[:size], low[size:]], axis=1)
    out = []
    for left, right, sign in ((xr, xi, -1), (xi, xr, 1)):
        a = jnp.concatenate([left[0], right[0] * sign], axis=0)
        b = jnp.concatenate([left[1], right[1] * sign], axis=0)
        out.append(dot(lead_h, a) + dot(lead_l, a) + dot(lead_h, b))
    return tuple(out)


def convolve(x, high_ref, low_ref, left):
    times = times_left if left else times_right
    x = spread_blocks(x)
    at = [k if left else (RADIX - k) % RADIX for k in range(RADIX)]
    return join_blocks([times(x[k], high_ref[at[k]], low_ref[at[k]]) for k in range(RADIX)])


def phase_parts(theta):
    q = theta * theta
    sin_v = theta * (1.0 + q * (-1 / 6 + q * (1 / 120 + q * (-1 / 5040 + q * (1 / 362880)))))
    cos_v = 1.0 + q * (-0.5 + q * (1 / 24 + q * (-1 / 720 + q * (1 / 40320 - q * (1 / 3628800)))))
    return cos_v, sin_v


def rotate(x, cos_v, sin_v):
    return (x[0] * cos_v - x[1] * sin_v, x[1] * cos_v + x[0] * sin_v)


def cosine_table(length):
    k = np.arange(length // 2)[:, None]
    n = np.arange(length)[None, :]
    table = np.cos(2.0 * math.pi * ((k * n) % length) / length) * np.where(k == 0, 1.0, 2.0)
    return jnp.asarray(table / length, F32)


def propagator(omega, m, length):
    ws0 = omega * ref_slow
    wave = m * (2.0 * math.pi / (length * dx_km))
    square = wave * wave
    kmax = math.pi / dx_km
    damp = jnp.exp(-taper * square / (kmax * kmax))
    phase = dz_km * (0.5 * ws0 - 0.5 * square / ws0)
    return damp * jnp.cos(phase), damp * jnp.sin(phase)


def make_blocks(omega, table_ref, high_ref, low_ref):
    half, length = table_ref.shape
    block = length // RADIX
    m = lax.broadcasted_iota(jnp.int32, (8, half), 1).astype(F32)
    g = propagator(omega, m, length)
    g = tuple(jnp.transpose(part) for part in g)
    lane = lax.broadcasted_iota(jnp.int32, (8, length), 1)
    row = lax.broadcasted_iota(jnp.int32, (8, length), 0)
    last = propagator(omega, jnp.full((8, length), half, F32), length)
    flip = jnp.where(lane % 2 == 0, 1.0, -1.0) / length
    flip = jnp.where(row == 0, flip, 0.0)
    total = [part * flip for part in last]
    for j in range(half // 8):
        here = table_ref[pl.ds(8 * j, 8), :]
        for c in range(2):
            total[c] = total[c] + here * g[c][8 * j : 8 * j + 8, 0:1]
    rows = []
    for c in range(2):
        line = jnp.sum(total[c], axis=0, keepdims=True) * (1.0 / RADIX)
        rows.append(
            pltpu.roll(jnp.broadcast_to(line, (block, length)), 0, 1, stride=1, stride_axis=0)
        )
    parts = [tuple(r[:, e * block : (e + 1) * block] for r in rows) for e in range(RADIX)]
    for k, value in enumerate(join_blocks(parts)):
        for c in range(2):
            high, low = halves(value[c])
            high_ref[k, pl.ds(c * block, block), :] = high
            low_ref[k, pl.ds(c * block, block), :] = low


def pick(ref_value, swap):
    return (ref_value[1], ref_value[0]) if swap else (ref_value[0], ref_value[1])


def store(ref, value, swap):
    ref[0], ref[1] = (value[1], value[0]) if swap else (value[0], value[1])


def first_kernel(form, shift_ref, slot_ref, *refs):
    fields, refs = refs[:RADIX], refs[RADIX:]
    if form:
        table_ref, refs = refs[0], refs[1:]
        outs, (high_ref, low_ref) = refs[:RADIX], refs[RADIX:]

        @pl.when(pl.program_id(0) == 0)
        def _():
            make_blocks(omega_of(slot_ref[0]), table_ref, high_ref, low_ref)

    else:
        (high_ref, low_ref), outs = refs[:2], refs[2:]
    x = [pick(f[:, 0], not form) for f in fields]
    for ref, value in zip(outs, convolve(x, high_ref, low_ref, False)):
        store(ref, value, False)


def first_stage(field, shift, slot, blocks, steps):
    _, _, rows, width = field.shape
    block = width // RADIX
    part = rows // steps
    form = blocks is None
    shape = (RADIX, 2 * block, block)
    specs = [
        pl.BlockSpec((2, 1, part, block), lambda i, sh, _, s=s: (0, 0, i, (sh[0] + s) % RADIX))
        for s in range(RADIX)
    ]
    outs = [jax.ShapeDtypeStruct((2, rows, block), F32)] * RADIX
    out_specs = [pl.BlockSpec((2, part, block), lambda i, *_: (0, i, 0))] * RADIX
    if form:
        more = (cosine_table(width),)
        outs = outs + [jax.ShapeDtypeStruct(shape, BF16)] * 2
        out_specs = out_specs + [whole(shape)] * 2
    else:
        more = tuple(blocks)
    got = pl.pallas_call(
        lambda *refs: first_kernel(form, *refs),
        grid_spec=pltpu.PrefetchScalarGridSpec(
            num_scalar_prefetch=2,
            grid=(steps,),
            in_specs=specs + [whole(a.shape) for a in more],
            out_specs=out_specs,
        ),
        out_shape=outs,
        compiler_params=params(),
        cost_estimate=pl.CostEstimate(flops=2 * 10**9, bytes_accessed=6 * 10**6, transcendentals=0),
        name="along_y_first_s" if form else "along_y_first_r",
    )(shift, slot, *[field] * RADIX, *more)
    return (got[:RADIX], tuple(got[RADIX:])) if form else (got, blocks)


def middle_kernel(count, with_image, *refs):
    fields, refs = refs[:RADIX], refs[RADIX:]
    cos_ref, sin_ref, high_ref, low_ref = refs[:4]
    refs = refs[4:]
    if with_image:
        other_ref, refs = refs[0], refs[1:]
    outs, extra = refs[: RADIX * count], refs[RADIX * count]
    x = convolve([pick(f, False) for f in fields], high_ref, low_ref, True)
    x = [rotate(x[s], cos_ref[s], sin_ref[s]) for s in range(RADIX)]
    for s in range(RADIX):
        if with_image:
            extra[s] = other_ref[s, 0] * x[s][1] + other_ref[s, 1] * x[s][0]
        else:
            extra[s, 0] = x[s][0]
            extra[s, 1] = x[s][1]
    x = convolve(x, high_ref, low_ref, True)
    part = x[0][0].shape[0] // count
    for s in range(RADIX):
        for c in range(count):
            value = tuple(v[c * part : (c + 1) * part] for v in x[s])
            store(outs[s * count + c], value, False)


def middle_stage(fields, phases, blocks, count, other):
    _, rows, cols = fields[0].shape
    with_image = other is not None
    piece = jax.ShapeDtypeStruct((2, rows // count, cols), F32)
    extra = (RADIX, rows, cols) if with_image else (RADIX, 2, rows, cols)
    args = list(fields) + list(phases) + list(blocks) + ([other] if with_image else [])
    outs = [piece] * (RADIX * count) + [jax.ShapeDtypeStruct(extra, F32)]
    got = pl.pallas_call(
        lambda *refs: middle_kernel(count, with_image, *refs),
        in_specs=[whole(a.shape) for a in args],
        out_specs=[whole(o.shape) for o in outs],
        out_shape=outs,
        compiler_params=params(),
        cost_estimate=pl.CostEstimate(flops=4 * 10**9, bytes_accessed=12 * 10**6, transcendentals=0),
        name="along_x_r" if with_image else "along_x_s",
    )(*args)
    pieces = [[got[s * count + c] for s in range(RADIX)] for c in range(count)]
    return pieces, got[-1]


def last_kernel(with_image, shift_ref, slot_ref, place_ref, *refs):
    fields, refs = refs[:RADIX], refs[RADIX:]
    slab_ref, high_ref, low_ref = refs[:3]
    refs = refs[3:]
    if with_image:
        other_ref = refs[0]
        out_ref, terms, line = refs[-(RADIX + 2)], refs[-(RADIX + 1) : -1], refs[-1]
    else:
        out_ref = refs[-1]
    block = fields[0].shape[2]
    omega = omega_of(slot_ref[0])
    x = convolve([pick(f, False) for f in fields], high_ref, low_ref, False)
    for s in range(RADIX):
        at = pl.ds(pl.multiple_of(lax.rem(shift_ref[0] + s, RADIX) * block, block), block)
        theta = omega * (slab_ref[:, at] - ref_slow) * dz_km
        value = rotate(x[s], *phase_parts(theta))
        if with_image:
            line[:, at] = other_ref[0, 0, :, at] * value[1] + other_ref[1, 0, :, at] * value[0]
            value = (value[1], value[0])
        out_ref[0, 0, :, at] = value[0]
        out_ref[1, 0, :, at] = value[1]
    if with_image:
        count = len(terms)
        part = line.shape[1] // count
        for t in range(count):
            at = pl.ds(pl.multiple_of(lax.rem(place_ref[0] + t, count) * part, part), part)
            terms[t][...] = line[:, at]


def last_stage(fields, slab, blocks, shift, slot, place, start, rows, other, held):
    _, part, block = fields[0].shape
    width = block * RADIX
    with_image = other is not None
    row = start // part
    wide = pl.BlockSpec((2, 1, part, width), lambda i, *_: (0, 0, row, 0))
    args = list(fields) + [slab] + list(blocks)
    specs = [whole(f.shape) for f in fields]
    specs += [pl.BlockSpec((part, width), lambda i, *_: (row, 0))]
    specs += [whole(b.shape) for b in blocks]
    outs = [jax.ShapeDtypeStruct((2, 1, rows, width), F32)]
    out_specs = [wide]
    scratch = []
    if with_image:
        args.append(other)
        specs.append(wide)
        cols = width // RADIX
        outs += [jax.ShapeDtypeStruct((part, cols), F32)] * RADIX
        out_specs += [whole((part, cols))] * RADIX
        scratch = [pltpu.VMEM((part, width), F32)]
    alias = {}
    if held is not None:
        alias = {3 + len(args): 0}
        args.append(held)
        specs.append(pl.BlockSpec(memory_space=pl.ANY))
    got = pl.pallas_call(
        lambda *refs: last_kernel(with_image, *refs),
        grid_spec=pltpu.PrefetchScalarGridSpec(
            num_scalar_prefetch=3,
            grid=(1,),
            in_specs=specs,
            out_specs=out_specs,
            scratch_shapes=scratch,
        ),
        out_shape=outs,
        input_output_aliases=alias,
        compiler_params=params(),
        cost_estimate=pl.CostEstimate(flops=10**9, bytes_accessed=6 * 10**6, transcendentals=0),
        name="along_y_last_r" if with_image else "along_y_last_s",
    )(shift, slot, place, *args)
    return got[0], got[1:]


def phase_kernel(slot_ref, place_ref, *refs):
    pieces, (cos_ref, sin_ref) = refs[:-2], refs[-2:]
    count = len(pieces)
    sub_rows = pieces[0].shape[1]
    omega = omega_of(slot_ref[0])
    for t in range(count):
        at = pl.ds(pl.multiple_of(lax.rem(place_ref[0] + t, count) * sub_rows, 8), sub_rows)
        for s in range(RADIX):
            theta = omega * (pieces[t][s] - ref_slow) * dz_km
            cos_ref[s, at, :], sin_ref[s, at, :] = phase_parts(theta)


def phase_stage(pieces, slot, place):
    _, sub_rows, cols = pieces[0].shape
    shape = (RADIX, sub_rows * len(pieces), cols)
    return pl.pallas_call(
        phase_kernel,
        grid_spec=pltpu.PrefetchScalarGridSpec(
            num_scalar_prefetch=2,
            grid=(1,),
            in_specs=[whole(p.shape) for p in pieces],
            out_specs=[whole(shape)] * 2,
        ),
        out_shape=[jax.ShapeDtypeStruct(shape, F32)] * 2,
        compiler_params=params(),
        cost_estimate=pl.CostEstimate(flops=10**7, bytes_accessed=3 * 10**6, transcendentals=0),
        name="phases",
    )(slot, place, *pieces)


def image_kernel(chunks, early_ref, *refs):
    out_ref = refs[-1]
    count = (len(refs) - 1) // chunks
    out_ref[0] = early_ref[...]
    part = refs[0].shape[0]
    for c in range(chunks):
        mine = refs[c * count : (c + 1) * count]
        total = mine[0][...]
        for ref in mine[1:]:
            total = total + ref[...]
        out_ref[1, pl.ds(c * part, part), :] = total


def image_stage(early, groups):
    rows, cols = early.shape
    args = [early] + [piece for group in groups for piece in group]
    return pl.pallas_call(
        lambda *refs: image_kernel(len(groups), *refs),
        out_shape=jax.ShapeDtypeStruct((NZ, rows, cols), F32),
        compiler_params=params(),
        cost_estimate=pl.CostEstimate(flops=10**6, bytes_accessed=3 * 10**6, transcendentals=0),
        name="image_sum",
    )(*args)


def shifted(value, axis, step):
    count = lax.axis_size(axis)
    return lax.ppermute(value, axis, [((i + step) % count, i) for i in range(count)])


def swap_slots(pieces, axis):
    count = len(pieces)
    sent = [lax.ppermute(pieces[s], axis, [(i, (i + s) % count) for i in range(count)]) for s in range(1, count)]
    return [pieces[0]] + [sent[count - s - 1] for s in range(1, count)]


def gather_slots(piece, axis):
    return [piece] + [shifted(piece, axis, s) for s in range(1, lax.axis_size(axis))]


CHUNKS = 2


def body(source_field, receiver_field, slowness, owner, freq_index):
    rows, width = source_field.shape[2:]
    row_count = lax.axis_size("row")
    freq_count = lax.axis_size("freq")
    row_at = lax.axis_index("row")
    place = lax.axis_index("freq")[None]
    slot = freq_index
    ringed = row_count == RADIX and freq_count == RADIX and slowness.shape[0] == 1
    shift = row_at[None] if ringed else jnp.zeros((1,), jnp.int32)
    if not ringed:
        return general(source_field, receiver_field, slowness, owner, slot, shift, place)
    block = width // RADIX
    sub_rows = rows // RADIX

    s_first, blocks = first_stage(source_field, shift, slot, None, 2)
    s_mid = swap_slots(s_first, "row")
    slab = slowness[0].reshape(RADIX, sub_rows, width)
    mine = [lax.dynamic_index_in_dim(slab, (place[0] + t) % RADIX, 0, keepdims=False) for t in range(RADIX)]
    shares = swap_slots(mine, "freq")
    r_first, _ = first_stage(receiver_field, shift, slot, blocks, 2)
    r_mid = swap_slots(r_first, "row")
    stack = jnp.stack(shares)
    early, late = [lax.dynamic_index_in_dim(stack, (owner[z] - place[0]) % RADIX, 0, keepdims=False) for z in range(NZ)]
    turned = early.reshape(sub_rows, RADIX, block)
    turned = [lax.dynamic_index_in_dim(turned, (row_at + s) % RADIX, 1, keepdims=False) for s in range(RADIX)]
    turned = jnp.stack(swap_slots(turned, "row"))
    phases = phase_stage(gather_slots(turned, "freq"), slot, place)
    late = lax.all_gather(late, "freq", axis=0, tiled=True)

    s_pieces, s_held = middle_stage(s_mid, phases, blocks, 1, None)
    s_last = swap_slots(s_pieces[0], "row")
    r_pieces, term = middle_stage(r_mid, phases, blocks, CHUNKS, s_held)
    r_last = [swap_slots(p, "row") for p in r_pieces]
    first_image = lax.psum_scatter(term, "freq", scatter_dimension=0, tiled=False)
    pairs = []
    for r in range(RADIX):
        for f in range(RADIX):
            pairs.append((r * RADIX + f, ((r + f) % RADIX) * RADIX + r))
    first_image = lax.ppermute(first_image, ("row", "freq"), pairs)

    source_out, _ = last_stage(s_last, late, blocks, shift, slot, place, 0, rows, None, None)
    receiver_out, groups = None, []
    for c in range(CHUNKS):
        receiver_out, terms = last_stage(
            r_last[c], late, blocks, shift, slot, place, c * (rows // CHUNKS), rows, source_out, receiver_out
        )
        groups.append(swap_slots(terms, "freq"))
    return (source_out, receiver_out, image_stage(first_image, groups))


def general(source_field, receiver_field, slowness, owner, slot, shift, place):
    rows, width = source_field.shape[2:]
    slab_dev = slowness.shape[0]
    slabs = []
    for depth in range(NZ):
        chosen = owner[depth]
        kept = lax.dynamic_index_in_dim(slowness, chosen % slab_dev, 0, keepdims=False)
        slabs.append(lax.psum(jnp.where(place[0] == chosen // slab_dev, kept, 0.0), "freq"))
    s_first, blocks = first_stage(source_field, shift, slot, None, 1)
    r_first, _ = first_stage(receiver_field, shift, slot, blocks, 1)

    def to_columns(pieces):
        whole_rows = jnp.concatenate(pieces, axis=2)
        return lax.all_to_all(whole_rows, "row", split_axis=2, concat_axis=1, tiled=True)

    def to_rows(pieces):
        whole_cols = jnp.concatenate(pieces, axis=1)
        return lax.all_to_all(whole_cols, "row", split_axis=1, concat_axis=2, tiled=True)

    s_mid = jnp.split(to_columns(s_first), RADIX, axis=1)
    r_mid = jnp.split(to_columns(r_first), RADIX, axis=1)
    turned = lax.all_to_all(slabs[0], "row", split_axis=1, concat_axis=0, tiled=True)
    theta = omega_of(slot[0]) * (turned - ref_slow) * dz_km
    theta = theta.reshape(RADIX, -1, theta.shape[1])
    phases = (jnp.cos(theta), jnp.sin(theta))
    s_pieces, s_held = middle_stage(s_mid, phases, blocks, 1, None)
    r_pieces, term = middle_stage(r_mid, phases, blocks, 1, s_held)
    s_last = jnp.split(to_rows(s_pieces[0]), RADIX, axis=2)
    r_last = jnp.split(to_rows(r_pieces[0]), RADIX, axis=2)
    source_out, _ = last_stage(s_last, slabs[1], blocks, shift, slot, shift, 0, rows, None, None)
    receiver_out, terms = last_stage(
        r_last, slabs[1], blocks, shift, slot, shift, 0, rows, source_out, None
    )
    term = term.reshape(-1, term.shape[2])
    images = [lax.all_to_all(term, "row", split_axis=0, concat_axis=1, tiled=True)]
    images.append(jnp.concatenate(terms, axis=1))
    parts = [lax.psum_scatter(t, "freq", scatter_dimension=1, tiled=True) for t in images]
    return (source_out, receiver_out, jnp.stack(parts))


def solution(mesh):
    in_specs = (
        P(None, ("shot", "freq"), "row", None),
        P(None, ("shot", "freq"), "row", None),
        P("freq", "row", None),
        P(),
        P(("shot", "freq")),
    )
    out_specs = (
        P(None, ("shot", "freq"), "row", None),
        P(None, ("shot", "freq"), "row", None),
        P("shot", "row", "freq"),
    )
    return jax.shard_map(body, mesh=mesh, in_specs=in_specs, out_specs=out_specs, check_vma=False)
```

time: 606 us -> 213 us (0.35); the launches traced: 596 us -> 212 us
  matrix products: 170 us -> 0 us
  local copies, waits for them, and re-layouts: 125 us -> 21.3 us
  waiting for transfers between devices: 175 us -> 102 us
  blocking collectives: 50.7 us -> 0 us
  other arithmetic: 42.9 us -> 1.22 us
  Pallas kernels: 0 us -> 37.3 us
  starting transfers between devices: 14.9 us -> 33.9 us
    dot_general x64 -> x0, matrix products: 170 us -> none  [contract(): return jnp.einsum(form, left, right, precision=lax.Precision.HIGHEST)]
    ppermute x0 -> x31, waiting for transfers between devices: none -> 102 us  [the longest x27 80.4 us: swap_slots(): lax.ppermute(pieces[s], axis, [(i, (i + s) % count) for i in range(count)])]
    psum x1 -> x0, waiting for transfers between devices: 90 us -> none  [spread(): return lax.psum(kept, axis)]
    all_to_all x3 -> x0, waiting for transfers between devices: 72.1 us -> none  [the longest x1 43.7 us: body(): lax.all_to_all(fields, 'row', split_axis=4, concat_axis=3, tiled=True)]
    all_to_all x1 -> x0, blocking collectives: 50.7 us -> none  [body(): lax.all_to_all(fields, 'row', split_axis=4, concat_axis=3, tiled=True)]
    all_to_all x8 -> x0, local copies, waits for them, and re-layouts: 39.4 us -> none  [the longest x4 20.5 us: body(): lax.all_to_all(fields, 'row', split_axis=3, concat_axis=4, tiled=True)]
    pallas_call x0 -> x9, Pallas kernels: none -> 37.3 us  [the longest x2 13.5 us: middle_stage(): pl.pallas_call(lambda *refs: middle_kernel(count, with_image, *refs), in_...]
    ppermute x0 -> x31, starting transfers between devices: none -> 33.9 us  [the longest x27 25.6 us: swap_slots(): lax.ppermute(pieces[s], axis, [(i, (i + s) % count) for i in range(count)])]
  transfers between devices with their start and end apart: 6 -> 33, of which waited for: 4 -> 12; matrix products, arithmetic and copies ran while one was open for 15% -> 2% of each run, Pallas kernels for 0% -> 17%
where the time goes in v1:
time: 213 us; the launch traced here: 212 us
  waiting for transfers between devices  102 us (48%)
  Pallas kernels  37.3 us (18%)
  starting transfers between devices  33.9 us (16%)
  local copies, waits for them, and re-layouts  21.3 us (10%)
  between operations  16.3 us (8%)
    ppermute x27, waiting for transfers between devices, swap_slots(): lax.ppermute(pieces[s], axis, [(i, (i + s) % count) for i in range(count)])  80.4 us
    ppermute x27, starting transfers between devices, swap_slots(): lax.ppermute(pieces[s], axis, [(i, (i + s) % count) for i in range(count)])  25.6 us
    ppermute x3, waiting for transfers between devices, shifted(): lax.ppermute(value, axis, [((i + step) % count, i) for i in range(count)])  22 us
    unnamed x62, local copies, waits for them, and re-layouts  15.4 us
    pallas_call x2, Pallas kernels, middle_stage(): pl.pallas_call(lambda *refs: middle_kernel(count, with_image, *refs), in_...  13.5 us
    pallas_call x3, Pallas kernels, last_stage(): pl.pallas_call(lambda *refs: last_kernel(with_image, *refs), grid_spec=pl...  12.5 us
    pallas_call x2, Pallas kernels, first_stage(): pl.pallas_call(lambda *refs: first_kernel(form, *refs), grid_spec=pltpu.P...  9.68 us
    ppermute x3, starting transfers between devices, shifted(): lax.ppermute(value, axis, [((i + step) % count, i) for i in range(count)])  6.69 us
  transfers between devices with their start and end apart: 33, of which 12 were waited for; matrix products, arithmetic and copies ran while one was open for 2% of the time, Pallas kernels for 17%

profile of v1, /device:TPU:0, one launch (start us, length us, event | category | flops | bytes accessed | tf_op | source)
XLA Modules:
  0.0 212.5 jit_solution(10222693999099628192)
XLA Ops:
  7.3 2.1 constant_dynamic-slice_fusion.6
  9.3 5.0 %collective-permute-start.3 = (f32[64,1024]{1,0:T(8,128)}, f32[64,1024]{1,0:T(8,128)}, u32[]{:S(2)}, u32[]{:S(2)}) collective-permute-start(f32[64,1024]{1,0:T(8,128)} %get-tuple-element.80), channel_id=1, source_target_pairs={{0,3},{1,0},{2,1},{3,2},{4,7},{5,4},{6,5},{7,6},{8,11},{9,8},{10,9... | collective-permute-start | bytes 786440 | tf_op jit(solution)/shard_map/ppermute | solution.py:399
  14.4 1.0 collective-permute-start.5
  16.1 6.1 %along_y_first_s.1 = (f32[2,256,256]{2,1,0:T(8,128)S(1)}, f32[2,256,256]{2,1,0:T(8,128)S(1)}, f32[2,256,256]{2,1,0:T(8,128)S(1)}, f32[2,256,256]{2,1,0:T(8,128)}...) custom-call(s32[1]{0:T(128)} %bitcast.refs_0_, s32[1]{0:T(128)S(6)} %copy.23.refs_1_.slot_ref, ...), custom_call_target="tpu_custom_call" | custom-call | flops 2000000000 | bytes 6000000 | tf_op jit(solution)/shard_map/along_y_first_s/pallas_call | solution.py:206
  22.2 0.8 copy-done.17
  23.0 0.8 copy-done.18
  23.9 0.6 fusion
  25.8 11.2 %collective-permute-done.4 = f32[64,1024]{1,0:T(8,128)} collective-permute-done((f32[64,1024]{1,0:T(8,128)}, f32[64,1024]{1,0:T(8,128)}, u32[]{:S(2)}, u32[]{:S(2)}) %collective-permute-start.4) | collective-permute-done | bytes 262176 | tf_op jit(solution)/shard_map/ppermute | solution.py:399
  37.0 1.2 pad_maximum_fusion
  38.2 0.7 constant_dynamic-slice_fusion
  39.1 0.8 reshape.11
  39.9 1.6 constant_dynamic-slice_fusion.4
  41.7 1.5 collective-permute-start.7
  43.4 0.5 collective-permute-start.1
  43.9 1.9 collective-permute-start.2
  45.8 1.5 collective-permute-done.7
  47.2 0.4 collective-permute-done.8
  47.7 2.9 %collective-permute-start.10 = (f32[4,64,256]{2,1,0:T(8,128)S(1)}, f32[4,64,256]{2,1,0:T(8,128)S(1)}, u32[]{:S(2)}, u32[]{:S(2)}) collective-permute-start(f32[4,64,256]{2,1,0:T(8,128)S(1)} %pad_maximum_fusion.1.refs_0_), channel_id=1, source_target_pairs={{2,0},{3,1},{0,2},{1,3},{6,4},{7,5},{4,6},{5,7},{10,8},{11,9},{8,1... | collective-permute-start | bytes 786440 | tf_op jit(solution)/shard_map/ppermute | solution.py:394
  50.6 3.8 %collective-permute-start.9 = (f32[4,64,256]{2,1,0:T(8,128)S(1)}, f32[4,64,256]{2,1,0:T(8,128)S(1)}, u32[]{:S(2)}, u32[]{:S(2)}) collective-permute-start(f32[4,64,256]{2,1,0:T(8,128)S(1)} %pad_maximum_fusion.1.refs_0_), channel_id=1, source_target_pairs={{1,0},{2,1},{3,2},{0,3},{5,4},{6,5},{7,6},{4,7},{9,8},{10,9},{11,1... | collective-permute-start | bytes 786440 | tf_op jit(solution)/shard_map/ppermute | solution.py:394
  54.4 3.6 %along_y_first_r.1 = (f32[2,256,256]{2,1,0:T(8,128)S(1)}, f32[2,256,256]{2,1,0:T(8,128)S(1)}, f32[2,256,256]{2,1,0:T(8,128)S(1)}, f32[2,256,256]{2,1,0:T(8,128)S(1)}) custom-call(s32[1]{0:T(128)} %bitcast.refs_0_, s32[1]{0:T(128)S(6)} %copy.23.refs_1_.slot_ref, f32[2,1,256,1024]{3,2,1,0:T(8,128)} %refs_5_.3, f32[2,1,256,1024]{3,2,1,0:T(8,128)} %refs_5_.3, ...), custom_call_target="tpu_custom_call" | custom-call | flops 2000000000 | bytes 6000000 | tf_op jit(solution)/shard_map/along_y_first_r/pallas_call | solution.py:206
  58.0 22.0 %collective-permute-done.10.refs_2_ = f32[4,64,256]{2,1,0:T(8,128)S(1)} collective-permute-done((f32[4,64,256]{2,1,0:T(8,128)S(1)}, f32[4,64,256]{2,1,0:T(8,128)S(1)}, u32[]{:S(2)}, u32[]{:S(2)}) %collective-permute-start.10) | collective-permute-done | bytes 262176 | tf_op jit(solution)/shard_map/ppermute | solution.py:394
  80.0 0.8 collective-permute-start.16
  80.8 0.2 collective-permute-start.17
  81.0 0.8 phases.1
  81.9 1.0 copy-done.14
  82.9 1.4 copy-done.16
  84.3 6.1 %along_x_s.1 = (f32[2,256,256]{2,1,0:T(8,128)S(1)}, f32[2,256,256]{2,1,0:T(8,128)S(1)}, f32[2,256,256]{2,1,0:T(8,128)S(1)}, f32[2,256,256]{2,1,0:T(8,128)S(1)}, f32[4,2,256,256]{3,2,1,0:T(8,128)}) custom-call(f32[2,256,256]{2,1,0:T(8,128)S(1)} %get-tuple-element.39.refs_0_, f32[2,256,256]{2,1,0:T(8,128)S(1)} %copy-done.16, ...), custom_call_target="tpu_custom_call" | custom-call | flops 4000000000 | bytes 12000000 | tf_op jit(solution)/shard_map/along_x_s/pallas_call | solution.py:252
  90.4 0.8 copy-done.21
  91.2 0.8 collective-permute-done.15.refs_1_
  92.0 12.1 %collective-permute-done.16.refs_2_ = f32[2,256,256]{2,1,0:T(8,128)S(1)} collective-permute-done((f32[2,256,256]{2,1,0:T(8,128)S(1)}, f32[2,256,256]{2,1,0:T(8,128)S(1)}, u32[]{:S(2)}, u32[]{:S(2)}) %collective-permute-start.16) | collective-permute-done | bytes 524320 | tf_op jit(solution)/shard_map/ppermute | solution.py:399
  104.1 0.7 collective-permute-done.17.refs_3_
  104.8 7.4 %along_x_r.1 = (f32[2,128,256]{2,1,0:T(8,128)S(1)}, f32[2,128,256]{2,1,0:T(8,128)S(1)}, f32[2,128,256]{2,1,0:T(8,128)S(1)}, f32[2,128,256]{2,1,0:T(8,128)S(1)}, ...) custom-call(f32[2,256,256]{2,1,0:T(8,128)S(1)} %get-tuple-element.51, ...), custom_call_target="tpu_custom_call" | custom-call | flops 4000000000 | bytes 12000000 | tf_op jit(solution)/shard_map/along_x_r/pallas_call | solution.py:252
  112.2 0.7 copy-done.9
  112.9 0.7 copy-done.22
  113.6 0.7 copy-done.23
  114.4 0.7 copy-done.24
  115.0 0.7 copy-done.25
  115.8 0.7 copy-done.26
  116.5 0.7 copy-done.27
  117.3 1.3 collective-permute-start.13
  118.7 1.6 collective-permute-start.21
  120.3 0.8 collective-permute-start.22
  121.1 24.9 %collective-permute-done.21.refs_4_ = f32[2,128,256]{2,1,0:T(8,128)S(1)} collective-permute-done((f32[2,128,256]{2,1,0:T(8,128)}, f32[2,128,256]{2,1,0:T(8,128)S(1)}, u32[]{:S(2)}, u32[]{:S(2)}) %collective-permute-start.21) | collective-permute-done | bytes 262176 | tf_op jit(solution)/shard_map/ppermute | solution.py:399
  146.1 0.7 copy-done.11
  146.8 1.8 collective-permute-start.23
  148.6 0.8 copy-done.5
  149.4 1.6 collective-permute-start.19
  151.0 0.8 copy-done.7
  151.8 1.2 copy-done.4
  153.0 1.0 copy-done.6
  154.1 1.0 copy-done.8
  155.1 4.4 %along_y_last_s.1.refs_10_ = f32[2,1,256,1024]{3,2,1,0:T(8,128)} custom-call(s32[1]{0:T(128)} %bitcast.refs_0_, s32[1]{0:T(128)S(6)} %copy.23.refs_1_.slot_ref, s32[1]{0:T(128)} %bitcast.1.place_ref.refs_2_, f32[2,256,256]{2,1,0:T(8,128)S(1)} %get-tuple-element.47.refs_3_, f32[2,256,256]{2,1,0:T(8,128)S(1)} %collective-permute-done.12.refs_4_, ...), custom_call_target="tpu_custom_call" | custom-call | flops 1000000000 | bytes 6000000 | tf_op jit(solution)/shard_map/along_y_last_s/pallas_call | solution.py:319
  159.5 4.0 %along_y_last_r.2 = (f32[2,1,256,1024]{3,2,1,0:T(8,128)}, f32[128,256]{1,0:T(8,128)S(1)}, f32[128,256]{1,0:T(8,128)S(1)}, f32[128,256]{1,0:T(8,128)S(1)}, f32[128,256]{1,0:T(8,128)S(1)}) custom-call(s32[1]{0:T(128)} %bitcast.refs_0_, s32[1]{0:T(128)S(6)} %copy.23.refs_1_.slot_ref, s32[1]{0:T(128)} %bitcast.1.place_ref.refs_2_, ...), custom_call_target="tpu_custom_call" | custom-call | flops 1000000000 | bytes 6000000 | tf_op jit(solution)/shard_map/along_y_last_r/pallas_call | solution.py:319
  163.6 1.7 collective-permute-done.20.refs_6_
  165.3 4.1 %along_y_last_r.3 = (f32[2,1,256,1024]{3,2,1,0:T(8,128)}, f32[128,256]{1,0:T(8,128)S(1)}, f32[128,256]{1,0:T(8,128)S(1)}, f32[128,256]{1,0:T(8,128)S(1)}, f32[128,256]{1,0:T(8,128)S(1)}) custom-call(s32[1]{0:T(128)} %bitcast.refs_0_, s32[1]{0:T(128)S(6)} %copy.23.refs_1_.slot_ref, s32[1]{0:T(128)} %bitcast.1.place_ref.refs_2_, ...), custom_call_target="tpu_custom_call", output_to_operand_aliasing={{0}: (11, {})} | custom-call | flops 1000000000 | bytes 6000000 | tf_op jit(solution)/shard_map/along_y_last_r/pallas_call | solution.py:319
  169.3 0.9 collective-permute-start.29
  170.3 1.6 collective-permute-start.24
  171.9 2.4 %collective-permute-start.30 = (f32[128,256]{1,0:T(8,128)S(1)}, f32[128,256]{1,0:T(8,128)S(1)}, u32[]{:S(2)}, u32[]{:S(2)}) collective-permute-start(f32[128,256]{1,0:T(8,128)S(1)} %get-tuple-element.74), channel_id=1, source_target_pairs={{0,1},{1,2},{2,3},{3,0},{4,5},{5,6},{6,7},{7,4},{8,9},{9,10},{10,1... | collective-permute-start | bytes 393224 | tf_op jit(solution)/shard_map/ppermute | solution.py:399
  174.3 1.5 collective-permute-start.25
  175.8 2.0 collective-permute-start.26
  177.8 10.8 %collective-permute-done.29.refs_7_ = f32[128,256]{1,0:T(8,128)S(1)} collective-permute-done((f32[128,256]{1,0:T(8,128)S(1)}, f32[128,256]{1,0:T(8,128)S(1)}, u32[]{:S(2)}, u32[]{:S(2)}) %collective-permute-start.29) | collective-permute-done | bytes 131104 | tf_op jit(solution)/shard_map/ppermute | solution.py:399
  188.7 0.4 collective-permute-done.25.refs_2_
  189.1 15.7 %collective-permute-done.26.refs_3_ = f32[128,256]{1,0:T(8,128)S(1)} collective-permute-done((f32[128,256]{1,0:T(8,128)S(1)}, f32[128,256]{1,0:T(8,128)S(1)}, u32[]{:S(2)}, u32[]{:S(2)}) %collective-permute-start.26) | collective-permute-done | bytes 131104 | tf_op jit(solution)/shard_map/ppermute | solution.py:399
  204.8 0.9 image_sum.1
  (82 shorter events, 0.9 us)
Async XLA Ops:
  7.2 144.6 %all-gather.3.cloned.1.call-start = ((), (), s32[]{:S(2)}) async-start(), calls=%async_computation.2 | async-start | bytes 1310720 | tf_op jit(solution)/shard_map/all_gather | solution.py:437
  9.3 16.4 %collective-permute-start.3 = (f32[64,1024]{1,0:T(8,128)}, f32[64,1024]{1,0:T(8,128)}, u32[]{:S(2)}, u32[]{:S(2)}) collective-permute-start(f32[64,1024]{1,0:T(8,128)} %get-tuple-element.80), channel_id=1, source_target_pairs={{0,3},{1,0},{2,1},{3,2},{4,7},{5,4},{6,5},{7,6},{8,11},{9,8},{10,9... | collective-permute-start | bytes 786440 | tf_op jit(solution)/shard_map/ppermute | solution.py:399
  14.4 22.6 %collective-permute-start.4 = (f32[64,1024]{1,0:T(8,128)}, f32[64,1024]{1,0:T(8,128)}, u32[]{:S(2)}, u32[]{:S(2)}) collective-permute-start(f32[64,1024]{1,0:T(8,128)} %get-tuple-element.79), channel_id=1, source_target_pairs={{0,2},{1,3},{2,0},{3,1},{4,6},{5,7},{6,4},{7,5},{8,10},{9,11},{10,... | collective-permute-start | bytes 786440 | tf_op jit(solution)/shard_map/ppermute | solution.py:399
  14.4 22.6 %collective-permute-start.5 = (f32[64,1024]{1,0:T(8,128)}, f32[64,1024]{1,0:T(8,128)}, u32[]{:S(2)}, u32[]{:S(2)}) collective-permute-start(f32[64,1024]{1,0:T(8,128)} %get-tuple-element.78), channel_id=1, source_target_pairs={{0,1},{1,2},{2,3},{3,0},{4,5},{5,6},{6,7},{7,4},{8,9},{9,10},{10,1... | collective-permute-start | bytes 786440 | tf_op jit(solution)/shard_map/ppermute | solution.py:399
  16.1 7.8 %copy-start.28 = (s32[4]{0:T(128)S(1)}, s32[4]{0:T(128)}, u32[]{:S(2)}) copy-start(s32[4]{0:T(128)} %param.9) | copy-start | bytes 52
  22.2 0.8 copy-start.17
  23.0 0.8 copy-start.18
  23.0 31.4 %copy-start = (bf16[4,512,256]{2,1,0:T(8,128)(2,1)}, bf16[4,512,256]{2,1,0:T(8,128)(2,1)S(1)}, u32[]{:S(2)}) copy-start(bf16[4,512,256]{2,1,0:T(8,128)(2,1)S(1)} %get-tuple-element.45.refs_6_.refs_8_) | copy-start | bytes 3145732
  23.0 31.4 %copy-start.2 = (bf16[4,512,256]{2,1,0:T(8,128)(2,1)}, bf16[4,512,256]{2,1,0:T(8,128)(2,1)S(1)}, u32[]{:S(2)}) copy-start(bf16[4,512,256]{2,1,0:T(8,128)(2,1)S(1)} %get-tuple-element.46.refs_7_.refs_9_) | copy-start | bytes 3145732
  23.8 26.8 %collective-permute-start = (f32[2,256,256]{2,1,0:T(8,128)}, f32[2,256,256]{2,1,0:T(8,128)S(1)}, u32[]{:S(2)}, u32[]{:S(2)}) collective-permute-start(f32[2,256,256]{2,1,0:T(8,128)} %get-tuple-element.40), channel_id=1, source_target_pairs={{0,12},{4,0},{8,4},{12,8},{1,13},{5,1},{9,5},{13,9},{2,14},{6,2},{... | collective-permute-start | bytes 1572872 | tf_op jit(solution)/shard_map/ppermute | solution.py:399
  39.0 131.3 %reduce-scatter.2.cloned.1.call-start = ((), (), s32[]{:S(2)}) async-start(), calls=%async_computation.1 | async-start | bytes 1310720 | tf_op jit(solution)/shard_map/reduce_scatter | solution.py:443
  41.6 2.3 %collective-permute-start.6 = (f32[64,256]{1,0:T(8,128)S(1)}, f32[64,256]{1,0:T(8,128)S(1)}, u32[]{:S(2)}, u32[]{:S(2)}) collective-permute-start(f32[64,256]{1,0:T(8,128)S(1)} %bitcast.37), channel_id=1, source_target_pairs={{0,12},{4,0},{8,4},{12,8},{1,13},{5,1},{9,5},{13,9},{2,14},{6,2},{... | collective-permute-start | bytes 196616 | tf_op jit(solution)/shard_map/ppermute | solution.py:399
  41.7 5.6 %collective-permute-start.7 = (f32[64,256]{1,0:T(8,128)S(1)}, f32[64,256]{1,0:T(8,128)S(1)}, u32[]{:S(2)}, u32[]{:S(2)}) collective-permute-start(f32[64,256]{1,0:T(8,128)S(1)} %bitcast.36), channel_id=1, source_target_pairs={{0,8},{4,12},{8,0},{12,4},{1,9},{5,13},{9,1},{13,5},{2,10},{6,14},... | collective-permute-start | bytes 196616 | tf_op jit(solution)/shard_map/ppermute | solution.py:399
  43.2 4.5 %collective-permute-start.8 = (f32[64,256]{1,0:T(8,128)S(1)}, f32[64,256]{1,0:T(8,128)S(1)}, u32[]{:S(2)}, u32[]{:S(2)}) collective-permute-start(f32[64,256]{1,0:T(8,128)S(1)} %bitcast.38), channel_id=1, source_target_pairs={{0,4},{4,8},{8,12},{12,0},{1,5},{5,9},{9,13},{13,1},{2,6},{6,10},{... | collective-permute-start | bytes 196616 | tf_op jit(solution)/shard_map/ppermute | solution.py:399
  43.4 39.5 %collective-permute-start.1 = (f32[2,256,256]{2,1,0:T(8,128)}, f32[2,256,256]{2,1,0:T(8,128)S(1)}, u32[]{:S(2)}, u32[]{:S(2)}) collective-permute-start(f32[2,256,256]{2,1,0:T(8,128)} %copy-done.18), channel_id=1, source_target_pairs={{0,8},{4,12},{8,0},{12,4},{1,9},{5,13},{9,1},{13,5},{2,10},{6,14},... | collective-permute-start | bytes 1572872 | tf_op jit(solution)/shard_map/ppermute | solution.py:399
  43.9 38.9 %collective-permute-start.2 = (f32[2,256,256]{2,1,0:T(8,128)}, f32[2,256,256]{2,1,0:T(8,128)S(1)}, u32[]{:S(2)}, u32[]{:S(2)}) collective-permute-start(f32[2,256,256]{2,1,0:T(8,128)} %copy-done.17), channel_id=1, source_target_pairs={{0,4},{4,8},{8,12},{12,0},{1,5},{5,9},{9,13},{13,1},{2,6},{6,10},{... | collective-permute-start | bytes 1572872 | tf_op jit(solution)/shard_map/ppermute | solution.py:399
  47.7 32.3 %collective-permute-start.10 = (f32[4,64,256]{2,1,0:T(8,128)S(1)}, f32[4,64,256]{2,1,0:T(8,128)S(1)}, u32[]{:S(2)}, u32[]{:S(2)}) collective-permute-start(f32[4,64,256]{2,1,0:T(8,128)S(1)} %pad_maximum_fusion.1.refs_0_), channel_id=1, source_target_pairs={{2,0},{3,1},{0,2},{1,3},{6,4},{7,5},{4,6},{5,7},{10,8},{11,9},{8,1... | collective-permute-start | bytes 786440 | tf_op jit(solution)/shard_map/ppermute | solution.py:394
  50.5 29.4 %collective-permute-start.11 = (f32[4,64,256]{2,1,0:T(8,128)S(1)}, f32[4,64,256]{2,1,0:T(8,128)S(1)}, u32[]{:S(2)}, u32[]{:S(2)}) collective-permute-start(f32[4,64,256]{2,1,0:T(8,128)S(1)} %pad_maximum_fusion.1.refs_0_), channel_id=1, source_target_pairs={{3,0},{0,1},{1,2},{2,3},{7,4},{4,5},{5,6},{6,7},{11,8},{8,9},{9,10... | collective-permute-start | bytes 786440 | tf_op jit(solution)/shard_map/ppermute | solution.py:394
  50.5 7.4 %copy-start.15 = (f32[2,256,256]{2,1,0:T(8,128)}, f32[2,256,256]{2,1,0:T(8,128)S(1)}, u32[]{:S(2)}) copy-start(f32[2,256,256]{2,1,0:T(8,128)S(1)} %collective-permute-done.refs_1_) | copy-start | bytes 1572868
  50.6 30.3 %collective-permute-start.9 = (f32[4,64,256]{2,1,0:T(8,128)S(1)}, f32[4,64,256]{2,1,0:T(8,128)S(1)}, u32[]{:S(2)}, u32[]{:S(2)}) collective-permute-start(f32[4,64,256]{2,1,0:T(8,128)S(1)} %pad_maximum_fusion.1.refs_0_), channel_id=1, source_target_pairs={{1,0},{2,1},{3,2},{0,3},{5,4},{6,5},{7,6},{4,7},{9,8},{10,9},{11,1... | collective-permute-start | bytes 786440 | tf_op jit(solution)/shard_map/ppermute | solution.py:394
  80.0 12.0 %collective-permute-start.15 = (f32[2,256,256]{2,1,0:T(8,128)S(1)}, f32[2,256,256]{2,1,0:T(8,128)S(1)}, u32[]{:S(2)}, u32[]{:S(2)}) collective-permute-start(f32[2,256,256]{2,1,0:T(8,128)S(1)} %get-tuple-element.52), channel_id=1, source_target_pairs={{0,12},{4,0},{8,4},{12,8},{1,13},{5,1},{9,5},{13,9},{2,14},{6,2},{... | collective-permute-start | bytes 1572872 | tf_op jit(solution)/shard_map/ppermute | solution.py:399
  80.0 24.2 %collective-permute-start.16 = (f32[2,256,256]{2,1,0:T(8,128)S(1)}, f32[2,256,256]{2,1,0:T(8,128)S(1)}, u32[]{:S(2)}, u32[]{:S(2)}) collective-permute-start(f32[2,256,256]{2,1,0:T(8,128)S(1)} %get-tuple-element.53), channel_id=1, source_target_pairs={{0,8},{4,12},{8,0},{12,4},{1,9},{5,13},{9,1},{13,5},{2,10},{6,14},... | collective-permute-start | bytes 1572872 | tf_op jit(solution)/shard_map/ppermute | solution.py:399
  80.8 24.0 %collective-permute-start.17 = (f32[2,256,256]{2,1,0:T(8,128)S(1)}, f32[2,256,256]{2,1,0:T(8,128)S(1)}, u32[]{:S(2)}, u32[]{:S(2)}) collective-permute-start(f32[2,256,256]{2,1,0:T(8,128)S(1)} %get-tuple-element.54), channel_id=1, source_target_pairs={{0,4},{4,8},{8,12},{12,0},{1,5},{5,9},{9,13},{13,1},{2,6},{6,10},{... | collective-permute-start | bytes 1572872 | tf_op jit(solution)/shard_map/ppermute | solution.py:399
  81.9 1.0 copy-start.14
  82.8 7.6 %copy-start.13 = (f32[4,256,256]{2,1,0:T(8,128)}, f32[4,256,256]{2,1,0:T(8,128)S(1)}, u32[]{:S(2)}) copy-start(f32[4,256,256]{2,1,0:T(8,128)S(1)} %get-tuple-element.43.refs_4_) | copy-start | bytes 3145732
  82.8 1.4 copy-start.16
  90.4 0.8 copy-start.21
  91.2 13.6 %copy-start.19 = (f32[2,256,256]{2,1,0:T(8,128)}, f32[2,256,256]{2,1,0:T(8,128)S(1)}, u32[]{:S(2)}) copy-start(f32[2,256,256]{2,1,0:T(8,128)S(1)} %get-tuple-element.50) | copy-start | bytes 1572868
  91.2 13.6 %copy-start.20 = (f32[2,256,256]{2,1,0:T(8,128)}, f32[2,256,256]{2,1,0:T(8,128)S(1)}, u32[]{:S(2)}) copy-start(f32[2,256,256]{2,1,0:T(8,128)S(1)} %get-tuple-element.49) | copy-start | bytes 1572868
  104.8 47.0 %copy-start.1 = (bf16[4,512,256]{2,1,0:T(8,128)(2,1)S(1)}, bf16[4,512,256]{2,1,0:T(8,128)(2,1)}, u32[]{:S(2)}) copy-start(bf16[4,512,256]{2,1,0:T(8,128)(2,1)} %copy-done) | copy-start | bytes 3145732
  104.8 47.0 %copy-start.3 = (bf16[4,512,256]{2,1,0:T(8,128)(2,1)S(1)}, bf16[4,512,256]{2,1,0:T(8,128)(2,1)}, u32[]{:S(2)}) copy-start(bf16[4,512,256]{2,1,0:T(8,128)(2,1)} %copy-done.2) | copy-start | bytes 3145732
  112.2 0.7 copy-start.9
  112.9 0.7 copy-start.22
  113.6 0.7 copy-start.23
  114.4 0.7 copy-start.24
  115.0 0.8 copy-start.25
  115.8 0.7 copy-start.26
  116.5 0.7 copy-start.27
  117.2 31.3 %collective-permute-start.12 = (f32[2,256,256]{2,1,0:T(8,128)}, f32[2,256,256]{2,1,0:T(8,128)S(1)}, u32[]{:S(2)}, u32[]{:S(2)}) collective-permute-start(f32[2,256,256]{2,1,0:T(8,128)} %copy-done.21), channel_id=1, source_target_pairs={{0,12},{4,0},{8,4},{12,8},{1,13},{5,1},{9,5},{13,9},{2,14},{6,2},{... | collective-permute-start | bytes 1572872 | tf_op jit(solution)/shard_map/ppermute | solution.py:399
  117.3 31.3 %collective-permute-start.13 = (f32[2,256,256]{2,1,0:T(8,128)}, f32[2,256,256]{2,1,0:T(8,128)S(1)}, u32[]{:S(2)}, u32[]{:S(2)}) collective-permute-start(f32[2,256,256]{2,1,0:T(8,128)} %copy-done.20), channel_id=1, source_target_pairs={{0,8},{4,12},{8,0},{12,4},{1,9},{5,13},{9,1},{13,5},{2,10},{6,14},... | collective-permute-start | bytes 1572872 | tf_op jit(solution)/shard_map/ppermute | solution.py:399
  118.5 32.4 %collective-permute-start.14 = (f32[2,256,256]{2,1,0:T(8,128)}, f32[2,256,256]{2,1,0:T(8,128)S(1)}, u32[]{:S(2)}, u32[]{:S(2)}) collective-permute-start(f32[2,256,256]{2,1,0:T(8,128)} %copy-done.19), channel_id=1, source_target_pairs={{0,4},{4,8},{8,12},{12,0},{1,5},{5,9},{9,13},{13,1},{2,6},{6,10},{... | collective-permute-start | bytes 1572872 | tf_op jit(solution)/shard_map/ppermute | solution.py:399
  118.7 27.4 %collective-permute-start.21 = (f32[2,128,256]{2,1,0:T(8,128)}, f32[2,128,256]{2,1,0:T(8,128)S(1)}, u32[]{:S(2)}, u32[]{:S(2)}) collective-permute-start(f32[2,128,256]{2,1,0:T(8,128)} %copy-done.27), channel_id=1, source_target_pairs={{0,12},{4,0},{8,4},{12,8},{1,13},{5,1},{9,5},{13,9},{2,14},{6,2},{... | collective-permute-start | bytes 786440 | tf_op jit(solution)/shard_map/ppermute | solution.py:399
  120.3 39.2 %collective-permute-start.22 = (f32[2,128,256]{2,1,0:T(8,128)}, f32[2,128,256]{2,1,0:T(8,128)}, u32[]{:S(2)}, u32[]{:S(2)}) collective-permute-start(f32[2,128,256]{2,1,0:T(8,128)} %copy-done.26), channel_id=1, source_target_pairs={{0,8},{4,12},{8,0},{12,4},{1,9},{5,13},{9,1},{13,5},{2,10},{6,14},... | collective-permute-start | bytes 786440 | tf_op jit(solution)/shard_map/ppermute | solution.py:399
  146.1 0.7 copy-start.11
  146.8 12.7 %collective-permute-start.23 = (f32[2,128,256]{2,1,0:T(8,128)}, f32[2,128,256]{2,1,0:T(8,128)}, u32[]{:S(2)}, u32[]{:S(2)}) collective-permute-start(f32[2,128,256]{2,1,0:T(8,128)} %copy-done.25), channel_id=1, source_target_pairs={{0,4},{4,8},{8,12},{12,0},{1,5},{5,9},{9,13},{13,1},{2,6},{6,10},{... | collective-permute-start | bytes 786440 | tf_op jit(solution)/shard_map/ppermute | solution.py:399
  148.6 15.0 %collective-permute-start.18 = (f32[2,128,256]{2,1,0:T(8,128)}, f32[2,128,256]{2,1,0:T(8,128)}, u32[]{:S(2)}, u32[]{:S(2)}) collective-permute-start(f32[2,128,256]{2,1,0:T(8,128)} %copy-done.24), channel_id=1, source_target_pairs={{0,12},{4,0},{8,4},{12,8},{1,13},{5,1},{9,5},{13,9},{2,14},{6,2},{... | collective-permute-start | bytes 786440 | tf_op jit(solution)/shard_map/ppermute | solution.py:399
  148.6 0.8 copy-start.5
  149.4 14.2 %collective-permute-start.19 = (f32[2,128,256]{2,1,0:T(8,128)}, f32[2,128,256]{2,1,0:T(8,128)}, u32[]{:S(2)}, u32[]{:S(2)}) collective-permute-start(f32[2,128,256]{2,1,0:T(8,128)} %copy-done.23), channel_id=1, source_target_pairs={{0,8},{4,12},{8,0},{12,4},{1,9},{5,13},{9,1},{13,5},{2,10},{6,14},... | collective-permute-start | bytes 786440 | tf_op jit(solution)/shard_map/ppermute | solution.py:399
  151.0 0.8 copy-start.7
  151.8 13.5 %collective-permute-start.20 = (f32[2,128,256]{2,1,0:T(8,128)}, f32[2,128,256]{2,1,0:T(8,128)}, u32[]{:S(2)}, u32[]{:S(2)}) collective-permute-start(f32[2,128,256]{2,1,0:T(8,128)} %copy-done.22), channel_id=1, source_target_pairs={{0,4},{4,8},{8,12},{12,0},{1,5},{5,9},{9,13},{13,1},{2,6},{6,10},{... | collective-permute-start | bytes 786440 | tf_op jit(solution)/shard_map/ppermute | solution.py:399
  151.8 1.2 copy-start.4
  153.0 1.0 copy-start.6
  154.1 1.0 copy-start.8
  155.1 4.4 %copy-start.10 = (f32[2,128,256]{2,1,0:T(8,128)S(1)}, f32[2,128,256]{2,1,0:T(8,128)}, u32[]{:S(2)}) copy-start(f32[2,128,256]{2,1,0:T(8,128)} %copy-done.9) | copy-start | bytes 786436
  155.1 4.4 %copy-start.12 = (f32[2,128,256]{2,1,0:T(8,128)S(1)}, f32[2,128,256]{2,1,0:T(8,128)}, u32[]{:S(2)}) copy-start(f32[2,128,256]{2,1,0:T(8,128)} %copy-done.11) | copy-start | bytes 786436
  169.3 6.4 %collective-permute-start.28 = (f32[128,256]{1,0:T(8,128)S(1)}, f32[128,256]{1,0:T(8,128)S(1)}, u32[]{:S(2)}, u32[]{:S(2)}) collective-permute-start(f32[128,256]{1,0:T(8,128)S(1)} %get-tuple-element.72), channel_id=1, source_target_pairs={{0,3},{1,0},{2,1},{3,2},{4,7},{5,4},{6,5},{7,6},{8,11},{9,8},{10,9... | collective-permute-start | bytes 393224 | tf_op jit(solution)/shard_map/ppermute | solution.py:399
  169.3 19.3 %collective-permute-start.29 = (f32[128,256]{1,0:T(8,128)S(1)}, f32[128,256]{1,0:T(8,128)S(1)}, u32[]{:S(2)}, u32[]{:S(2)}) collective-permute-start(f32[128,256]{1,0:T(8,128)S(1)} %get-tuple-element.73), channel_id=1, source_target_pairs={{0,2},{1,3},{2,0},{3,1},{4,6},{5,7},{6,4},{7,5},{8,10},{9,11},{10,... | collective-permute-start | bytes 393224 | tf_op jit(solution)/shard_map/ppermute | solution.py:399
  170.3 34.5 %collective-permute-start.24 = (f32[256,256]{1,0:T(8,128)}, f32[256,256]{1,0:T(8,128)S(1)}, u32[]{:S(2)}, u32[]{:S(2)}) collective-permute-start(f32[256,256]{1,0:T(8,128)} %bitcast.42), channel_id=1, source_target_pairs={{0,0},{1,4},{2,8},{3,12},{4,5},{5,9},{6,13},{7,1},{8,10},{9,14},{1... | collective-permute-start | bytes 786440 | tf_op jit(solution)/shard_map/ppermute | solution.py:448
  171.9 16.8 %collective-permute-start.30 = (f32[128,256]{1,0:T(8,128)S(1)}, f32[128,256]{1,0:T(8,128)S(1)}, u32[]{:S(2)}, u32[]{:S(2)}) collective-permute-start(f32[128,256]{1,0:T(8,128)S(1)} %get-tuple-element.74), channel_id=1, source_target_pairs={{0,1},{1,2},{2,3},{3,0},{4,5},{5,6},{6,7},{7,4},{8,9},{9,10},{10,1... | collective-permute-start | bytes 393224 | tf_op jit(solution)/shard_map/ppermute | solution.py:399
  174.3 14.8 %collective-permute-start.25 = (f32[128,256]{1,0:T(8,128)S(1)}, f32[128,256]{1,0:T(8,128)S(1)}, u32[]{:S(2)}, u32[]{:S(2)}) collective-permute-start(f32[128,256]{1,0:T(8,128)S(1)} %get-tuple-element.68), channel_id=1, source_target_pairs={{0,3},{1,0},{2,1},{3,2},{4,7},{5,4},{6,5},{7,6},{8,11},{9,8},{10,9... | collective-permute-start | bytes 393224 | tf_op jit(solution)/shard_map/ppermute | solution.py:399
  175.8 29.0 %collective-permute-start.26 = (f32[128,256]{1,0:T(8,128)S(1)}, f32[128,256]{1,0:T(8,128)S(1)}, u32[]{:S(2)}, u32[]{:S(2)}) collective-permute-start(f32[128,256]{1,0:T(8,128)S(1)} %get-tuple-element.69), channel_id=1, source_target_pairs={{0,2},{1,3},{2,0},{3,1},{4,6},{5,7},{6,4},{7,5},{8,10},{9,11},{10,... | collective-permute-start | bytes 393224 | tf_op jit(solution)/shard_map/ppermute | solution.py:399
  188.7 16.1 %collective-permute-start.27 = (f32[128,256]{1,0:T(8,128)S(1)}, f32[128,256]{1,0:T(8,128)S(1)}, u32[]{:S(2)}, u32[]{:S(2)}) collective-permute-start(f32[128,256]{1,0:T(8,128)S(1)} %get-tuple-element.70), channel_id=1, source_target_pairs={{0,1},{1,2},{2,3},{3,0},{4,5},{5,6},{6,7},{7,4},{8,9},{9,10},{10,1... | collective-permute-start | bytes 393224 | tf_op jit(solution)/shard_map/ppermute | solution.py:399
Sparse Core Ops, SparseCore 0:
  39.1 47.9 all-gather.2
  117.4 25.0 reduce-scatter.1

commit v2 on v1

--- a/solution.py
+++ b/solution.py
@@ -18,8 +18,11 @@
 taper = 0.5
 
 RADIX = 4
-LIMIT = 48 * 1024 * 1024
+BRIEF = pl.CostEstimate(flops=1000, bytes_accessed=1000, transcendentals=0)
+LONG = pl.CostEstimate(flops=10**11, bytes_accessed=10**7, transcendentals=0)
+LIMIT = 20 * 1024 * 1024
 F32 = jnp.float32
+ANY = pl.BlockSpec(memory_space=pl.ANY)
 BF16 = jnp.bfloat16
 
 
@@ -29,6 +32,10 @@
 
 def whole(shape):
     return pl.BlockSpec(shape, lambda *_: (0,) * len(shape))
+
+
+def far(arrays):
+    return [pltpu.with_memory_space_constraint(a, pltpu.HBM) for a in arrays]
 
 
 def omega_of(slot):
@@ -95,11 +102,21 @@
     return tuple(out)
 
 
-def convolve(x, high_ref, low_ref, left):
+def block_of(me, slot):
+    return lax.bitwise_xor(me, slot)
+
+
+def convolve(x, high_ref, low_ref, left, me):
     times = times_left if left else times_right
     x = spread_blocks(x)
-    at = [k if left else (RADIX - k) % RADIX for k in range(RADIX)]
-    return join_blocks([times(x[k], high_ref[at[k]], low_ref[at[k]]) for k in range(RADIX)])
+    flip = lax.bitwise_and(me, 1) * 2
+    y = []
+    for k in range(RADIX):
+        at = k if left else (RADIX - k) % RADIX
+        if k % 2 == 1:
+            at = lax.bitwise_xor(flip, at)
+        y.append(times(x[k], high_ref[at], low_ref[at]))
+    return join_blocks(y)
 
 
 def phase_parts(theta):
@@ -168,8 +185,10 @@
     ref[0], ref[1] = (value[1], value[0]) if swap else (value[0], value[1])
 
 
-def first_kernel(form, shift_ref, slot_ref, *refs):
+def first_kernel(form, waits, shift_ref, slot_ref, *refs):
     fields, refs = refs[:RADIX], refs[RADIX:]
+    if waits:
+        refs = refs[waits:]
     if form:
         table_ref, refs = refs[0], refs[1:]
         outs, (high_ref, low_ref) = refs[:RADIX], refs[RADIX:]
@@ -181,21 +200,21 @@
     else:
         (high_ref, low_ref), outs = refs[:2], refs[2:]
     x = [pick(f[:, 0], not form) for f in fields]
-    for ref, value in zip(outs, convolve(x, high_ref, low_ref, False)):
+    for ref, value in zip(outs, convolve(x, high_ref, low_ref, False, shift_ref[0])):
         store(ref, value, False)
 
 
-def first_stage(field, shift, slot, blocks, steps):
+def first_stage(field, shift, slot, blocks, steps, after=()):
     _, _, rows, width = field.shape
     block = width // RADIX
     part = rows // steps
     form = blocks is None
     shape = (RADIX, 2 * block, block)
     specs = [
-        pl.BlockSpec((2, 1, part, block), lambda i, sh, _, s=s: (0, 0, i, (sh[0] + s) % RADIX))
+        pl.BlockSpec((2, 1, part, block), lambda i, sh, _, s=s: (0, 0, i, block_of(sh[0], s)))
         for s in range(RADIX)
     ]
-    outs = [jax.ShapeDtypeStruct((2, rows, block), F32)] * RADIX
+    outs = [pltpu.HBM((2, rows, block), F32)] * RADIX
     out_specs = [pl.BlockSpec((2, part, block), lambda i, *_: (0, i, 0))] * RADIX
     if form:
         more = (cosine_table(width),)
@@ -204,37 +223,67 @@
     else:
         more = tuple(blocks)
     got = pl.pallas_call(
-        lambda *refs: first_kernel(form, *refs),
+        lambda *refs: first_kernel(form, len(after), *refs),
         grid_spec=pltpu.PrefetchScalarGridSpec(
             num_scalar_prefetch=2,
             grid=(steps,),
-            in_specs=specs + [whole(a.shape) for a in more],
+            in_specs=specs + [ANY] * len(after) + [whole(a.shape) for a in more],
             out_specs=out_specs,
         ),
         out_shape=outs,
         compiler_params=params(),
-        cost_estimate=pl.CostEstimate(flops=2 * 10**9, bytes_accessed=6 * 10**6, transcendentals=0),
+        cost_estimate=LONG,
         name="along_y_first_s" if form else "along_y_first_r",
-    )(shift, slot, *[field] * RADIX, *more)
+    )(shift, slot, *[field] * RADIX, *far(after), *more)
     return (got[:RADIX], tuple(got[RADIX:])) if form else (got, blocks)
 
 
-def middle_kernel(count, with_image, *refs):
-    fields, refs = refs[:RADIX], refs[RADIX:]
+def half_kernel(shift_ref, *refs):
+    fields, (high_ref, low_ref, out_ref) = refs[:RADIX], refs[RADIX:]
+    x = convolve([pick(f, False) for f in fields], high_ref, low_ref, True, shift_ref[0])
+    for s in range(RADIX):
+        store(out_ref.at[s], x[s], False)
+
+
+def half_stage(fields, blocks, shift):
+    _, rows, cols = fields[0].shape
+    args = list(fields) + list(blocks)
+    shape = (RADIX, 2, rows, cols)
+    return pl.pallas_call(
+        half_kernel,
+        grid_spec=pltpu.PrefetchScalarGridSpec(
+            num_scalar_prefetch=1,
+            grid=(1,),
+            in_specs=[whole(a.shape) for a in args],
+            out_specs=whole(shape),
+        ),
+        out_shape=jax.ShapeDtypeStruct(shape, F32),
+        compiler_params=params(),
+        cost_estimate=LONG,
+        name="along_x_s_first",
+    )(shift, *far(fields), *blocks)
+
+
+def middle_kernel(count, with_image, waits, shift_ref, *refs):
+    if with_image:
+        fields, refs = refs[:RADIX], refs[RADIX:]
+        other_ref, refs = refs[0], refs[1:]
+    else:
+        half_ref, refs = refs[0], refs[1:]
     cos_ref, sin_ref, high_ref, low_ref = refs[:4]
-    refs = refs[4:]
+    refs = refs[4 + waits :]
+    outs, extra = refs[: RADIX * count], refs[RADIX * count :]
     if with_image:
-        other_ref, refs = refs[0], refs[1:]
-    outs, extra = refs[: RADIX * count], refs[RADIX * count]
-    x = convolve([pick(f, False) for f in fields], high_ref, low_ref, True)
+        x = convolve([pick(f, False) for f in fields], high_ref, low_ref, True, shift_ref[0])
+    else:
+        x = [pick(half_ref.at[s], False) for s in range(RADIX)]
     x = [rotate(x[s], cos_ref[s], sin_ref[s]) for s in range(RADIX)]
     for s in range(RADIX):
         if with_image:
-            extra[s] = other_ref[s, 0] * x[s][1] + other_ref[s, 1] * x[s][0]
+            extra[0][s] = other_ref[s, 0] * x[s][1] + other_ref[s, 1] * x[s][0]
         else:
-            extra[s, 0] = x[s][0]
-            extra[s, 1] = x[s][1]
-    x = convolve(x, high_ref, low_ref, True)
+            store(extra[0].at[s], x[s], False)
+    x = convolve(x, high_ref, low_ref, True, shift_ref[0])
     part = x[0][0].shape[0] // count
     for s in range(RADIX):
         for c in range(count):
@@ -242,22 +291,27 @@
             store(outs[s * count + c], value, False)
 
 
-def middle_stage(fields, phases, blocks, count, other):
-    _, rows, cols = fields[0].shape
+def middle_stage(fields, phases, blocks, shift, count, other, after=()):
     with_image = other is not None
-    piece = jax.ShapeDtypeStruct((2, rows // count, cols), F32)
+    _, rows, cols = phases[0].shape
+    piece = pltpu.HBM((2, rows // count, cols), F32)
+    fields = far(fields) if with_image else fields
     extra = (RADIX, rows, cols) if with_image else (RADIX, 2, rows, cols)
-    args = list(fields) + list(phases) + list(blocks) + ([other] if with_image else [])
+    args = list(fields) + ([other] if with_image else []) + list(phases) + list(blocks)
     outs = [piece] * (RADIX * count) + [jax.ShapeDtypeStruct(extra, F32)]
     got = pl.pallas_call(
-        lambda *refs: middle_kernel(count, with_image, *refs),
-        in_specs=[whole(a.shape) for a in args],
-        out_specs=[whole(o.shape) for o in outs],
+        lambda *refs: middle_kernel(count, with_image, len(after), *refs),
+        grid_spec=pltpu.PrefetchScalarGridSpec(
+            num_scalar_prefetch=1,
+            grid=(1,),
+            in_specs=[whole(a.shape) for a in args] + [ANY] * len(after),
+            out_specs=[whole(o.shape) for o in outs],
+        ),
         out_shape=outs,
         compiler_params=params(),
-        cost_estimate=pl.CostEstimate(flops=4 * 10**9, bytes_accessed=12 * 10**6, transcendentals=0),
-        name="along_x_r" if with_image else "along_x_s",
-    )(*args)
+        cost_estimate=LONG,
+        name="along_x_r" if with_image else "along_x_s_second",
+    )(shift, *args, *far(after))
     pieces = [[got[s * count + c] for s in range(RADIX)] for c in range(count)]
     return pieces, got[-1]
 
@@ -273,9 +327,9 @@
         out_ref = refs[-1]
     block = fields[0].shape[2]
     omega = omega_of(slot_ref[0])
-    x = convolve([pick(f, False) for f in fields], high_ref, low_ref, False)
+    x = convolve([pick(f, False) for f in fields], high_ref, low_ref, False, shift_ref[0])
     for s in range(RADIX):
-        at = pl.ds(pl.multiple_of(lax.rem(shift_ref[0] + s, RADIX) * block, block), block)
+        at = pl.ds(pl.multiple_of(block_of(shift_ref[0], s) * block, block), block)
         theta = omega * (slab_ref[:, at] - ref_slow) * dz_km
         value = rotate(x[s], *phase_parts(theta))
         if with_image:
@@ -297,7 +351,7 @@
     with_image = other is not None
     row = start // part
     wide = pl.BlockSpec((2, 1, part, width), lambda i, *_: (0, 0, row, 0))
-    args = list(fields) + [slab] + list(blocks)
+    args = far(fields) + [slab] + list(blocks)
     specs = [whole(f.shape) for f in fields]
     specs += [pl.BlockSpec((part, width), lambda i, *_: (row, 0))]
     specs += [whole(b.shape) for b in blocks]
@@ -305,7 +359,7 @@
     out_specs = [wide]
     scratch = []
     if with_image:
-        args.append(other)
+        args += far([other])
         specs.append(wide)
         cols = width // RADIX
         outs += [jax.ShapeDtypeStruct((part, cols), F32)] * RADIX
@@ -314,8 +368,8 @@
     alias = {}
     if held is not None:
         alias = {3 + len(args): 0}
-        args.append(held)
-        specs.append(pl.BlockSpec(memory_space=pl.ANY))
+        args += far([held])
+        specs.append(ANY)
     got = pl.pallas_call(
         lambda *refs: last_kernel(with_image, *refs),
         grid_spec=pltpu.PrefetchScalarGridSpec(
@@ -328,40 +382,121 @@
         out_shape=outs,
         input_output_aliases=alias,
         compiler_params=params(),
-        cost_estimate=pl.CostEstimate(flops=10**9, bytes_accessed=6 * 10**6, transcendentals=0),
+        cost_estimate=LONG,
         name="along_y_last_r" if with_image else "along_y_last_s",
     )(shift, slot, place, *args)
     return got[0], got[1:]
 
 
-def phase_kernel(slot_ref, place_ref, *refs):
-    pieces, (cos_ref, sin_ref) = refs[:-2], refs[-2:]
-    count = len(pieces)
-    sub_rows = pieces[0].shape[1]
+def cut_kernel(shift_ref, shot_ref, place_ref, owner_ref, slab_ref, *outs):
+    part, block = outs[0].shape[1:]
+    for t in range(RADIX):
+        row = 2 * lax.rem(place_ref[0] + t, RADIX) + shot_ref[0]
+        rows = pl.ds(pl.multiple_of(row * part, part), part)
+        for s in range(RADIX):
+            cols = pl.ds(pl.multiple_of(block_of(shift_ref[0], s) * block, block), block)
+            outs[s][t] = slab_ref[0, rows, cols]
+    kept = (owner_ref[NZ - 1] == place_ref[0]).astype(F32)
+    outs[-1][...] = slab_ref[0] * kept
+
+
+def cut_stage(slowness, shift, shot, place, owner):
+    _, rows, width = slowness.shape
+    outs = [(RADIX, rows // (2 * RADIX), width // RADIX)] * RADIX + [(rows, width)]
+    got = pl.pallas_call(
+        cut_kernel,
+        grid_spec=pltpu.PrefetchScalarGridSpec(
+            num_scalar_prefetch=4,
+            grid=(1,),
+            in_specs=[whole(slowness.shape)],
+            out_specs=[whole(o) for o in outs],
+        ),
+        out_shape=[jax.ShapeDtypeStruct(o, F32) for o in outs],
+        compiler_params=params(),
+        cost_estimate=LONG,
+        name="cut_slab",
+    )(shift, shot, place, owner, slowness)
+    return got[:RADIX], got[RADIX]
+
+
+def regroup_kernel(*refs):
+    ins, outs = refs[:RADIX], refs[-RADIX:]
+    for t in range(RADIX):
+        for s in range(RADIX):
+            outs[t][s] = ins[s][t]
+
+
+def regroup_stage(pieces, after):
+    shape = pieces[0].shape
+    return pl.pallas_call(
+        regroup_kernel,
+        grid=(1,),
+        in_specs=[whole(shape)] * RADIX + [ANY],
+        out_specs=[whole(shape)] * RADIX,
+        out_shape=[jax.ShapeDtypeStruct(shape, F32)] * RADIX,
+        compiler_params=params(),
+        cost_estimate=LONG,
+        name="regroup_slab",
+    )(*pieces, after)
+
+
+def choose_kernel(place_ref, owner_ref, *refs):
+    pieces, out_ref = refs[:RADIX], refs[-1]
+    at = lax.rem(owner_ref[0] - place_ref[0] + RADIX, RADIX)
+    for t, piece in enumerate(pieces):
+
+        @pl.when(at == t)
+        def _():
+            out_ref[...] = piece[...]
+
+
+def choose_stage(pieces, place, owner, after):
+    shape = pieces[0].shape
+    return pl.pallas_call(
+        choose_kernel,
+        grid_spec=pltpu.PrefetchScalarGridSpec(
+            num_scalar_prefetch=2,
+            grid=(1,),
+            in_specs=[whole(shape)] * RADIX + [ANY] * len(after),
+            out_specs=whole(shape),
+        ),
+        out_shape=jax.ShapeDtypeStruct(shape, F32),
+        compiler_params=params(),
+        cost_estimate=LONG,
+        name="choose_slab",
+    )(place, owner, *pieces, *far(after))
+
+
+def phase_kernel(slot_ref, place_ref, shot_ref, *refs):
+    pieces, (cos_ref, sin_ref) = refs[: 2 * RADIX], refs[-2:]
+    part = pieces[0].shape[1]
     omega = omega_of(slot_ref[0])
-    for t in range(count):
-        at = pl.ds(pl.multiple_of(lax.rem(place_ref[0] + t, count) * sub_rows, 8), sub_rows)
+    for n, piece in enumerate(pieces):
+        t, other = n % RADIX, n // RADIX
+        shot = shot_ref[0] if other == 0 else 1 - shot_ref[0]
+        row = 2 * lax.rem(place_ref[0] + t, RADIX) + shot
+        at = pl.ds(pl.multiple_of(row * part, part), part)
         for s in range(RADIX):
-            theta = omega * (pieces[t][s] - ref_slow) * dz_km
+            theta = omega * (piece[s] - ref_slow) * dz_km
             cos_ref[s, at, :], sin_ref[s, at, :] = phase_parts(theta)
 
 
-def phase_stage(pieces, slot, place):
-    _, sub_rows, cols = pieces[0].shape
-    shape = (RADIX, sub_rows * len(pieces), cols)
+def phase_stage(pieces, slot, place, shot, after):
+    _, part, cols = pieces[0].shape
+    shape = (RADIX, part * len(pieces), cols)
     return pl.pallas_call(
         phase_kernel,
         grid_spec=pltpu.PrefetchScalarGridSpec(
-            num_scalar_prefetch=2,
+            num_scalar_prefetch=3,
             grid=(1,),
-            in_specs=[whole(p.shape) for p in pieces],
+            in_specs=[whole(p.shape) for p in pieces] + [ANY],
             out_specs=[whole(shape)] * 2,
         ),
         out_shape=[jax.ShapeDtypeStruct(shape, F32)] * 2,
         compiler_params=params(),
-        cost_estimate=pl.CostEstimate(flops=10**7, bytes_accessed=3 * 10**6, transcendentals=0),
+        cost_estimate=BRIEF,
         name="phases",
-    )(slot, place, *pieces)
+    )(slot, place, shot, *pieces, after)
 
 
 def image_kernel(chunks, early_ref, *refs):
@@ -384,7 +519,7 @@
         lambda *refs: image_kernel(len(groups), *refs),
         out_shape=jax.ShapeDtypeStruct((NZ, rows, cols), F32),
         compiler_params=params(),
-        cost_estimate=pl.CostEstimate(flops=10**6, bytes_accessed=3 * 10**6, transcendentals=0),
+        cost_estimate=LONG,
         name="image_sum",
     )(*args)
 
@@ -398,6 +533,13 @@
     count = len(pieces)
     sent = [lax.ppermute(pieces[s], axis, [(i, (i + s) % count) for i in range(count)]) for s in range(1, count)]
     return [pieces[0]] + [sent[count - s - 1] for s in range(1, count)]
+
+
+def swap_pairs(pieces, axis):
+    count = len(pieces)
+    return [pieces[0]] + [
+        lax.ppermute(pieces[s], axis, [(i, i ^ s) for i in range(count)]) for s in range(1, count)
+    ]
 
 
 def gather_slots(piece, axis):
@@ -413,39 +555,37 @@
     freq_count = lax.axis_size("freq")
     row_at = lax.axis_index("row")
     place = lax.axis_index("freq")[None]
+    shot = lax.axis_index("shot")[None]
     slot = freq_index
     ringed = row_count == RADIX and freq_count == RADIX and slowness.shape[0] == 1
+    ringed = ringed and lax.axis_size("shot") == 2
     shift = row_at[None] if ringed else jnp.zeros((1,), jnp.int32)
     if not ringed:
         return general(source_field, receiver_field, slowness, owner, slot, shift, place)
-    block = width // RADIX
-    sub_rows = rows // RADIX
-
-    s_first, blocks = first_stage(source_field, shift, slot, None, 2)
-    s_mid = swap_slots(s_first, "row")
-    slab = slowness[0].reshape(RADIX, sub_rows, width)
-    mine = [lax.dynamic_index_in_dim(slab, (place[0] + t) % RADIX, 0, keepdims=False) for t in range(RADIX)]
-    shares = swap_slots(mine, "freq")
-    r_first, _ = first_stage(receiver_field, shift, slot, blocks, 2)
-    r_mid = swap_slots(r_first, "row")
-    stack = jnp.stack(shares)
-    early, late = [lax.dynamic_index_in_dim(stack, (owner[z] - place[0]) % RADIX, 0, keepdims=False) for z in range(NZ)]
-    turned = early.reshape(sub_rows, RADIX, block)
-    turned = [lax.dynamic_index_in_dim(turned, (row_at + s) % RADIX, 1, keepdims=False) for s in range(RADIX)]
-    turned = jnp.stack(swap_slots(turned, "row"))
-    phases = phase_stage(gather_slots(turned, "freq"), slot, place)
-    late = lax.all_gather(late, "freq", axis=0, tiled=True)
-
-    s_pieces, s_held = middle_stage(s_mid, phases, blocks, 1, None)
-    s_last = swap_slots(s_pieces[0], "row")
-    r_pieces, term = middle_stage(r_mid, phases, blocks, CHUNKS, s_held)
-    r_last = [swap_slots(p, "row") for p in r_pieces]
-    first_image = lax.psum_scatter(term, "freq", scatter_dimension=0, tiled=False)
+
+    turned, late = cut_stage(slowness, shift, shot, place, owner)
+    turned = swap_pairs(turned, "row")
+    late = lax.psum(late, "freq")
+    s_first, blocks = first_stage(source_field, shift, slot, None, 2, (turned[0],))
+    s_mid = swap_pairs(s_first, "row")
+    r_first, _ = first_stage(receiver_field, shift, slot, blocks, 2, turned[1:])
+    r_mid = swap_pairs(r_first, "row")
+    shares = swap_slots(regroup_stage(turned, r_first[0]), "freq")
+    gathered = gather_slots(choose_stage(shares, place, owner, [s_mid[2], r_mid[2]]), "freq")
+    gathered += [lax.ppermute(g, "shot", [(0, 1), (1, 0)]) for g in gathered]
+    s_half = half_stage(s_mid, blocks, shift)
+    phases = phase_stage(gathered, slot, place, shot, s_half)
+
+    s_pieces, s_held = middle_stage([s_half], phases, blocks, shift, 1, None, r_mid[1:])
+    s_last = swap_pairs(s_pieces[0], "row")
+    r_pieces, term = middle_stage(r_mid, phases, blocks, shift, CHUNKS, s_held)
+    r_last = [swap_pairs(p, "row") for p in r_pieces]
+    total = lax.psum_scatter(term, "freq", scatter_dimension=0, tiled=False)
     pairs = []
     for r in range(RADIX):
         for f in range(RADIX):
-            pairs.append((r * RADIX + f, ((r + f) % RADIX) * RADIX + r))
-    first_image = lax.ppermute(first_image, ("row", "freq"), pairs)
+            pairs.append((r * RADIX + f, (r ^ f) * RADIX + r))
+    first_image = lax.ppermute(total, ("row", "freq"), pairs)
 
     source_out, _ = last_stage(s_last, late, blocks, shift, slot, place, 0, rows, None, None)
     receiver_out, groups = None, []
@@ -482,8 +622,8 @@
     theta = omega_of(slot[0]) * (turned - ref_slow) * dz_km
     theta = theta.reshape(RADIX, -1, theta.shape[1])
     phases = (jnp.cos(theta), jnp.sin(theta))
-    s_pieces, s_held = middle_stage(s_mid, phases, blocks, 1, None)
-    r_pieces, term = middle_stage(r_mid, phases, blocks, 1, s_held)
+    s_pieces, s_held = middle_stage([half_stage(s_mid, blocks, shift)], phases, blocks, shift, 1, None)
+    r_pieces, term = middle_stage(r_mid, phases, blocks, shift, 1, s_held)
     s_last = jnp.split(to_rows(s_pieces[0]), RADIX, axis=2)
     r_last = jnp.split(to_rows(r_pieces[0]), RADIX, axis=2)
     source_out, _ = last_stage(s_last, slabs[1], blocks, shift, slot, shift, 0, rows, None, None)

time: 213 us -> 178 us (0.84)
  waiting for transfers between devices: 102 us -> 63 us
  starting transfers between devices: 33.9 us -> 44.4 us
  local copies, waits for them, and re-layouts: 21.3 us -> 14 us
  Pallas kernels: 37.3 us -> 41.1 us
    ppermute x27 -> x9, waiting for transfers between devices: 80.4 us -> 29.5 us  [swap_slots(): lax.ppermute(pieces[s], axis, [(i, (i + s) % count) for i in range(count)])]
    ppermute x1 -> x23, waiting for transfers between devices: 0.01 us -> 29.9 us  [the longest x18 26.5 us: swap_pairs(): lax.ppermute(pieces[s], axis, [(i, i ^ s) for i in range(count)])]
    ppermute x3, waiting for transfers between devices: 22 us -> 1.93 us  [shifted(): lax.ppermute(value, axis, [((i + step) % count, i) for i in range(count)])]
    ppermute x1 -> x23, starting transfers between devices: 1.6 us -> 19.8 us  [the longest x18 12.8 us: swap_pairs(): lax.ppermute(pieces[s], axis, [(i, i ^ s) for i in range(count)])]
    ppermute x27 -> x9, starting transfers between devices: 25.6 us -> 19.7 us  [swap_slots(): lax.ppermute(pieces[s], axis, [(i, (i + s) % count) for i in range(count)])]
    dynamic_slice x3 -> x0, local copies, waits for them, and re-layouts: 4.43 us -> none  [the longest x1 2.08 us: body(): lax.dynamic_index_in_dim(slab, (place[0] + t) % RADIX, 0, keepdims=False)]
    pallas_call x4 -> x8, Pallas kernels: 23.2 us -> 24.9 us  [the longest x2 11.1 us: middle_stage(): pl.pallas_call(lambda *refs: middle_kernel(count, with_image, len(after),...]
    unnamed x62 -> x64, local copies, waits for them, and re-layouts: 15.4 us -> 14 us
  transfers between devices with their start and end apart: 33 -> 37, of which waited for: 12 -> 15; matrix products, arithmetic and copies ran while one was open for 2% -> 0% of each run, Pallas kernels for 17% -> 22%
where the time goes in v2:
time: 178 us; the launch traced here: 177 us
  waiting for transfers between devices  63 us (35%)
  starting transfers between devices  44.4 us (25%)
  Pallas kernels  41.1 us (23%)
  between operations  14.9 us (8%)
  local copies, waits for them, and re-layouts  14 us (8%)
    ppermute x9, waiting for transfers between devices, swap_slots(): lax.ppermute(pieces[s], axis, [(i, (i + s) % count) for i in range(count)])  29.5 us
    ppermute x18, waiting for transfers between devices, swap_pairs(): lax.ppermute(pieces[s], axis, [(i, i ^ s) for i in range(count)])  26.5 us
    ppermute x9, starting transfers between devices, swap_slots(): lax.ppermute(pieces[s], axis, [(i, (i + s) % count) for i in range(count)])  19.7 us
    pallas_call x3, Pallas kernels, last_stage(): pl.pallas_call(lambda *refs: last_kernel(with_image, *refs), grid_spec=pl...  14.6 us
    unnamed x64, local copies, waits for them, and re-layouts  14 us
    ppermute x18, starting transfers between devices, swap_pairs(): lax.ppermute(pieces[s], axis, [(i, i ^ s) for i in range(count)])  12.8 us
    pallas_call x2, Pallas kernels, middle_stage(): pl.pallas_call(lambda *refs: middle_kernel(count, with_image, len(after),...  11.1 us
    pallas_call x2, Pallas kernels, first_stage(): pl.pallas_call(lambda *refs: first_kernel(form, len(after), *refs), grid_...  7.98 us
  transfers between devices with their start and end apart: 37, of which 15 were waited for; matrix products, arithmetic and copies ran while one was open for 0% of the time, Pallas kernels for 22%

profile of v2, /device:TPU:0, one launch (start us, length us, event | category | flops | bytes accessed | tf_op | source)
XLA Modules:
  0.0 177.4 jit_solution(1597918074707371664)
XLA Ops:
  7.2 1.2 copy-done.2
  8.4 0.7 copy-done.11
  9.1 1.6 cut_slab.1
  10.7 0.6 copy-done.21
  11.8 2.5 %collective-permute-start.4 = (f32[4,32,256]{2,1,0:T(8,128)S(1)}, f32[4,32,256]{2,1,0:T(8,128)S(1)}, u32[]{:S(2)}, u32[]{:S(2)}) collective-permute-start(f32[4,32,256]{2,1,0:T(8,128)S(1)} %get-tuple-element.56), channel_id=1, source_target_pairs={{0,8},{4,12},{8,0},{12,4},{1,9},{5,13},{9,1},{13,5},{2,10},{6,14},... | collective-permute-start | bytes 393224 | tf_op jit(solution)/shard_map/ppermute | solution.py:541
  15.1 4.5 %along_y_first_s.1 = (f32[2,256,256]{2,1,0:T(8,128)}, f32[2,256,256]{2,1,0:T(8,128)}, f32[2,256,256]{2,1,0:T(8,128)}, f32[2,256,256]{2,1,0:T(8,128)}, bf16[4,512...) custom-call(s32[1]{0:T(128)} %bitcast.shift_ref.refs_0_, s32[1]{0:T(128)S(6)} %copy.12.refs_1_.slot_ref, ...), custom_call_target="tpu_custom_call" | custom-call | flops 99999997952 | bytes 10000000 | tf_op jit(solution)/shard_map/along_y_first_s/pallas_call | solution.py:225
  19.7 1.7 collective-permute-start.1
  21.4 0.6 copy-done.5
  22.1 3.5 %along_y_first_r.1 = (f32[2,256,256]{2,1,0:T(8,128)}, f32[2,256,256]{2,1,0:T(8,128)}, f32[2,256,256]{2,1,0:T(8,128)}, f32[2,256,256]{2,1,0:T(8,128)}) custom-call(s32[1]{0:T(128)} %bitcast.shift_ref.refs_0_, s32[1]{0:T(128)S(6)} %copy.12.refs_1_.slot_ref, f32[2,1,256,1024]{3,2,1,0:T(8,128)S(1)} %copy-done.1, f32[2,1,256,1024]{3,2,1,0:T(8,128)S(1)} %copy-done.1, ...), custom_call_target="tpu_custom_call" | custom-call | flops 99999997952 | bytes 10000000 | tf_op jit(solution)/shard_map/along_y_first_r/pallas_call | solution.py:225
  25.6 1.0 copy-done.14
  26.6 1.0 copy-done.16
  27.6 1.2 collective-permute-start.9
  28.7 0.9 copy-done.6
  29.6 0.9 copy-done.8
  30.5 0.9 copy-done.10
  31.5 1.0 copy-done.20
  32.5 3.7 %collective-permute-start.6 = (f32[4,32,256]{2,1,0:T(8,128)S(1)}, f32[4,32,256]{2,1,0:T(8,128)S(1)}, u32[]{:S(2)}, u32[]{:S(2)}) collective-permute-start(f32[4,32,256]{2,1,0:T(8,128)S(1)} %get-tuple-element.60), channel_id=1, source_target_pairs={{0,3},{1,0},{2,1},{3,2},{4,7},{5,4},{6,5},{7,6},{8,11},{9,8},{10,9... | collective-permute-start | bytes 393224 | tf_op jit(solution)/shard_map/ppermute | solution.py:534
  36.2 1.0 collective-permute-start.8
  37.2 2.9 %collective-permute-done.6.refs_1_ = f32[4,32,256]{2,1,0:T(8,128)S(1)} collective-permute-done((f32[4,32,256]{2,1,0:T(8,128)S(1)}, f32[4,32,256]{2,1,0:T(8,128)S(1)}, u32[]{:S(2)}, u32[]{:S(2)}) %collective-permute-start.6) | collective-permute-done | bytes 131104 | tf_op jit(solution)/shard_map/ppermute | solution.py:534
  40.1 7.4 %collective-permute-done.7.refs_2_ = f32[4,32,256]{2,1,0:T(8,128)S(1)} collective-permute-done((f32[4,32,256]{2,1,0:T(8,128)S(1)}, f32[4,32,256]{2,1,0:T(8,128)S(1)}, u32[]{:S(2)}, u32[]{:S(2)}) %collective-permute-start.7) | collective-permute-done | bytes 131104 | tf_op jit(solution)/shard_map/ppermute | solution.py:534
  47.6 0.8 copy-done.23
  49.0 1.6 collective-permute-start.10
  50.6 1.1 collective-permute-start.11
  51.7 1.9 %collective-permute-start.12 = (f32[4,32,256]{2,1,0:T(8,128)S(1)}, f32[4,32,256]{2,1,0:T(8,128)S(1)}, u32[]{:S(2)}, u32[]{:S(2)}) collective-permute-start(f32[4,32,256]{2,1,0:T(8,128)S(1)} %choose_slab.1.refs_0_), channel_id=1, source_target_pairs={{3,0},{0,1},{1,2},{2,3},{7,4},{4,5},{5,6},{6,7},{11,8},{8,9},{9,10... | collective-permute-start | bytes 393224 | tf_op jit(solution)/shard_map/ppermute | solution.py:529
  53.6 0.8 copy-done.26
  54.4 1.5 collective-permute-start.13
  56.2 5.5 %collective-permute-done.2.refs_3_ = f32[2,256,256]{2,1,0:T(8,128)} collective-permute-done((f32[2,256,256]{2,1,0:T(8,128)}, f32[2,256,256]{2,1,0:T(8,128)}, u32[]{:S(2)}, u32[]{:S(2)}) %collective-permute-start.2) | collective-permute-done | bytes 524320 | tf_op jit(solution)/shard_map/ppermute | solution.py:541
  61.7 1.0 collective-permute-start.18
  62.7 1.9 %collective-permute-done.11.refs_2_ = f32[4,32,256]{2,1,0:T(8,128)S(1)} collective-permute-done((f32[4,32,256]{2,1,0:T(8,128)S(1)}, f32[4,32,256]{2,1,0:T(8,128)S(1)}, u32[]{:S(2)}, u32[]{:S(2)}) %collective-permute-start.11) | collective-permute-done | bytes 131104 | tf_op jit(solution)/shard_map/ppermute | solution.py:529
  64.6 1.9 %collective-permute-start.14 = (f32[4,32,256]{2,1,0:T(8,128)S(1)}, f32[4,32,256]{2,1,0:T(8,128)S(1)}, u32[]{:S(2)}, u32[]{:S(2)}) collective-permute-start(f32[4,32,256]{2,1,0:T(8,128)S(1)} %collective-permute-done.10.refs_1_), channel_id=1, source_target_pairs={{0,16},{16,0},{1,17},{17,1},{2,18},{18,2},{3,19},{19,3},{4,20},{20... | collective-permute-start | bytes 393224 | tf_op jit(solution)/shard_map/ppermute | solution.py:575
  66.7 1.9 %collective-permute-start.16 = (f32[4,32,256]{2,1,0:T(8,128)S(1)}, f32[4,32,256]{2,1,0:T(8,128)S(1)}, u32[]{:S(2)}, u32[]{:S(2)}) collective-permute-start(f32[4,32,256]{2,1,0:T(8,128)S(1)} %collective-permute-done.12.refs_3_), channel_id=1, source_target_pairs={{0,16},{16,0},{1,17},{17,1},{2,18},{18,2},{3,19},{19,3},{4,20},{20... | collective-permute-start | bytes 393224 | tf_op jit(solution)/shard_map/ppermute | solution.py:575
  68.6 3.6 %along_x_s_first.1.refs_8_.refs_1_ = f32[4,2,256,256]{3,2,1,0:T(8,128)S(1)} custom-call(s32[1]{0:T(128)} %bitcast.shift_ref.refs_0_, f32[2,256,256]{2,1,0:T(8,128)} %get-tuple-element.49.refs_0_, f32[2,256,256]{2,1,0:T(8,128)} %copy-done.26, f32[2,256,256]{2,1,0:T(8,128)} %collective-permute-done.1.refs_2_.refs_4_, ...), custom_call_target="tpu_custom_call" | custom-call | flops 99999997952 | bytes 10000000 | tf_op jit(solution)/shard_map/along_x_s_first/pallas_call | solution.py:252
  72.2 1.6 collective-permute-done.15.refs_6_
  73.8 1.7 collective-permute-done.16.refs_7_
  75.6 0.8 phases.1
  76.4 0.8 copy-done.27
  77.3 3.6 %along_x_s_second.1 = (f32[2,256,256]{2,1,0:T(8,128)}, f32[2,256,256]{2,1,0:T(8,128)}, f32[2,256,256]{2,1,0:T(8,128)}, f32[2,256,256]{2,1,0:T(8,128)}, f32[4,2,256,256]{3,2,1,0:T(8,128)S(1)}) custom-call(s32[1]{0:T(128)} %bitcast.shift_ref.refs_0_, f32[4,2,256,256]{3,2,1,0:T(8,128)S(1)} %along_x_s_first.1.refs_8_.refs_1_, ...), custom_call_target="tpu_custom_call" | custom-call | flops 99999997952 | bytes 10000000 | tf_op jit(solution)/shard_map/along_x_s_second/pallas_call | solution.py:302
  80.9 0.6 collective-permute-start.20
  81.6 1.2 collective-permute-start.21
  82.8 7.5 %along_x_r.1 = (f32[2,128,256]{2,1,0:T(8,128)}, f32[2,128,256]{2,1,0:T(8,128)}, f32[2,128,256]{2,1,0:T(8,128)}, f32[2,128,256]{2,1,0:T(8,128)}, f32[2,128,256]{2...) custom-call(s32[1]{0:T(128)} %bitcast.shift_ref.refs_0_, ...), custom_call_target="tpu_custom_call" | custom-call | flops 99999997952 | bytes 10000000 | tf_op jit(solution)/shard_map/along_x_r/pallas_call | solution.py:302
  90.6 0.6 collective-permute-start.23
  91.4 4.5 %collective-permute-done.20.refs_5_ = f32[2,256,256]{2,1,0:T(8,128)S(1)} collective-permute-done((f32[2,256,256]{2,1,0:T(8,128)}, f32[2,256,256]{2,1,0:T(8,128)S(1)}, u32[]{:S(2)}, u32[]{:S(2)}) %collective-permute-start.20) | collective-permute-done | bytes 524320 | tf_op jit(solution)/shard_map/ppermute | solution.py:541
  95.9 0.7 collective-permute-start.26
  96.5 9.9 %collective-permute-done.21.refs_6_ = f32[2,256,256]{2,1,0:T(8,128)} collective-permute-done((f32[2,256,256]{2,1,0:T(8,128)}, f32[2,256,256]{2,1,0:T(8,128)}, u32[]{:S(2)}, u32[]{:S(2)}) %collective-permute-start.21) | collective-permute-done | bytes 524320 | tf_op jit(solution)/shard_map/ppermute | solution.py:541
  106.4 1.2 collective-permute-start.27
  107.6 0.6 all-reduce.2.cloned.1.call-done.refs_7_
  108.2 1.2 copy-done.3
  109.4 6.2 %along_y_last_s.1.refs_10_ = f32[2,1,256,1024]{3,2,1,0:T(8,128)} custom-call(s32[1]{0:T(128)} %bitcast.shift_ref.refs_0_, s32[1]{0:T(128)S(6)} %copy.12.refs_1_.slot_ref, s32[1]{0:T(128)} %bitcast.1.place_ref.refs_2_, f32[2,256,256]{2,1,0:T(8,128)} %get-tuple-element.68.refs_3_, f32[2,256,256]{2,1,0:T(8,128)} %copy-done.29, f32[2,256,256]{2,1,0:T(8,128)} %copy-done.30, ...), custom_call_target="tpu_custom_call" | custom-call | flops 99999997952 | bytes 10000000 | tf_op jit(solution)/shard_map/along_y_last_s/pallas_call | solution.py:373
  115.6 1.1 collective-permute-start.24
  116.7 1.7 collective-permute-done.26.refs_5_
  118.4 4.8 %collective-permute-done.27.refs_6_ = f32[2,128,256]{2,1,0:T(8,128)} collective-permute-done((f32[2,128,256]{2,1,0:T(8,128)}, f32[2,128,256]{2,1,0:T(8,128)}, u32[]{:S(2)}, u32[]{:S(2)}) %collective-permute-start.27) | collective-permute-done | bytes 262176 | tf_op jit(solution)/shard_map/ppermute | solution.py:541
  123.3 4.3 %along_y_last_r.2 = (f32[2,1,256,1024]{3,2,1,0:T(8,128)}, f32[128,256]{1,0:T(8,128)S(1)}, f32[128,256]{1,0:T(8,128)S(1)}, f32[128,256]{1,0:T(8,128)S(1)}, f32[128,256]{1,0:T(8,128)S(1)}) custom-call(s32[1]{0:T(128)} %bitcast.shift_ref.refs_0_, s32[1]{0:T(128)S(6)} %copy.12.refs_1_.slot_ref, s32[1]{0:T(128)} %bitcast.1.place_ref.refs_2_, ...), custom_call_target="tpu_custom_call" | custom-call | flops 99999997952 | bytes 10000000 | tf_op jit(solution)/shard_map/along_y_last_r/pallas_call | solution.py:373
  128.1 6.0 %collective-permute-start.30 = (f32[128,256]{1,0:T(8,128)S(1)}, f32[128,256]{1,0:T(8,128)S(1)}, u32[]{:S(2)}, u32[]{:S(2)}) collective-permute-start(f32[128,256]{1,0:T(8,128)S(1)} %get-tuple-element.87), channel_id=1, source_target_pairs={{0,2},{1,3},{2,0},{3,1},{4,6},{5,7},{6,4},{7,5},{8,10},{9,11},{10,... | collective-permute-start | bytes 393224 | tf_op jit(solution)/shard_map/ppermute | solution.py:534
  134.1 2.0 %collective-permute-start.31 = (f32[128,256]{1,0:T(8,128)S(1)}, f32[128,256]{1,0:T(8,128)S(1)}, u32[]{:S(2)}, u32[]{:S(2)}) collective-permute-start(f32[128,256]{1,0:T(8,128)S(1)} %get-tuple-element.88), channel_id=1, source_target_pairs={{0,1},{1,2},{2,3},{3,0},{4,5},{5,6},{6,7},{7,4},{8,9},{9,10},{10,1... | collective-permute-start | bytes 393224 | tf_op jit(solution)/shard_map/ppermute | solution.py:534
  136.1 1.0 reduce-scatter.2.cloned.1.call-done
  137.2 1.6 collective-permute-start.28
  138.8 1.2 copy-done.19
  140.0 4.2 %along_y_last_r.3 = (f32[2,1,256,1024]{3,2,1,0:T(8,128)}, f32[128,256]{1,0:T(8,128)S(1)}, f32[128,256]{1,0:T(8,128)S(1)}, f32[128,256]{1,0:T(8,128)S(1)}, f32[128,256]{1,0:T(8,128)S(1)}) custom-call(s32[1]{0:T(128)} %bitcast.shift_ref.refs_0_, s32[1]{0:T(128)S(6)} %copy.12.refs_1_.slot_ref, ...), custom_call_target="tpu_custom_call", output_to_operand_aliasing={{0}: (11, {})} | custom-call | flops 99999997952 | bytes 10000000 | tf_op jit(solution)/shard_map/along_y_last_r/pallas_call | solution.py:373
  144.1 4.7 %collective-permute-start.32 = (f32[128,256]{1,0:T(8,128)S(1)}, f32[128,256]{1,0:T(8,128)S(1)}, u32[]{:S(2)}, u32[]{:S(2)}) collective-permute-start(f32[128,256]{1,0:T(8,128)S(1)} %get-tuple-element.90), channel_id=1, source_target_pairs={{0,3},{1,0},{2,1},{3,2},{4,7},{5,4},{6,5},{7,6},{8,11},{9,8},{10,9... | collective-permute-start | bytes 393224 | tf_op jit(solution)/shard_map/ppermute | solution.py:534
  148.9 1.7 collective-permute-start.33
  150.6 2.4 %collective-permute-done.30.refs_3_ = f32[128,256]{1,0:T(8,128)S(1)} collective-permute-done((f32[128,256]{1,0:T(8,128)S(1)}, f32[128,256]{1,0:T(8,128)S(1)}, u32[]{:S(2)}, u32[]{:S(2)}) %collective-permute-start.30) | collective-permute-done | bytes 131104 | tf_op jit(solution)/shard_map/ppermute | solution.py:534
  152.9 4.1 %collective-permute-done.32.refs_6_ = f32[128,256]{1,0:T(8,128)S(1)} collective-permute-done((f32[128,256]{1,0:T(8,128)S(1)}, f32[128,256]{1,0:T(8,128)S(1)}, u32[]{:S(2)}, u32[]{:S(2)}) %collective-permute-start.32) | collective-permute-done | bytes 131104 | tf_op jit(solution)/shard_map/ppermute | solution.py:534
  157.0 12.7 %collective-permute-done.33.refs_7_ = f32[128,256]{1,0:T(8,128)S(1)} collective-permute-done((f32[128,256]{1,0:T(8,128)S(1)}, f32[128,256]{1,0:T(8,128)S(1)}, u32[]{:S(2)}, u32[]{:S(2)}) %collective-permute-start.33) | collective-permute-done | bytes 131104 | tf_op jit(solution)/shard_map/ppermute | solution.py:534
  169.7 0.9 image_sum.1
  (89 shorter events, 3.0 us)
Async XLA Ops:
  7.2 101.0 %all-reduce.2.cloned.1.call-start = ((), (), s32[]{:S(2)}) async-start(), calls=%async_computation.1 | async-start | bytes 2097152 | tf_op jit(solution)/shard_map/psum | solution.py:568
  7.2 1.2 copy-start.2
  9.1 6.0 %copy-start = (f32[2,1,256,1024]{3,2,1,0:T(8,128)S(1)}, f32[2,1,256,1024]{3,2,1,0:T(8,128)}, u32[]{:S(2)}) copy-start(f32[2,1,256,1024]{3,2,1,0:T(8,128)} %refs_5_.2) | copy-start | bytes 6291460
  9.1 6.0 %copy-start.13 = (f32[512,1024]{1,0:T(8,128)S(1)}, f32[512,1024]{1,0:T(8,128)}, u32[]{:S(2)}) copy-start(f32[512,1024]{1,0:T(8,128)} %constant.15.clone.refs_7_) | copy-start | bytes 6291460
  11.4 10.0 %collective-permute-start.3 = (f32[4,32,256]{2,1,0:T(8,128)S(1)}, f32[4,32,256]{2,1,0:T(8,128)S(1)}, u32[]{:S(2)}, u32[]{:S(2)}) collective-permute-start(f32[4,32,256]{2,1,0:T(8,128)S(1)} %get-tuple-element.55), channel_id=1, source_target_pairs={{0,4},{4,0},{8,12},{12,8},{1,5},{5,1},{9,13},{13,9},{2,6},{6,2},{1... | collective-permute-start | bytes 393224 | tf_op jit(solution)/shard_map/ppermute | solution.py:541
  11.8 9.6 %collective-permute-start.4 = (f32[4,32,256]{2,1,0:T(8,128)S(1)}, f32[4,32,256]{2,1,0:T(8,128)S(1)}, u32[]{:S(2)}, u32[]{:S(2)}) collective-permute-start(f32[4,32,256]{2,1,0:T(8,128)S(1)} %get-tuple-element.56), channel_id=1, source_target_pairs={{0,8},{4,12},{8,0},{12,4},{1,9},{5,13},{9,1},{13,5},{2,10},{6,14},... | collective-permute-start | bytes 393224 | tf_op jit(solution)/shard_map/ppermute | solution.py:541
  14.3 7.1 %collective-permute-start.5 = (f32[4,32,256]{2,1,0:T(8,128)S(1)}, f32[4,32,256]{2,1,0:T(8,128)S(1)}, u32[]{:S(2)}, u32[]{:S(2)}) collective-permute-start(f32[4,32,256]{2,1,0:T(8,128)S(1)} %get-tuple-element.57), channel_id=1, source_target_pairs={{0,12},{4,8},{8,4},{12,0},{1,13},{5,9},{9,5},{13,1},{2,14},{6,10},... | collective-permute-start | bytes 393224 | tf_op jit(solution)/shard_map/ppermute | solution.py:541
  15.1 7.0 %copy-start.1 = (f32[2,1,256,1024]{3,2,1,0:T(8,128)S(1)}, f32[2,1,256,1024]{3,2,1,0:T(8,128)}, u32[]{:S(2)}) copy-start(f32[2,1,256,1024]{3,2,1,0:T(8,128)} %refs_5_.3) | copy-start | bytes 6291460
  19.7 27.9 %collective-permute-start.1 = (f32[2,256,256]{2,1,0:T(8,128)}, f32[2,256,256]{2,1,0:T(8,128)}, u32[]{:S(2)}, u32[]{:S(2)}) collective-permute-start(f32[2,256,256]{2,1,0:T(8,128)} %get-tuple-element.51), channel_id=1, source_target_pairs={{0,8},{4,12},{8,0},{12,4},{1,9},{5,13},{9,1},{13,5},{2,10},{6,14},... | collective-permute-start | bytes 1572872 | tf_op jit(solution)/shard_map/ppermute | solution.py:541
  22.1 6.6 %copy-start.22 = (f32[4,32,256]{2,1,0:T(8,128)S(1)}, f32[4,32,256]{2,1,0:T(8,128)}, u32[]{:S(2)}) copy-start(f32[4,32,256]{2,1,0:T(8,128)} %copy-done.21) | copy-start | bytes 393220
  25.6 1.0 copy-start.14
  26.6 1.0 copy-start.16
  27.6 20.0 %collective-permute-start.9 = (f32[2,256,256]{2,1,0:T(8,128)}, f32[2,256,256]{2,1,0:T(8,128)S(1)}, u32[]{:S(2)}, u32[]{:S(2)}) collective-permute-start(f32[2,256,256]{2,1,0:T(8,128)} %get-tuple-element.63), channel_id=1, source_target_pairs={{0,8},{4,12},{8,0},{12,4},{1,9},{5,13},{9,1},{13,5},{2,10},{6,14},... | collective-permute-start | bytes 1572872 | tf_op jit(solution)/shard_map/ppermute | solution.py:541
  28.7 0.9 copy-start.6
  29.6 0.9 copy-start.8
  30.5 0.9 copy-start.10
  31.4 1.0 copy-start.20
  32.5 7.6 %copy-start.25 = (f32[2,256,256]{2,1,0:T(8,128)S(1)}, f32[2,256,256]{2,1,0:T(8,128)}, u32[]{:S(2)}) copy-start(f32[2,256,256]{2,1,0:T(8,128)} %get-tuple-element.50) | copy-start | bytes 1572868
  32.5 15.9 %copy-start.12 = (s32[4]{0:T(128)S(1)}, s32[4]{0:T(128)}, u32[]{:S(2)}) copy-start(s32[4]{0:T(128)} %owner_ref.3) | copy-start | bytes 52
  32.5 7.6 %collective-permute-start.6 = (f32[4,32,256]{2,1,0:T(8,128)S(1)}, f32[4,32,256]{2,1,0:T(8,128)S(1)}, u32[]{:S(2)}, u32[]{:S(2)}) collective-permute-start(f32[4,32,256]{2,1,0:T(8,128)S(1)} %get-tuple-element.60), channel_id=1, source_target_pairs={{0,3},{1,0},{2,1},{3,2},{4,7},{5,4},{6,5},{7,6},{8,11},{9,8},{10,9... | collective-permute-start | bytes 393224 | tf_op jit(solution)/shard_map/ppermute | solution.py:534
  36.2 11.4 %collective-permute-start.7 = (f32[4,32,256]{2,1,0:T(8,128)S(1)}, f32[4,32,256]{2,1,0:T(8,128)S(1)}, u32[]{:S(2)}, u32[]{:S(2)}) collective-permute-start(f32[4,32,256]{2,1,0:T(8,128)S(1)} %get-tuple-element.61), channel_id=1, source_target_pairs={{0,2},{1,3},{2,0},{3,1},{4,6},{5,7},{6,4},{7,5},{8,10},{9,11},{10,... | collective-permute-start | bytes 393224 | tf_op jit(solution)/shard_map/ppermute | solution.py:534
  36.2 11.4 %collective-permute-start.8 = (f32[4,32,256]{2,1,0:T(8,128)S(1)}, f32[4,32,256]{2,1,0:T(8,128)S(1)}, u32[]{:S(2)}, u32[]{:S(2)}) collective-permute-start(f32[4,32,256]{2,1,0:T(8,128)S(1)} %get-tuple-element.62), channel_id=1, source_target_pairs={{0,1},{1,2},{2,3},{3,0},{4,5},{5,6},{6,7},{7,4},{8,9},{9,10},{10,1... | collective-permute-start | bytes 393224 | tf_op jit(solution)/shard_map/ppermute | solution.py:534
  40.1 13.5 %collective-permute-start = (f32[2,256,256]{2,1,0:T(8,128)S(1)}, f32[2,256,256]{2,1,0:T(8,128)S(1)}, u32[]{:S(2)}, u32[]{:S(2)}) collective-permute-start(f32[2,256,256]{2,1,0:T(8,128)S(1)} %copy-done.25), channel_id=1, source_target_pairs={{0,4},{4,0},{8,12},{12,8},{1,5},{5,1},{9,13},{13,9},{2,6},{6,2},{1... | collective-permute-start | bytes 1572872 | tf_op jit(solution)/shard_map/ppermute | solution.py:541
  47.5 14.1 %collective-permute-start.2 = (f32[2,256,256]{2,1,0:T(8,128)}, f32[2,256,256]{2,1,0:T(8,128)}, u32[]{:S(2)}, u32[]{:S(2)}) collective-permute-start(f32[2,256,256]{2,1,0:T(8,128)} %get-tuple-element.52), channel_id=1, source_target_pairs={{0,12},{4,8},{8,4},{12,0},{1,13},{5,9},{9,5},{13,1},{2,14},{6,10},... | collective-permute-start | bytes 1572872 | tf_op jit(solution)/shard_map/ppermute | solution.py:541
  47.6 0.8 copy-start.23
  48.4 13.3 %copy-start.24 = (f32[2,256,256]{2,1,0:T(8,128)S(1)}, f32[2,256,256]{2,1,0:T(8,128)}, u32[]{:S(2)}) copy-start(f32[2,256,256]{2,1,0:T(8,128)} %get-tuple-element.67) | copy-start | bytes 1572868
  48.4 20.2 %copy-start.15 = (bf16[4,512,256]{2,1,0:T(8,128)(2,1)S(1)}, bf16[4,512,256]{2,1,0:T(8,128)(2,1)}, u32[]{:S(2)}) copy-start(bf16[4,512,256]{2,1,0:T(8,128)(2,1)} %copy-done.14) | copy-start | bytes 3145732
  48.4 20.2 %copy-start.17 = (bf16[4,512,256]{2,1,0:T(8,128)(2,1)S(1)}, bf16[4,512,256]{2,1,0:T(8,128)(2,1)}, u32[]{:S(2)}) copy-start(bf16[4,512,256]{2,1,0:T(8,128)(2,1)} %copy-done.16) | copy-start | bytes 3145732
  49.0 12.7 %collective-permute-start.10 = (f32[4,32,256]{2,1,0:T(8,128)S(1)}, f32[4,32,256]{2,1,0:T(8,128)S(1)}, u32[]{:S(2)}, u32[]{:S(2)}) collective-permute-start(f32[4,32,256]{2,1,0:T(8,128)S(1)} %choose_slab.1.refs_0_), channel_id=1, source_target_pairs={{1,0},{2,1},{3,2},{0,3},{5,4},{6,5},{7,6},{4,7},{9,8},{10,9},{11,1... | collective-permute-start | bytes 393224 | tf_op jit(solution)/shard_map/ppermute | solution.py:529
  50.6 14.1 %collective-permute-start.11 = (f32[4,32,256]{2,1,0:T(8,128)S(1)}, f32[4,32,256]{2,1,0:T(8,128)S(1)}, u32[]{:S(2)}, u32[]{:S(2)}) collective-permute-start(f32[4,32,256]{2,1,0:T(8,128)S(1)} %choose_slab.1.refs_0_), channel_id=1, source_target_pairs={{2,0},{3,1},{0,2},{1,3},{6,4},{7,5},{4,6},{5,7},{10,8},{11,9},{8,1... | collective-permute-start | bytes 393224 | tf_op jit(solution)/shard_map/ppermute | solution.py:529
  51.7 14.9 %collective-permute-start.12 = (f32[4,32,256]{2,1,0:T(8,128)S(1)}, f32[4,32,256]{2,1,0:T(8,128)S(1)}, u32[]{:S(2)}, u32[]{:S(2)}) collective-permute-start(f32[4,32,256]{2,1,0:T(8,128)S(1)} %choose_slab.1.refs_0_), channel_id=1, source_target_pairs={{3,0},{0,1},{1,2},{2,3},{7,4},{4,5},{5,6},{6,7},{11,8},{8,9},{9,10... | collective-permute-start | bytes 393224 | tf_op jit(solution)/shard_map/ppermute | solution.py:529
  53.6 0.8 copy-start.26
  54.4 12.3 %collective-permute-start.13 = (f32[4,32,256]{2,1,0:T(8,128)S(1)}, f32[4,32,256]{2,1,0:T(8,128)S(1)}, u32[]{:S(2)}, u32[]{:S(2)}) collective-permute-start(f32[4,32,256]{2,1,0:T(8,128)S(1)} %choose_slab.1.refs_0_), channel_id=1, source_target_pairs={{0,16},{16,0},{1,17},{17,1},{2,18},{18,2},{3,19},{19,3},{4,20},{20... | collective-permute-start | bytes 393224 | tf_op jit(solution)/shard_map/ppermute | solution.py:575
  56.0 81.2 %reduce-scatter.2.cloned.1.call-start = ((), (), s32[]{:S(2)}) async-start(), calls=%async_computation.2 | async-start | bytes 1310720 | tf_op jit(solution)/shard_map/reduce_scatter | solution.py:583
  61.7 14.7 %collective-permute-start.17 = (f32[2,256,256]{2,1,0:T(8,128)}, f32[2,256,256]{2,1,0:T(8,128)S(1)}, u32[]{:S(2)}, u32[]{:S(2)}) collective-permute-start(f32[2,256,256]{2,1,0:T(8,128)} %get-tuple-element.66), channel_id=1, source_target_pairs={{0,4},{4,0},{8,12},{12,8},{1,5},{5,1},{9,13},{13,9},{2,6},{6,2},{1... | collective-permute-start | bytes 1572872 | tf_op jit(solution)/shard_map/ppermute | solution.py:541
  61.7 14.7 %collective-permute-start.18 = (f32[2,256,256]{2,1,0:T(8,128)S(1)}, f32[2,256,256]{2,1,0:T(8,128)S(1)}, u32[]{:S(2)}, u32[]{:S(2)}) collective-permute-start(f32[2,256,256]{2,1,0:T(8,128)S(1)} %copy-done.24), channel_id=1, source_target_pairs={{0,12},{4,8},{8,4},{12,0},{1,13},{5,9},{9,5},{13,1},{2,14},{6,10},... | collective-permute-start | bytes 1572872 | tf_op jit(solution)/shard_map/ppermute | solution.py:541
  64.6 7.5 %collective-permute-start.14 = (f32[4,32,256]{2,1,0:T(8,128)S(1)}, f32[4,32,256]{2,1,0:T(8,128)S(1)}, u32[]{:S(2)}, u32[]{:S(2)}) collective-permute-start(f32[4,32,256]{2,1,0:T(8,128)S(1)} %collective-permute-done.10.refs_1_), channel_id=1, source_target_pairs={{0,16},{16,0},{1,17},{17,1},{2,18},{18,2},{3,19},{19,3},{4,20},{20... | collective-permute-start | bytes 393224 | tf_op jit(solution)/shard_map/ppermute | solution.py:575
  66.5 7.3 %collective-permute-start.15 = (f32[4,32,256]{2,1,0:T(8,128)S(1)}, f32[4,32,256]{2,1,0:T(8,128)S(1)}, u32[]{:S(2)}, u32[]{:S(2)}) collective-permute-start(f32[4,32,256]{2,1,0:T(8,128)S(1)} %collective-permute-done.11.refs_2_), channel_id=1, source_target_pairs={{0,16},{16,0},{1,17},{17,1},{2,18},{18,2},{3,19},{19,3},{4,20},{20... | collective-permute-start | bytes 393224 | tf_op jit(solution)/shard_map/ppermute | solution.py:575
  66.7 8.9 %collective-permute-start.16 = (f32[4,32,256]{2,1,0:T(8,128)S(1)}, f32[4,32,256]{2,1,0:T(8,128)S(1)}, u32[]{:S(2)}, u32[]{:S(2)}) collective-permute-start(f32[4,32,256]{2,1,0:T(8,128)S(1)} %collective-permute-done.12.refs_3_), channel_id=1, source_target_pairs={{0,16},{16,0},{1,17},{17,1},{2,18},{18,2},{3,19},{19,3},{4,20},{20... | collective-permute-start | bytes 393224 | tf_op jit(solution)/shard_map/ppermute | solution.py:575
  76.4 0.8 copy-start.27
  76.4 0.9 copy-start.28
  80.9 10.3 %collective-permute-start.19 = (f32[2,256,256]{2,1,0:T(8,128)}, f32[2,256,256]{2,1,0:T(8,128)S(1)}, u32[]{:S(2)}, u32[]{:S(2)}) collective-permute-start(f32[2,256,256]{2,1,0:T(8,128)} %get-tuple-element.69), channel_id=1, source_target_pairs={{0,4},{4,0},{8,12},{12,8},{1,5},{5,1},{9,13},{13,9},{2,6},{6,2},{1... | collective-permute-start | bytes 1572872 | tf_op jit(solution)/shard_map/ppermute | solution.py:541
  80.9 14.9 %collective-permute-start.20 = (f32[2,256,256]{2,1,0:T(8,128)}, f32[2,256,256]{2,1,0:T(8,128)S(1)}, u32[]{:S(2)}, u32[]{:S(2)}) collective-permute-start(f32[2,256,256]{2,1,0:T(8,128)} %get-tuple-element.70), channel_id=1, source_target_pairs={{0,8},{4,12},{8,0},{12,4},{1,9},{5,13},{9,1},{13,5},{2,10},{6,14},... | collective-permute-start | bytes 1572872 | tf_op jit(solution)/shard_map/ppermute | solution.py:541
  81.6 24.9 %collective-permute-start.21 = (f32[2,256,256]{2,1,0:T(8,128)}, f32[2,256,256]{2,1,0:T(8,128)}, u32[]{:S(2)}, u32[]{:S(2)}) collective-permute-start(f32[2,256,256]{2,1,0:T(8,128)} %get-tuple-element.71), channel_id=1, source_target_pairs={{0,12},{4,8},{8,4},{12,0},{1,13},{5,9},{9,5},{13,1},{2,14},{6,10},... | collective-permute-start | bytes 1572872 | tf_op jit(solution)/shard_map/ppermute | solution.py:541
  90.3 43.8 %collective-permute-start.22 = (f32[2,128,256]{2,1,0:T(8,128)}, f32[2,128,256]{2,1,0:T(8,128)}, u32[]{:S(2)}, u32[]{:S(2)}) collective-permute-start(f32[2,128,256]{2,1,0:T(8,128)} %get-tuple-element.75), channel_id=1, source_target_pairs={{0,4},{4,0},{8,12},{12,8},{1,5},{5,1},{9,13},{13,9},{2,6},{6,2},{1... | collective-permute-start | bytes 786440 | tf_op jit(solution)/shard_map/ppermute | solution.py:541
  90.6 45.5 %collective-permute-start.23 = (f32[2,128,256]{2,1,0:T(8,128)}, f32[2,128,256]{2,1,0:T(8,128)}, u32[]{:S(2)}, u32[]{:S(2)}) collective-permute-start(f32[2,128,256]{2,1,0:T(8,128)} %get-tuple-element.76), channel_id=1, source_target_pairs={{0,8},{4,12},{8,0},{12,4},{1,9},{5,13},{9,1},{13,5},{2,10},{6,14},... | collective-permute-start | bytes 786440 | tf_op jit(solution)/shard_map/ppermute | solution.py:541
  91.3 16.9 %copy-start.29 = (f32[2,256,256]{2,1,0:T(8,128)}, f32[2,256,256]{2,1,0:T(8,128)S(1)}, u32[]{:S(2)}) copy-start(f32[2,256,256]{2,1,0:T(8,128)S(1)} %collective-permute-done.19.refs_4_) | copy-start | bytes 1572868
  91.3 24.3 %collective-permute-start.25 = (f32[2,128,256]{2,1,0:T(8,128)}, f32[2,128,256]{2,1,0:T(8,128)}, u32[]{:S(2)}, u32[]{:S(2)}) collective-permute-start(f32[2,128,256]{2,1,0:T(8,128)} %get-tuple-element.79), channel_id=1, source_target_pairs={{0,4},{4,0},{8,12},{12,8},{1,5},{5,1},{9,13},{13,9},{2,6},{6,2},{1... | collective-permute-start | bytes 786440 | tf_op jit(solution)/shard_map/ppermute | solution.py:541
  95.9 12.3 %copy-start.30 = (f32[2,256,256]{2,1,0:T(8,128)}, f32[2,256,256]{2,1,0:T(8,128)S(1)}, u32[]{:S(2)}) copy-start(f32[2,256,256]{2,1,0:T(8,128)S(1)} %collective-permute-done.20.refs_5_) | copy-start | bytes 1572868
  95.9 22.6 %collective-permute-start.26 = (f32[2,128,256]{2,1,0:T(8,128)}, f32[2,128,256]{2,1,0:T(8,128)}, u32[]{:S(2)}, u32[]{:S(2)}) collective-permute-start(f32[2,128,256]{2,1,0:T(8,128)} %get-tuple-element.80), channel_id=1, source_target_pairs={{0,8},{4,12},{8,0},{12,4},{1,9},{5,13},{9,1},{13,5},{2,10},{6,14},... | collective-permute-start | bytes 786440 | tf_op jit(solution)/shard_map/ppermute | solution.py:541
  106.4 16.9 %collective-permute-start.27 = (f32[2,128,256]{2,1,0:T(8,128)}, f32[2,128,256]{2,1,0:T(8,128)}, u32[]{:S(2)}, u32[]{:S(2)}) collective-permute-start(f32[2,128,256]{2,1,0:T(8,128)} %get-tuple-element.81), channel_id=1, source_target_pairs={{0,12},{4,8},{8,4},{12,0},{1,13},{5,9},{9,5},{13,1},{2,14},{6,10},... | collective-permute-start | bytes 786440 | tf_op jit(solution)/shard_map/ppermute | solution.py:541
  108.2 1.2 copy-start.3
  109.4 6.2 %copy-start.31 = (f32[2,128,256]{2,1,0:T(8,128)S(1)}, f32[2,128,256]{2,1,0:T(8,128)}, u32[]{:S(2)}) copy-start(f32[2,128,256]{2,1,0:T(8,128)} %get-tuple-element.77) | copy-start | bytes 786436
  109.4 13.8 %copy-start.18 = (bf16[4,512,256]{2,1,0:T(8,128)(2,1)S(1)}, bf16[4,512,256]{2,1,0:T(8,128)(2,1)}, u32[]{:S(2)}) copy-start(bf16[4,512,256]{2,1,0:T(8,128)(2,1)} %copy-done.16) | copy-start | bytes 3145732
  115.6 23.2 %collective-permute-start.24 = (f32[2,128,256]{2,1,0:T(8,128)S(1)}, f32[2,128,256]{2,1,0:T(8,128)}, u32[]{:S(2)}, u32[]{:S(2)}) collective-permute-start(f32[2,128,256]{2,1,0:T(8,128)S(1)} %copy-done.31), channel_id=1, source_target_pairs={{0,12},{4,8},{8,4},{12,0},{1,13},{5,9},{9,5},{13,1},{2,14},{6,10},... | collective-permute-start | bytes 786440 | tf_op jit(solution)/shard_map/ppermute | solution.py:541
  123.3 15.5 %copy-start.4 = (f32[256,1024]{1,0:T(8,128)S(1)}, f32[256,1024]{1,0:T(8,128)}, u32[]{:S(2)}) copy-start(f32[256,1024]{1,0:T(8,128)} %all-reduce.2.cloned.1.call-done.refs_7_) | copy-start | bytes 3145732
  127.5 21.3 %collective-permute-start.29 = (f32[128,256]{1,0:T(8,128)S(1)}, f32[128,256]{1,0:T(8,128)S(1)}, u32[]{:S(2)}, u32[]{:S(2)}) collective-permute-start(f32[128,256]{1,0:T(8,128)S(1)} %get-tuple-element.86), channel_id=1, source_target_pairs={{0,3},{1,0},{2,1},{3,2},{4,7},{5,4},{6,5},{7,6},{8,11},{9,8},{10,9... | collective-permute-start | bytes 393224 | tf_op jit(solution)/shard_map/ppermute | solution.py:534
  128.1 24.8 %collective-permute-start.30 = (f32[128,256]{1,0:T(8,128)S(1)}, f32[128,256]{1,0:T(8,128)S(1)}, u32[]{:S(2)}, u32[]{:S(2)}) collective-permute-start(f32[128,256]{1,0:T(8,128)S(1)} %get-tuple-element.87), channel_id=1, source_target_pairs={{0,2},{1,3},{2,0},{3,1},{4,6},{5,7},{6,4},{7,5},{8,10},{9,11},{10,... | collective-permute-start | bytes 393224 | tf_op jit(solution)/shard_map/ppermute | solution.py:534
  134.1 18.8 %collective-permute-start.31 = (f32[128,256]{1,0:T(8,128)S(1)}, f32[128,256]{1,0:T(8,128)S(1)}, u32[]{:S(2)}, u32[]{:S(2)}) collective-permute-start(f32[128,256]{1,0:T(8,128)S(1)} %get-tuple-element.88), channel_id=1, source_target_pairs={{0,1},{1,2},{2,3},{3,0},{4,5},{5,6},{6,7},{7,4},{8,9},{9,10},{10,1... | collective-permute-start | bytes 393224 | tf_op jit(solution)/shard_map/ppermute | solution.py:534
  137.2 32.6 %collective-permute-start.28 = (f32[256,256]{1,0:T(8,128)}, f32[256,256]{1,0:T(8,128)S(1)}, u32[]{:S(2)}, u32[]{:S(2)}) collective-permute-start(f32[256,256]{1,0:T(8,128)} %bitcast.4), channel_id=1, source_target_pairs={{0,0},{1,4},{2,8},{3,12},{4,5},{5,1},{6,13},{7,9},{8,10},{9,14},{1... | collective-permute-start | bytes 786440 | tf_op jit(solution)/shard_map/ppermute | solution.py:588
  138.8 1.2 copy-start.19
  144.1 12.9 %collective-permute-start.32 = (f32[128,256]{1,0:T(8,128)S(1)}, f32[128,256]{1,0:T(8,128)S(1)}, u32[]{:S(2)}, u32[]{:S(2)}) collective-permute-start(f32[128,256]{1,0:T(8,128)S(1)} %get-tuple-element.90), channel_id=1, source_target_pairs={{0,3},{1,0},{2,1},{3,2},{4,7},{5,4},{6,5},{7,6},{8,11},{9,8},{10,9... | collective-permute-start | bytes 393224 | tf_op jit(solution)/shard_map/ppermute | solution.py:534
  148.9 20.9 %collective-permute-start.33 = (f32[128,256]{1,0:T(8,128)S(1)}, f32[128,256]{1,0:T(8,128)S(1)}, u32[]{:S(2)}, u32[]{:S(2)}) collective-permute-start(f32[128,256]{1,0:T(8,128)S(1)} %get-tuple-element.91), channel_id=1, source_target_pairs={{0,2},{1,3},{2,0},{3,1},{4,6},{5,7},{6,4},{7,5},{8,10},{9,11},{10,... | collective-permute-start | bytes 393224 | tf_op jit(solution)/shard_map/ppermute | solution.py:534
  152.9 16.8 %collective-permute-start.34 = (f32[128,256]{1,0:T(8,128)S(1)}, f32[128,256]{1,0:T(8,128)S(1)}, u32[]{:S(2)}, u32[]{:S(2)}) collective-permute-start(f32[128,256]{1,0:T(8,128)S(1)} %get-tuple-element.92), channel_id=1, source_target_pairs={{0,1},{1,2},{2,3},{3,0},{4,5},{5,6},{6,7},{7,4},{8,9},{9,10},{10,1... | collective-permute-start | bytes 393224 | tf_op jit(solution)/shard_map/ppermute | solution.py:534
  (5 other events, 3.4 us)
Sparse Core Ops, SparseCore 0:
  56.1 52.0 all-reduce.1
  110.6 26.5 reduce-scatter.1

commit v3 on v2

--- a/solution.py
+++ b/solution.py
@@ -264,7 +264,7 @@
     )(shift, *far(fields), *blocks)
 
 
-def middle_kernel(count, with_image, waits, shift_ref, *refs):
+def middle_kernel(count, with_image, waits, shift_ref, place_ref, *refs):
     if with_image:
         fields, refs = refs[:RADIX], refs[RADIX:]
         other_ref, refs = refs[0], refs[1:]
@@ -280,9 +280,14 @@
     x = [rotate(x[s], cos_ref[s], sin_ref[s]) for s in range(RADIX)]
     for s in range(RADIX):
         if with_image:
-            extra[0][s] = other_ref[s, 0] * x[s][1] + other_ref[s, 1] * x[s][0]
+            extra[2][s] = other_ref[s, 0] * x[s][1] + other_ref[s, 1] * x[s][0]
         else:
             store(extra[0].at[s], x[s], False)
+    if with_image:
+        mine = lax.bitwise_and(place_ref[0], 1)
+        for j in range(RADIX // 2):
+            extra[0][j] = extra[2][mine + 2 * j]
+            extra[1][j] = extra[2][1 - mine + 2 * j]
     x = convolve(x, high_ref, low_ref, True, shift_ref[0])
     part = x[0][0].shape[0] // count
     for s in range(RADIX):
@@ -291,29 +296,30 @@
             store(outs[s * count + c], value, False)
 
 
-def middle_stage(fields, phases, blocks, shift, count, other, after=()):
+def middle_stage(fields, phases, blocks, shift, place, count, other, after=()):
     with_image = other is not None
     _, rows, cols = phases[0].shape
     piece = pltpu.HBM((2, rows // count, cols), F32)
     fields = far(fields) if with_image else fields
-    extra = (RADIX, rows, cols) if with_image else (RADIX, 2, rows, cols)
+    extra = [(RADIX // 2, rows, cols)] * 2 if with_image else [(RADIX, 2, rows, cols)]
     args = list(fields) + ([other] if with_image else []) + list(phases) + list(blocks)
-    outs = [piece] * (RADIX * count) + [jax.ShapeDtypeStruct(extra, F32)]
+    outs = [piece] * (RADIX * count) + [jax.ShapeDtypeStruct(e, F32) for e in extra]
     got = pl.pallas_call(
         lambda *refs: middle_kernel(count, with_image, len(after), *refs),
         grid_spec=pltpu.PrefetchScalarGridSpec(
-            num_scalar_prefetch=1,
+            num_scalar_prefetch=2,
             grid=(1,),
             in_specs=[whole(a.shape) for a in args] + [ANY] * len(after),
             out_specs=[whole(o.shape) for o in outs],
+            scratch_shapes=[pltpu.VMEM((RADIX, rows, cols), F32)] if with_image else [],
         ),
         out_shape=outs,
         compiler_params=params(),
         cost_estimate=LONG,
         name="along_x_r" if with_image else "along_x_s_second",
-    )(shift, *args, *far(after))
+    )(shift, place, *args, *far(after))
     pieces = [[got[s * count + c] for s in range(RADIX)] for c in range(count)]
-    return pieces, got[-1]
+    return pieces, got[RADIX * count :] if with_image else got[-1]
 
 
 def last_kernel(with_image, shift_ref, slot_ref, place_ref, *refs):
@@ -345,7 +351,7 @@
             terms[t][...] = line[:, at]
 
 
-def last_stage(fields, slab, blocks, shift, slot, place, start, rows, other, held):
+def last_stage(fields, slab, blocks, shift, slot, place, start, rows, other, held, after=()):
     _, part, block = fields[0].shape
     width = block * RADIX
     with_image = other is not None
@@ -370,6 +376,8 @@
         alias = {3 + len(args): 0}
         args += far([held])
         specs.append(ANY)
+    args += far(after)
+    specs += [ANY] * len(after)
     got = pl.pallas_call(
         lambda *refs: last_kernel(with_image, *refs),
         grid_spec=pltpu.PrefetchScalarGridSpec(
@@ -397,12 +405,13 @@
             cols = pl.ds(pl.multiple_of(block_of(shift_ref[0], s) * block, block), block)
             outs[s][t] = slab_ref[0, rows, cols]
     kept = (owner_ref[NZ - 1] == place_ref[0]).astype(F32)
-    outs[-1][...] = slab_ref[0] * kept
+    half = outs[-1].shape[0]
+    outs[-1][...] = slab_ref[0, pl.ds(pl.multiple_of(shot_ref[0] * half, half), half), :] * kept
 
 
 def cut_stage(slowness, shift, shot, place, owner):
     _, rows, width = slowness.shape
-    outs = [(RADIX, rows // (2 * RADIX), width // RADIX)] * RADIX + [(rows, width)]
+    outs = [(RADIX, rows // (2 * RADIX), width // RADIX)] * RADIX + [(rows // 2, width)]
     got = pl.pallas_call(
         cut_kernel,
         grid_spec=pltpu.PrefetchScalarGridSpec(
@@ -437,7 +446,7 @@
         compiler_params=params(),
         cost_estimate=LONG,
         name="regroup_slab",
-    )(*pieces, after)
+    )(*far(pieces), after)
 
 
 def choose_kernel(place_ref, owner_ref, *refs):
@@ -499,6 +508,69 @@
     )(slot, place, shot, *pieces, after)
 
 
+def add_kernel(a_ref, b_ref, *refs):
+    refs[-1][...] = a_ref[...] + b_ref[...]
+
+
+def add_stage(a, b, name, after=()):
+    return pl.pallas_call(
+        add_kernel,
+        grid=(1,),
+        in_specs=[whole(a.shape)] * 2 + [ANY] * len(after),
+        out_specs=whole(a.shape),
+        out_shape=jax.ShapeDtypeStruct(a.shape, F32),
+        compiler_params=params(),
+        cost_estimate=BRIEF,
+        name=name,
+    )(a, b, *far(after))
+
+
+def fold_kernel(place_ref, a_ref, b_ref, keep_ref, send_ref):
+    mine = lax.shift_right_logical(place_ref[0], 1)
+    keep_ref[...] = a_ref[mine] + b_ref[mine]
+    send_ref[...] = a_ref[1 - mine] + b_ref[1 - mine]
+
+
+def fold_stage(a, b, place):
+    shape = a.shape[1:]
+    return pl.pallas_call(
+        fold_kernel,
+        grid_spec=pltpu.PrefetchScalarGridSpec(
+            num_scalar_prefetch=1,
+            grid=(1,),
+            in_specs=[whole(a.shape)] * 2,
+            out_specs=[whole(shape)] * 2,
+        ),
+        out_shape=[jax.ShapeDtypeStruct(shape, F32)] * 2,
+        compiler_params=params(),
+        cost_estimate=BRIEF,
+        name="first_image_fold",
+    )(place, a, b)
+
+
+def join_kernel(shot_ref, a_ref, b_ref, out_ref):
+    half = a_ref.shape[0]
+    out_ref[pl.ds(pl.multiple_of(shot_ref[0] * half, half), half), :] = a_ref[...]
+    out_ref[pl.ds(pl.multiple_of((1 - shot_ref[0]) * half, half), half), :] = b_ref[...]
+
+
+def join_stage(a, b, shot):
+    shape = (2 * a.shape[0], a.shape[1])
+    return pl.pallas_call(
+        join_kernel,
+        grid_spec=pltpu.PrefetchScalarGridSpec(
+            num_scalar_prefetch=1,
+            grid=(1,),
+            in_specs=[whole(a.shape)] * 2,
+            out_specs=whole(shape),
+        ),
+        out_shape=jax.ShapeDtypeStruct(shape, F32),
+        compiler_params=params(),
+        cost_estimate=BRIEF,
+        name="late_join",
+    )(shot, a, b)
+
+
 def image_kernel(chunks, early_ref, *refs):
     out_ref = refs[-1]
     count = (len(refs) - 1) // chunks
@@ -533,6 +605,10 @@
     count = len(pieces)
     sent = [lax.ppermute(pieces[s], axis, [(i, (i + s) % count) for i in range(count)]) for s in range(1, count)]
     return [pieces[0]] + [sent[count - s - 1] for s in range(1, count)]
+
+
+def paired(value, axis, bits):
+    return lax.ppermute(value, axis, [(i, i ^ bits) for i in range(lax.axis_size(axis))])
 
 
 def swap_pairs(pieces, axis):
@@ -565,35 +641,39 @@
 
     turned, late = cut_stage(slowness, shift, shot, place, owner)
     turned = swap_pairs(turned, "row")
-    late = lax.psum(late, "freq")
+    late = add_stage(late, paired(late, "freq", 2), "late_first")
     s_first, blocks = first_stage(source_field, shift, slot, None, 2, (turned[0],))
     s_mid = swap_pairs(s_first, "row")
     r_first, _ = first_stage(receiver_field, shift, slot, blocks, 2, turned[1:])
     r_mid = swap_pairs(r_first, "row")
     shares = swap_slots(regroup_stage(turned, r_first[0]), "freq")
-    gathered = gather_slots(choose_stage(shares, place, owner, [s_mid[2], r_mid[2]]), "freq")
+    gathered = gather_slots(choose_stage(shares, place, owner, [s_mid[2], r_mid[2], late]), "freq")
     gathered += [lax.ppermute(g, "shot", [(0, 1), (1, 0)]) for g in gathered]
     s_half = half_stage(s_mid, blocks, shift)
     phases = phase_stage(gathered, slot, place, shot, s_half)
 
-    s_pieces, s_held = middle_stage([s_half], phases, blocks, shift, 1, None, r_mid[1:])
+    s_pieces, s_held = middle_stage([s_half], phases, blocks, shift, place, 1, None, r_mid[1:])
     s_last = swap_pairs(s_pieces[0], "row")
-    r_pieces, term = middle_stage(r_mid, phases, blocks, shift, CHUNKS, s_held)
+    late_total = add_stage(late, paired(late, "freq", 1), "late_second")
+    r_pieces, term = middle_stage(r_mid, phases, blocks, shift, place, CHUNKS, s_held)
     r_last = [swap_pairs(p, "row") for p in r_pieces]
-    total = lax.psum_scatter(term, "freq", scatter_dimension=0, tiled=False)
+    late = join_stage(late_total, paired(late_total, "shot", 1), shot)
+    keep, send = fold_stage(term[0], paired(term[1], "freq", 1), place)
+    total = add_stage(keep, paired(send, "freq", 2), "first_image")
     pairs = []
     for r in range(RADIX):
         for f in range(RADIX):
             pairs.append((r * RADIX + f, (r ^ f) * RADIX + r))
-    first_image = lax.ppermute(total, ("row", "freq"), pairs)
 
     source_out, _ = last_stage(s_last, late, blocks, shift, slot, place, 0, rows, None, None)
     receiver_out, groups = None, []
     for c in range(CHUNKS):
         receiver_out, terms = last_stage(
-            r_last[c], late, blocks, shift, slot, place, c * (rows // CHUNKS), rows, source_out, receiver_out
+            r_last[c], late, blocks, shift, slot, place, c * (rows // CHUNKS), rows, source_out, receiver_out,
+            [total] if c == CHUNKS - 1 else [],
         )
         groups.append(swap_slots(terms, "freq"))
+    first_image = lax.ppermute(total, ("row", "freq"), pairs)
     return (source_out, receiver_out, image_stage(first_image, groups))
 
 
@@ -622,15 +702,15 @@
     theta = omega_of(slot[0]) * (turned - ref_slow) * dz_km
     theta = theta.reshape(RADIX, -1, theta.shape[1])
     phases = (jnp.cos(theta), jnp.sin(theta))
-    s_pieces, s_held = middle_stage([half_stage(s_mid, blocks, shift)], phases, blocks, shift, 1, None)
-    r_pieces, term = middle_stage(r_mid, phases, blocks, shift, 1, s_held)
+    s_pieces, s_held = middle_stage([half_stage(s_mid, blocks, shift)], phases, blocks, shift, shift, 1, None)
+    r_pieces, term = middle_stage(r_mid, phases, blocks, shift, shift, 1, s_held)
     s_last = jnp.split(to_rows(s_pieces[0]), RADIX, axis=2)
     r_last = jnp.split(to_rows(r_pieces[0]), RADIX, axis=2)
     source_out, _ = last_stage(s_last, slabs[1], blocks, shift, slot, shift, 0, rows, None, None)
     receiver_out, terms = last_stage(
         r_last, slabs[1], blocks, shift, slot, shift, 0, rows, source_out, None
     )
-    term = term.reshape(-1, term.shape[2])
+    term = jnp.stack([term[0][0], term[1][0], term[0][1], term[1][1]]).reshape(-1, term[0].shape[2])
     images = [lax.all_to_all(term, "row", split_axis=0, concat_axis=1, tiled=True)]
     images.append(jnp.concatenate(terms, axis=1))
     parts = [lax.psum_scatter(t, "freq", scatter_dimension=1, tiled=True) for t in images]

time: 178 us -> 173 us (0.972)
  between operations: 14.9 us -> 1.64 us
  starting transfers between devices: 44.4 us -> 54 us
  local copies, waits for them, and re-layouts: 14 us -> 7.49 us
  Pallas kernels: 41.1 us -> 45.9 us
    ppermute x0 -> x5, waiting for transfers between devices: none -> 25.1 us  [paired(): lax.ppermute(value, axis, [(i, i ^ bits) for i in range(lax.axis_size(axi...]
    ppermute x9, waiting for transfers between devices: 29.5 us -> 16.9 us  [swap_slots(): lax.ppermute(pieces[s], axis, [(i, (i + s) % count) for i in range(count)])]
    ppermute x18, waiting for transfers between devices: 26.5 us -> 15.9 us  [swap_pairs(): lax.ppermute(pieces[s], axis, [(i, i ^ s) for i in range(count)])]
    ppermute x0 -> x5, starting transfers between devices: none -> 6.77 us  [paired(): lax.ppermute(value, axis, [(i, i ^ bits) for i in range(lax.axis_size(axi...]
    unnamed x64 -> x76, local copies, waits for them, and re-layouts: 14 us -> 7.49 us
    ppermute x9, starting transfers between devices: 19.7 us -> 23.7 us  [swap_slots(): lax.ppermute(pieces[s], axis, [(i, (i + s) % count) for i in range(count)])]
    pallas_call x0 -> x5, Pallas kernels: none -> 3.52 us  [the longest x3 3.4 us: add_stage(): pl.pallas_call(add_kernel, grid=(1,), in_specs=[whole(a.shape)] * 2 + [AN...]
    ppermute x18, starting transfers between devices: 12.8 us -> 14.8 us  [swap_pairs(): lax.ppermute(pieces[s], axis, [(i, i ^ s) for i in range(count)])]
  transfers between devices with their start and end apart: 37 -> 40, of which waited for: 15 -> 14; matrix products, arithmetic and copies ran while one was open for 0% -> 0% of each run, Pallas kernels for 22% -> 25%
where the time goes in v3:
time: 173 us
  waiting for transfers between devices  64 us (37%)
  starting transfers between devices  54 us (31%)
  Pallas kernels  45.9 us (27%)
  local copies, waits for them, and re-layouts  7.49 us (4%)
    ppermute x5, waiting for transfers between devices, paired(): lax.ppermute(value, axis, [(i, i ^ bits) for i in range(lax.axis_size(axi...  25.1 us
    ppermute x9, starting transfers between devices, swap_slots(): lax.ppermute(pieces[s], axis, [(i, (i + s) % count) for i in range(count)])  23.7 us
    ppermute x9, waiting for transfers between devices, swap_slots(): lax.ppermute(pieces[s], axis, [(i, (i + s) % count) for i in range(count)])  16.9 us
    ppermute x18, waiting for transfers between devices, swap_pairs(): lax.ppermute(pieces[s], axis, [(i, i ^ s) for i in range(count)])  15.9 us
    ppermute x18, starting transfers between devices, swap_pairs(): lax.ppermute(pieces[s], axis, [(i, i ^ s) for i in range(count)])  14.8 us
    pallas_call x3, Pallas kernels, last_stage(): pl.pallas_call(lambda *refs: last_kernel(with_image, *refs), grid_spec=pl...  14.6 us
    pallas_call x2, Pallas kernels, middle_stage(): pl.pallas_call(lambda *refs: middle_kernel(count, with_image, len(after),...  11.3 us
    pallas_call x2, Pallas kernels, first_stage(): pl.pallas_call(lambda *refs: first_kernel(form, len(after), *refs), grid_...  7.96 us
  transfers between devices with their start and end apart: 40, of which 14 were waited for; matrix products, arithmetic and copies ran while one was open for 0% of the time, Pallas kernels for 25%

profile of v3, /device:TPU:0, one launch (start us, length us, event | category | flops | bytes accessed | tf_op | source)
XLA Modules:
  0.0 173.0 jit_solution(16240429579429765816)
XLA Ops:
  0.6 1.2 copy-done.3
  1.9 0.7 copy-done.4
  2.5 1.4 cut_slab.1
  3.9 0.7 copy-done.12
  5.0 2.5 %collective-permute-start.4 = (f32[4,32,256]{2,1,0:T(8,128)S(1)}, f32[4,32,256]{2,1,0:T(8,128)S(1)}, u32[]{:S(2)}, u32[]{:S(2)}) collective-permute-start(f32[4,32,256]{2,1,0:T(8,128)S(1)} %get-tuple-element.59), channel_id=1, source_target_pairs={{0,8},{4,12},{8,0},{12,4},{1,9},{5,13},{9,1},{13,5},{2,10},{6,14},... | collective-permute-start | bytes 393224 | tf_op jit(solution)/shard_map/ppermute | solution.py:617
  7.7 2.8 %collective-permute-start.10 = (f32[128,1024]{1,0:T(8,128)}, f32[128,1024]{1,0:T(8,128)}, u32[]{:S(2)}, u32[]{:S(2)}) collective-permute-start(f32[128,1024]{1,0:T(8,128)} %get-tuple-element.67.a_ref), channel_id=1, source_target_pairs={{0,2},{1,3},{2,0},{3,1},{4,6},{5,7},{6,4},{7,5},{8,10},{9,11},{10,... | collective-permute-start | bytes 1572872 | tf_op jit(solution)/shard_map/ppermute | solution.py:611
  11.2 4.6 %along_y_first_s.1 = (f32[2,256,256]{2,1,0:T(8,128)}, f32[2,256,256]{2,1,0:T(8,128)}, f32[2,256,256]{2,1,0:T(8,128)}, f32[2,256,256]{2,1,0:T(8,128)}, bf16[4,512...) custom-call(s32[1]{0:T(128)} %bitcast.shift_ref.refs_0_, s32[1]{0:T(128)S(6)} %copy.11.refs_1_.slot_ref, ...), custom_call_target="tpu_custom_call" | custom-call | flops 99999997952 | bytes 10000000 | tf_op jit(solution)/shard_map/along_y_first_s/pallas_call | solution.py:225
  15.7 1.5 collective-permute-start.1
  17.3 0.6 copy-done.35
  18.0 3.4 %along_y_first_r.1 = (f32[2,256,256]{2,1,0:T(8,128)}, f32[2,256,256]{2,1,0:T(8,128)}, f32[2,256,256]{2,1,0:T(8,128)}, f32[2,256,256]{2,1,0:T(8,128)}) custom-call(s32[1]{0:T(128)} %bitcast.shift_ref.refs_0_, s32[1]{0:T(128)S(6)} %copy.11.refs_1_.slot_ref, f32[2,1,256,1024]{3,2,1,0:T(8,128)S(1)} %copy-done.2, f32[2,1,256,1024]{3,2,1,0:T(8,128)S(1)} %copy-done.2, ...), custom_call_target="tpu_custom_call" | custom-call | flops 99999997952 | bytes 10000000 | tf_op jit(solution)/shard_map/along_y_first_r/pallas_call | solution.py:225
  21.4 0.7 collective-permute-start.9
  22.1 1.0 copy-done.11
  23.1 1.2 regroup_slab.1
  24.4 1.5 collective-permute-start.6
  25.9 1.6 collective-permute-start.7
  27.5 10.2 %collective-permute-done.10.b_ref = f32[128,1024]{1,0:T(8,128)} collective-permute-done((f32[128,1024]{1,0:T(8,128)}, f32[128,1024]{1,0:T(8,128)}, u32[]{:S(2)}, u32[]{:S(2)}) %collective-permute-start.10) | collective-permute-done | bytes 524320 | tf_op jit(solution)/shard_map/ppermute | solution.py:611
  37.7 3.1 %collective-permute-start.8 = (f32[4,32,256]{2,1,0:T(8,128)S(1)}, f32[4,32,256]{2,1,0:T(8,128)S(1)}, u32[]{:S(2)}, u32[]{:S(2)}) collective-permute-start(f32[4,32,256]{2,1,0:T(8,128)S(1)} %get-tuple-element.65), channel_id=1, source_target_pairs={{0,1},{1,2},{2,3},{3,0},{4,5},{5,6},{6,7},{7,4},{8,9},{9,10},{10,1... | collective-permute-start | bytes 393224 | tf_op jit(solution)/shard_map/ppermute | solution.py:606
  40.8 2.1 %late_first.1.refs_6_.a_ref = f32[128,1024]{1,0:T(8,128)} custom-call(f32[128,1024]{1,0:T(8,128)} %get-tuple-element.67.a_ref, f32[128,1024]{1,0:T(8,128)} %collective-permute-done.10.b_ref), custom_call_target="tpu_custom_call" | custom-call | flops 1000 | bytes 1000 | tf_op jit(solution)/shard_map/late_first/pallas_call | solution.py:516
  42.9 1.6 collective-permute-start.2
  44.5 2.8 %collective-permute-done.8.refs_3_ = f32[4,32,256]{2,1,0:T(8,128)S(1)} collective-permute-done((f32[4,32,256]{2,1,0:T(8,128)S(1)}, f32[4,32,256]{2,1,0:T(8,128)S(1)}, u32[]{:S(2)}, u32[]{:S(2)}) %collective-permute-start.8) | collective-permute-done | bytes 131104 | tf_op jit(solution)/shard_map/ppermute | solution.py:606
  47.3 0.8 copy-done.13
  48.1 0.6 choose_slab.1.refs_0_
  48.7 1.9 %collective-permute-start.11 = (f32[4,32,256]{2,1,0:T(8,128)S(1)}, f32[4,32,256]{2,1,0:T(8,128)S(1)}, u32[]{:S(2)}, u32[]{:S(2)}) collective-permute-start(f32[4,32,256]{2,1,0:T(8,128)S(1)} %choose_slab.1.refs_0_), channel_id=1, source_target_pairs={{1,0},{2,1},{3,2},{0,3},{5,4},{6,5},{7,6},{4,7},{9,8},{10,9},{11,1... | collective-permute-start | bytes 393224 | tf_op jit(solution)/shard_map/ppermute | solution.py:601
  50.5 1.1 collective-permute-start.13
  51.7 1.5 collective-permute-start.14
  53.2 3.5 %collective-permute-done.2.refs_3_ = f32[2,256,256]{2,1,0:T(8,128)S(1)} collective-permute-done((f32[2,256,256]{2,1,0:T(8,128)S(1)}, f32[2,256,256]{2,1,0:T(8,128)S(1)}, u32[]{:S(2)}, u32[]{:S(2)}) %collective-permute-start.2) | collective-permute-done | bytes 524320 | tf_op jit(solution)/shard_map/ppermute | solution.py:617
  56.6 0.7 collective-permute-start.18
  57.3 1.2 collective-permute-start.19
  58.5 3.3 %collective-permute-done.12.refs_2_ = f32[4,32,256]{2,1,0:T(8,128)S(1)} collective-permute-done((f32[4,32,256]{2,1,0:T(8,128)S(1)}, f32[4,32,256]{2,1,0:T(8,128)S(1)}, u32[]{:S(2)}, u32[]{:S(2)}) %collective-permute-start.12) | collective-permute-done | bytes 131104 | tf_op jit(solution)/shard_map/ppermute | solution.py:601
  61.8 1.5 collective-permute-start.15
  63.3 0.5 collective-permute-start.16
  63.8 1.5 collective-permute-start.17
  65.3 3.7 %along_x_s_first.1.refs_8_.refs_2_ = f32[4,2,256,256]{3,2,1,0:T(8,128)S(1)} custom-call(s32[1]{0:T(128)} %bitcast.shift_ref.refs_0_, f32[2,256,256]{2,1,0:T(8,128)} %get-tuple-element.52.refs_0_, f32[2,256,256]{2,1,0:T(8,128)} %copy-done.19, f32[2,256,256]{2,1,0:T(8,128)} %collective-permute-done.1.refs_2_.refs_4_, f32[2,256,256]{2,1,0:T(8,128)} %copy-done.22, ...), custom_call_target="tpu_custom_call" | custom-call | flops 99999997952 | bytes 10000000 | tf_op jit(solution)/shard_map/along_x_s_first/pallas_call | solution.py:252
  69.1 1.4 collective-permute-done.16.refs_6_
  70.5 1.4 collective-permute-done.17.refs_7_
  71.9 0.8 phases.1
  72.7 0.8 copy-done.18
  73.7 3.7 %along_x_s_second.1 = (f32[2,256,256]{2,1,0:T(8,128)}, f32[2,256,256]{2,1,0:T(8,128)}, f32[2,256,256]{2,1,0:T(8,128)}, f32[2,256,256]{2,1,0:T(8,128)}, f32[4,2,256,256]{3,2,1,0:T(8,128)S(1)}) custom-call(s32[1]{0:T(128)} %bitcast.shift_ref.refs_0_, s32[1]{0:T(128)} %bitcast.1.place_ref.refs_1_.refs_2_, ...), custom_call_target="tpu_custom_call" | custom-call | flops 99999997952 | bytes 10000000 | tf_op jit(solution)/shard_map/along_x_s_second/pallas_call | solution.py:307
  77.3 7.6 %along_x_r.1 = (f32[2,128,256]{2,1,0:T(8,128)}, f32[2,128,256]{2,1,0:T(8,128)}, f32[2,128,256]{2,1,0:T(8,128)}, f32[2,128,256]{2,1,0:T(8,128)}, f32[2,128,256]{2...) custom-call(s32[1]{0:T(128)} %bitcast.shift_ref.refs_0_, ...), custom_call_target="tpu_custom_call" | custom-call | flops 99999997952 | bytes 10000000 | tf_op jit(solution)/shard_map/along_x_r/pallas_call | solution.py:307
  85.0 1.3 late_second.1.a_ref
  86.3 1.6 collective-permute-start.24
  87.9 1.6 collective-permute-start.21
  89.8 7.8 %collective-permute-done.31.b_ref = f32[2,256,256]{2,1,0:T(8,128)S(1)} collective-permute-done((f32[2,256,256]{2,1,0:T(8,128)S(1)}, f32[2,256,256]{2,1,0:T(8,128)S(1)}, u32[]{:S(2)}, u32[]{:S(2)}) %collective-permute-start.31) | collective-permute-done | bytes 524320 | tf_op jit(solution)/shard_map/ppermute | solution.py:611
  97.7 1.3 collective-permute-done.24.b_ref
  99.0 1.5 collective-permute-start.29
  100.7 2.0 %collective-permute-done.21.refs_5_ = f32[2,256,256]{2,1,0:T(8,128)S(1)} collective-permute-done((f32[2,256,256]{2,1,0:T(8,128)S(1)}, f32[2,256,256]{2,1,0:T(8,128)S(1)}, u32[]{:S(2)}, u32[]{:S(2)}) %collective-permute-start.21) | collective-permute-done | bytes 524320 | tf_op jit(solution)/shard_map/ppermute | solution.py:617
  102.7 10.3 %collective-permute-done.22.refs_6_ = f32[2,256,256]{2,1,0:T(8,128)S(1)} collective-permute-done((f32[2,256,256]{2,1,0:T(8,128)S(1)}, f32[2,256,256]{2,1,0:T(8,128)S(1)}, u32[]{:S(2)}, u32[]{:S(2)}) %collective-permute-start.22) | collective-permute-done | bytes 524320 | tf_op jit(solution)/shard_map/ppermute | solution.py:617
  113.0 1.5 collective-permute-start.26
  114.5 6.2 %along_y_last_s.1.refs_10_ = f32[2,1,256,1024]{3,2,1,0:T(8,128)} custom-call(s32[1]{0:T(128)} %bitcast.shift_ref.refs_0_, s32[1]{0:T(128)S(6)} %copy.11.refs_1_.slot_ref, s32[1]{0:T(128)} %bitcast.1.place_ref.refs_1_.refs_2_, f32[2,256,256]{2,1,0:T(8,128)} %get-tuple-element.72.refs_3_, f32[2,256,256]{2,1,0:T(8,128)} %copy-done.25, ...), custom_call_target="tpu_custom_call" | custom-call | flops 99999997952 | bytes 10000000 | tf_op jit(solution)/shard_map/along_y_last_s/pallas_call | solution.py:381
  120.7 1.2 collective-permute-start.27
  121.9 2.2 %collective-permute-start.32 = (f32[256,256]{1,0:T(8,128)S(1)}, f32[256,256]{1,0:T(8,128)S(1)}, u32[]{:S(2)}, u32[]{:S(2)}) collective-permute-start(f32[256,256]{1,0:T(8,128)S(1)} %get-tuple-element.89), channel_id=1, source_target_pairs={{0,2},{1,3},{2,0},{3,1},{4,6},{5,7},{6,4},{7,5},{8,10},{9,11},{10,... | collective-permute-start | bytes 786440 | tf_op jit(solution)/shard_map/ppermute | solution.py:611
  124.3 0.7 copy-done.34
  125.0 4.2 %along_y_last_r.2 = (f32[2,1,256,1024]{3,2,1,0:T(8,128)}, f32[128,256]{1,0:T(8,128)S(1)}, f32[128,256]{1,0:T(8,128)S(1)}, f32[128,256]{1,0:T(8,128)S(1)}, f32[128,256]{1,0:T(8,128)S(1)}) custom-call(s32[1]{0:T(128)} %bitcast.shift_ref.refs_0_, s32[1]{0:T(128)S(6)} %copy.11.refs_1_.slot_ref, s32[1]{0:T(128)} %bitcast.1.place_ref.refs_1_.refs_2_, ...), custom_call_target="tpu_custom_call" | custom-call | flops 99999997952 | bytes 10000000 | tf_op jit(solution)/shard_map/along_y_last_r/pallas_call | solution.py:381
  129.2 2.9 %collective-permute-start.34 = (f32[128,256]{1,0:T(8,128)S(1)}, f32[128,256]{1,0:T(8,128)S(1)}, u32[]{:S(2)}, u32[]{:S(2)}) collective-permute-start(f32[128,256]{1,0:T(8,128)S(1)} %get-tuple-element.92), channel_id=1, source_target_pairs={{0,3},{1,0},{2,1},{3,2},{4,7},{5,4},{6,5},{7,6},{8,11},{9,8},{10,9... | collective-permute-start | bytes 393224 | tf_op jit(solution)/shard_map/ppermute | solution.py:606
  132.0 5.7 %collective-permute-done.32.b_ref = f32[256,256]{1,0:T(8,128)S(1)} collective-permute-done((f32[256,256]{1,0:T(8,128)S(1)}, f32[256,256]{1,0:T(8,128)S(1)}, u32[]{:S(2)}, u32[]{:S(2)}) %collective-permute-start.32) | collective-permute-done | bytes 262176 | tf_op jit(solution)/shard_map/ppermute | solution.py:611
  137.7 7.8 %collective-permute-start.36 = (f32[128,256]{1,0:T(8,128)S(1)}, f32[128,256]{1,0:T(8,128)S(1)}, u32[]{:S(2)}, u32[]{:S(2)}) collective-permute-start(f32[128,256]{1,0:T(8,128)S(1)} %get-tuple-element.94), channel_id=1, source_target_pairs={{0,1},{1,2},{2,3},{3,0},{4,5},{5,6},{6,7},{7,4},{8,9},{9,10},{10,1... | collective-permute-start | bytes 393224 | tf_op jit(solution)/shard_map/ppermute | solution.py:606
  145.6 0.7 collective-permute-start.33
  146.3 0.7 copy-done.31
  146.9 4.2 %along_y_last_r.3 = (f32[2,1,256,1024]{3,2,1,0:T(8,128)}, f32[128,256]{1,0:T(8,128)S(1)}, f32[128,256]{1,0:T(8,128)S(1)}, f32[128,256]{1,0:T(8,128)S(1)}, f32[128,256]{1,0:T(8,128)S(1)}) custom-call(s32[1]{0:T(128)} %bitcast.shift_ref.refs_0_, s32[1]{0:T(128)S(6)} %copy.11.refs_1_.slot_ref, ...), custom_call_target="tpu_custom_call", output_to_operand_aliasing={{0}: (11, {})} | custom-call | flops 99999997952 | bytes 10000000 | tf_op jit(solution)/shard_map/along_y_last_r/pallas_call | solution.py:381
  151.2 4.5 %collective-permute-start.37 = (f32[128,256]{1,0:T(8,128)S(1)}, f32[128,256]{1,0:T(8,128)S(1)}, u32[]{:S(2)}, u32[]{:S(2)}) collective-permute-start(f32[128,256]{1,0:T(8,128)S(1)} %get-tuple-element.96), channel_id=1, source_target_pairs={{0,3},{1,0},{2,1},{3,2},{4,7},{5,4},{6,5},{7,6},{8,11},{9,8},{10,9... | collective-permute-start | bytes 393224 | tf_op jit(solution)/shard_map/ppermute | solution.py:606
  156.1 2.0 %collective-permute-start.39 = (f32[128,256]{1,0:T(8,128)S(1)}, f32[128,256]{1,0:T(8,128)S(1)}, u32[]{:S(2)}, u32[]{:S(2)}) collective-permute-start(f32[128,256]{1,0:T(8,128)S(1)} %get-tuple-element.98), channel_id=1, source_target_pairs={{0,1},{1,2},{2,3},{3,0},{4,5},{5,6},{6,7},{7,4},{8,9},{9,10},{10,1... | collective-permute-start | bytes 393224 | tf_op jit(solution)/shard_map/ppermute | solution.py:606
  158.0 1.6 collective-permute-done.37.refs_6_
  159.6 12.5 %collective-permute-done.38.refs_7_ = f32[128,256]{1,0:T(8,128)S(1)} collective-permute-done((f32[128,256]{1,0:T(8,128)S(1)}, f32[128,256]{1,0:T(8,128)S(1)}, u32[]{:S(2)}, u32[]{:S(2)}) %collective-permute-start.38) | collective-permute-done | bytes 131104 | tf_op jit(solution)/shard_map/ppermute | solution.py:606
  172.2 0.9 image_sum.1
  (110 shorter events, 2.2 us)
Async XLA Ops:
  2.5 8.6 %copy-start.1 = (f32[2,1,256,1024]{3,2,1,0:T(8,128)S(1)}, f32[2,1,256,1024]{3,2,1,0:T(8,128)}, u32[]{:S(2)}) copy-start(f32[2,1,256,1024]{3,2,1,0:T(8,128)} %refs_5_.2) | copy-start | bytes 6291460
  2.5 8.6 %copy-start.6 = (f32[512,1024]{1,0:T(8,128)S(1)}, f32[512,1024]{1,0:T(8,128)}, u32[]{:S(2)}) copy-start(f32[512,1024]{1,0:T(8,128)} %constant.15.clone.refs_7_) | copy-start | bytes 6291460
  4.6 12.6 %collective-permute-start.3 = (f32[4,32,256]{2,1,0:T(8,128)S(1)}, f32[4,32,256]{2,1,0:T(8,128)S(1)}, u32[]{:S(2)}, u32[]{:S(2)}) collective-permute-start(f32[4,32,256]{2,1,0:T(8,128)S(1)} %get-tuple-element.58), channel_id=1, source_target_pairs={{0,4},{4,0},{8,12},{12,8},{1,5},{5,1},{9,13},{13,9},{2,6},{6,2},{1... | collective-permute-start | bytes 393224 | tf_op jit(solution)/shard_map/ppermute | solution.py:617
  5.0 12.2 %collective-permute-start.4 = (f32[4,32,256]{2,1,0:T(8,128)S(1)}, f32[4,32,256]{2,1,0:T(8,128)S(1)}, u32[]{:S(2)}, u32[]{:S(2)}) collective-permute-start(f32[4,32,256]{2,1,0:T(8,128)S(1)} %get-tuple-element.59), channel_id=1, source_target_pairs={{0,8},{4,12},{8,0},{12,4},{1,9},{5,13},{9,1},{13,5},{2,10},{6,14},... | collective-permute-start | bytes 393224 | tf_op jit(solution)/shard_map/ppermute | solution.py:617
  7.5 9.7 %collective-permute-start.5 = (f32[4,32,256]{2,1,0:T(8,128)S(1)}, f32[4,32,256]{2,1,0:T(8,128)S(1)}, u32[]{:S(2)}, u32[]{:S(2)}) collective-permute-start(f32[4,32,256]{2,1,0:T(8,128)S(1)} %get-tuple-element.60), channel_id=1, source_target_pairs={{0,12},{4,8},{8,4},{12,0},{1,13},{5,9},{9,5},{13,1},{2,14},{6,10},... | collective-permute-start | bytes 393224 | tf_op jit(solution)/shard_map/ppermute | solution.py:617
  7.7 30.0 %collective-permute-start.10 = (f32[128,1024]{1,0:T(8,128)}, f32[128,1024]{1,0:T(8,128)}, u32[]{:S(2)}, u32[]{:S(2)}) collective-permute-start(f32[128,1024]{1,0:T(8,128)} %get-tuple-element.67.a_ref), channel_id=1, source_target_pairs={{0,2},{1,3},{2,0},{3,1},{4,6},{5,7},{6,4},{7,5},{8,10},{9,11},{10,... | collective-permute-start | bytes 1572872 | tf_op jit(solution)/shard_map/ppermute | solution.py:611
  11.2 6.8 %copy-start.2 = (f32[2,1,256,1024]{3,2,1,0:T(8,128)S(1)}, f32[2,1,256,1024]{3,2,1,0:T(8,128)}, u32[]{:S(2)}) copy-start(f32[2,1,256,1024]{3,2,1,0:T(8,128)} %refs_5_.3) | copy-start | bytes 6291460
  15.7 5.7 %copy-start.7 = (bf16[4,512,256]{2,1,0:T(8,128)(2,1)}, bf16[4,512,256]{2,1,0:T(8,128)(2,1)S(1)}, u32[]{:S(2)}) copy-start(bf16[4,512,256]{2,1,0:T(8,128)(2,1)S(1)} %get-tuple-element.56.refs_4_.refs_9_.refs_5_.refs_8_) | copy-start | bytes 3145732
  15.7 5.7 %copy-start.9 = (bf16[4,512,256]{2,1,0:T(8,128)(2,1)}, bf16[4,512,256]{2,1,0:T(8,128)(2,1)S(1)}, u32[]{:S(2)}) copy-start(bf16[4,512,256]{2,1,0:T(8,128)(2,1)S(1)} %get-tuple-element.57.refs_5_.refs_10_.refs_6_.refs_9_) | copy-start | bytes 3145732
  15.7 31.5 %collective-permute-start.1 = (f32[2,256,256]{2,1,0:T(8,128)}, f32[2,256,256]{2,1,0:T(8,128)}, u32[]{:S(2)}, u32[]{:S(2)}) collective-permute-start(f32[2,256,256]{2,1,0:T(8,128)} %get-tuple-element.54), channel_id=1, source_target_pairs={{0,8},{4,12},{8,0},{12,4},{1,9},{5,13},{9,1},{13,5},{2,10},{6,14},... | collective-permute-start | bytes 1572872 | tf_op jit(solution)/shard_map/ppermute | solution.py:617
  21.4 25.9 %collective-permute-start.9 = (f32[2,256,256]{2,1,0:T(8,128)}, f32[2,256,256]{2,1,0:T(8,128)S(1)}, u32[]{:S(2)}, u32[]{:S(2)}) collective-permute-start(f32[2,256,256]{2,1,0:T(8,128)} %get-tuple-element.66), channel_id=1, source_target_pairs={{0,8},{4,12},{8,0},{12,4},{1,9},{5,13},{9,1},{13,5},{2,10},{6,14},... | collective-permute-start | bytes 1572872 | tf_op jit(solution)/shard_map/ppermute | solution.py:617
  23.1 19.7 %copy-start.17 = (f32[2,256,256]{2,1,0:T(8,128)S(1)}, f32[2,256,256]{2,1,0:T(8,128)}, u32[]{:S(2)}) copy-start(f32[2,256,256]{2,1,0:T(8,128)} %get-tuple-element.53) | copy-start | bytes 1572868
  23.1 19.8 %copy-start.16 = (f32[2,256,256]{2,1,0:T(8,128)S(1)}, f32[2,256,256]{2,1,0:T(8,128)}, u32[]{:S(2)}) copy-start(f32[2,256,256]{2,1,0:T(8,128)} %get-tuple-element.55) | copy-start | bytes 1572868
  23.1 24.9 %copy-start.5 = (s32[4]{0:T(128)S(1)}, s32[4]{0:T(128)}, u32[]{:S(2)}) copy-start(s32[4]{0:T(128)} %owner_ref.3) | copy-start | bytes 52
  24.4 18.5 %collective-permute-start.6 = (f32[4,32,256]{2,1,0:T(8,128)S(1)}, f32[4,32,256]{2,1,0:T(8,128)S(1)}, u32[]{:S(2)}, u32[]{:S(2)}) collective-permute-start(f32[4,32,256]{2,1,0:T(8,128)S(1)} %get-tuple-element.63), channel_id=1, source_target_pairs={{0,3},{1,0},{2,1},{3,2},{4,7},{5,4},{6,5},{7,6},{8,11},{9,8},{10,9... | collective-permute-start | bytes 393224 | tf_op jit(solution)/shard_map/ppermute | solution.py:606
  25.9 17.0 %collective-permute-start.7 = (f32[4,32,256]{2,1,0:T(8,128)S(1)}, f32[4,32,256]{2,1,0:T(8,128)S(1)}, u32[]{:S(2)}, u32[]{:S(2)}) collective-permute-start(f32[4,32,256]{2,1,0:T(8,128)S(1)} %get-tuple-element.64), channel_id=1, source_target_pairs={{0,2},{1,3},{2,0},{3,1},{4,6},{5,7},{6,4},{7,5},{8,10},{9,11},{10,... | collective-permute-start | bytes 393224 | tf_op jit(solution)/shard_map/ppermute | solution.py:606
  37.7 9.6 %collective-permute-start.8 = (f32[4,32,256]{2,1,0:T(8,128)S(1)}, f32[4,32,256]{2,1,0:T(8,128)S(1)}, u32[]{:S(2)}, u32[]{:S(2)}) collective-permute-start(f32[4,32,256]{2,1,0:T(8,128)S(1)} %get-tuple-element.65), channel_id=1, source_target_pairs={{0,1},{1,2},{2,3},{3,0},{4,5},{5,6},{6,7},{7,4},{8,9},{9,10},{10,1... | collective-permute-start | bytes 393224 | tf_op jit(solution)/shard_map/ppermute | solution.py:606
  42.9 8.8 %collective-permute-start = (f32[2,256,256]{2,1,0:T(8,128)S(1)}, f32[2,256,256]{2,1,0:T(8,128)S(1)}, u32[]{:S(2)}, u32[]{:S(2)}) collective-permute-start(f32[2,256,256]{2,1,0:T(8,128)S(1)} %copy-done.17), channel_id=1, source_target_pairs={{0,4},{4,0},{8,12},{12,8},{1,5},{5,1},{9,13},{13,9},{2,6},{6,2},{1... | collective-permute-start | bytes 1572872 | tf_op jit(solution)/shard_map/ppermute | solution.py:617
  42.9 13.7 %collective-permute-start.2 = (f32[2,256,256]{2,1,0:T(8,128)S(1)}, f32[2,256,256]{2,1,0:T(8,128)S(1)}, u32[]{:S(2)}, u32[]{:S(2)}) collective-permute-start(f32[2,256,256]{2,1,0:T(8,128)S(1)} %copy-done.16), channel_id=1, source_target_pairs={{0,12},{4,8},{8,4},{12,0},{1,13},{5,9},{9,5},{13,1},{2,14},{6,10},... | collective-permute-start | bytes 1572872 | tf_op jit(solution)/shard_map/ppermute | solution.py:617
  48.1 8.6 %copy-start.15 = (f32[2,256,256]{2,1,0:T(8,128)S(1)}, f32[2,256,256]{2,1,0:T(8,128)}, u32[]{:S(2)}) copy-start(f32[2,256,256]{2,1,0:T(8,128)} %get-tuple-element.70) | copy-start | bytes 1572868
  48.1 9.3 %copy-start.14 = (f32[2,256,256]{2,1,0:T(8,128)S(1)}, f32[2,256,256]{2,1,0:T(8,128)}, u32[]{:S(2)}) copy-start(f32[2,256,256]{2,1,0:T(8,128)} %get-tuple-element.71) | copy-start | bytes 1572868
  48.1 17.3 %copy-start.8 = (bf16[4,512,256]{2,1,0:T(8,128)(2,1)S(1)}, bf16[4,512,256]{2,1,0:T(8,128)(2,1)}, u32[]{:S(2)}) copy-start(bf16[4,512,256]{2,1,0:T(8,128)(2,1)} %copy-done.7) | copy-start | bytes 3145732
  48.1 17.3 %copy-start.10 = (bf16[4,512,256]{2,1,0:T(8,128)(2,1)S(1)}, bf16[4,512,256]{2,1,0:T(8,128)(2,1)}, u32[]{:S(2)}) copy-start(bf16[4,512,256]{2,1,0:T(8,128)(2,1)} %copy-done.9) | copy-start | bytes 3145732
  48.7 8.7 %collective-permute-start.11 = (f32[4,32,256]{2,1,0:T(8,128)S(1)}, f32[4,32,256]{2,1,0:T(8,128)S(1)}, u32[]{:S(2)}, u32[]{:S(2)}) collective-permute-start(f32[4,32,256]{2,1,0:T(8,128)S(1)} %choose_slab.1.refs_0_), channel_id=1, source_target_pairs={{1,0},{2,1},{3,2},{0,3},{5,4},{6,5},{7,6},{4,7},{9,8},{10,9},{11,1... | collective-permute-start | bytes 393224 | tf_op jit(solution)/shard_map/ppermute | solution.py:601
  50.5 11.2 %collective-permute-start.12 = (f32[4,32,256]{2,1,0:T(8,128)S(1)}, f32[4,32,256]{2,1,0:T(8,128)S(1)}, u32[]{:S(2)}, u32[]{:S(2)}) collective-permute-start(f32[4,32,256]{2,1,0:T(8,128)S(1)} %choose_slab.1.refs_0_), channel_id=1, source_target_pairs={{2,0},{3,1},{0,2},{1,3},{6,4},{7,5},{4,6},{5,7},{10,8},{11,9},{8,1... | collective-permute-start | bytes 393224 | tf_op jit(solution)/shard_map/ppermute | solution.py:601
  50.5 12.8 %collective-permute-start.13 = (f32[4,32,256]{2,1,0:T(8,128)S(1)}, f32[4,32,256]{2,1,0:T(8,128)S(1)}, u32[]{:S(2)}, u32[]{:S(2)}) collective-permute-start(f32[4,32,256]{2,1,0:T(8,128)S(1)} %choose_slab.1.refs_0_), channel_id=1, source_target_pairs={{3,0},{0,1},{1,2},{2,3},{7,4},{4,5},{5,6},{6,7},{11,8},{8,9},{9,10... | collective-permute-start | bytes 393224 | tf_op jit(solution)/shard_map/ppermute | solution.py:601
  51.7 13.7 %copy-start.19 = (f32[2,256,256]{2,1,0:T(8,128)}, f32[2,256,256]{2,1,0:T(8,128)S(1)}, u32[]{:S(2)}) copy-start(f32[2,256,256]{2,1,0:T(8,128)S(1)} %collective-permute-done.refs_1_) | copy-start | bytes 1572868
  51.7 12.1 %collective-permute-start.14 = (f32[4,32,256]{2,1,0:T(8,128)S(1)}, f32[4,32,256]{2,1,0:T(8,128)S(1)}, u32[]{:S(2)}, u32[]{:S(2)}) collective-permute-start(f32[4,32,256]{2,1,0:T(8,128)S(1)} %choose_slab.1.refs_0_), channel_id=1, source_target_pairs={{0,16},{16,0},{1,17},{17,1},{2,18},{18,2},{3,19},{19,3},{4,20},{20... | collective-permute-start | bytes 393224 | tf_op jit(solution)/shard_map/ppermute | solution.py:651
  56.6 8.7 %copy-start.22 = (f32[2,256,256]{2,1,0:T(8,128)}, f32[2,256,256]{2,1,0:T(8,128)S(1)}, u32[]{:S(2)}) copy-start(f32[2,256,256]{2,1,0:T(8,128)S(1)} %collective-permute-done.2.refs_3_) | copy-start | bytes 1572868
  56.6 16.0 %collective-permute-start.18 = (f32[2,256,256]{2,1,0:T(8,128)S(1)}, f32[2,256,256]{2,1,0:T(8,128)S(1)}, u32[]{:S(2)}, u32[]{:S(2)}) collective-permute-start(f32[2,256,256]{2,1,0:T(8,128)S(1)} %copy-done.15), channel_id=1, source_target_pairs={{0,4},{4,0},{8,12},{12,8},{1,5},{5,1},{9,13},{13,9},{2,6},{6,2},{1... | collective-permute-start | bytes 1572872 | tf_op jit(solution)/shard_map/ppermute | solution.py:617
  57.3 15.4 %collective-permute-start.19 = (f32[2,256,256]{2,1,0:T(8,128)S(1)}, f32[2,256,256]{2,1,0:T(8,128)S(1)}, u32[]{:S(2)}, u32[]{:S(2)}) collective-permute-start(f32[2,256,256]{2,1,0:T(8,128)S(1)} %copy-done.14), channel_id=1, source_target_pairs={{0,12},{4,8},{8,4},{12,0},{1,13},{5,9},{9,5},{13,1},{2,14},{6,10},... | collective-permute-start | bytes 1572872 | tf_op jit(solution)/shard_map/ppermute | solution.py:617
  61.8 7.3 %collective-permute-start.15 = (f32[4,32,256]{2,1,0:T(8,128)S(1)}, f32[4,32,256]{2,1,0:T(8,128)S(1)}, u32[]{:S(2)}, u32[]{:S(2)}) collective-permute-start(f32[4,32,256]{2,1,0:T(8,128)S(1)} %collective-permute-done.11.refs_1_), channel_id=1, source_target_pairs={{0,16},{16,0},{1,17},{17,1},{2,18},{18,2},{3,19},{19,3},{4,20},{20... | collective-permute-start | bytes 393224 | tf_op jit(solution)/shard_map/ppermute | solution.py:651
  63.3 7.2 %collective-permute-start.16 = (f32[4,32,256]{2,1,0:T(8,128)S(1)}, f32[4,32,256]{2,1,0:T(8,128)S(1)}, u32[]{:S(2)}, u32[]{:S(2)}) collective-permute-start(f32[4,32,256]{2,1,0:T(8,128)S(1)} %collective-permute-done.12.refs_2_), channel_id=1, source_target_pairs={{0,16},{16,0},{1,17},{17,1},{2,18},{18,2},{3,19},{19,3},{4,20},{20... | collective-permute-start | bytes 393224 | tf_op jit(solution)/shard_map/ppermute | solution.py:651
  63.8 8.1 %collective-permute-start.17 = (f32[4,32,256]{2,1,0:T(8,128)S(1)}, f32[4,32,256]{2,1,0:T(8,128)S(1)}, u32[]{:S(2)}, u32[]{:S(2)}) collective-permute-start(f32[4,32,256]{2,1,0:T(8,128)S(1)} %collective-permute-done.13.refs_3_), channel_id=1, source_target_pairs={{0,16},{16,0},{1,17},{17,1},{2,18},{18,2},{3,19},{19,3},{4,20},{20... | collective-permute-start | bytes 393224 | tf_op jit(solution)/shard_map/ppermute | solution.py:651
  69.0 16.0 %collective-permute-start.23 = (f32[128,1024]{1,0:T(8,128)}, f32[128,1024]{1,0:T(8,128)}, u32[]{:S(2)}, u32[]{:S(2)}) collective-permute-start(f32[128,1024]{1,0:T(8,128)} %late_first.1.refs_6_.a_ref), channel_id=1, source_target_pairs={{0,1},{1,0},{2,3},{3,2},{4,5},{5,4},{6,7},{7,6},{8,9},{9,8},{10,11... | collective-permute-start | bytes 1572872 | tf_op jit(solution)/shard_map/ppermute | solution.py:611
  77.3 10.6 %copy-start.24 = (f32[2,256,256]{2,1,0:T(8,128)S(1)}, f32[2,256,256]{2,1,0:T(8,128)}, u32[]{:S(2)}) copy-start(f32[2,256,256]{2,1,0:T(8,128)} %get-tuple-element.73) | copy-start | bytes 1572868
  77.3 10.6 %copy-start.23 = (f32[2,256,256]{2,1,0:T(8,128)S(1)}, f32[2,256,256]{2,1,0:T(8,128)}, u32[]{:S(2)}) copy-start(f32[2,256,256]{2,1,0:T(8,128)} %get-tuple-element.74) | copy-start | bytes 1572868
  77.3 12.1 %copy-start.20 = (f32[2,256,256]{2,1,0:T(8,128)S(1)}, f32[2,256,256]{2,1,0:T(8,128)}, u32[]{:S(2)}) copy-start(f32[2,256,256]{2,1,0:T(8,128)} %get-tuple-element.75) | copy-start | bytes 1572868
  84.9 14.1 %copy-start.30 = (f32[2,128,256]{2,1,0:T(8,128)S(1)}, f32[2,128,256]{2,1,0:T(8,128)}, u32[]{:S(2)}) copy-start(f32[2,128,256]{2,1,0:T(8,128)} %get-tuple-element.83) | copy-start | bytes 786436
  84.9 15.7 %copy-start.29 = (f32[2,128,256]{2,1,0:T(8,128)S(1)}, f32[2,128,256]{2,1,0:T(8,128)}, u32[]{:S(2)}) copy-start(f32[2,128,256]{2,1,0:T(8,128)} %get-tuple-element.84) | copy-start | bytes 786436
  84.9 12.7 %collective-permute-start.31 = (f32[2,256,256]{2,1,0:T(8,128)S(1)}, f32[2,256,256]{2,1,0:T(8,128)S(1)}, u32[]{:S(2)}, u32[]{:S(2)}) collective-permute-start(f32[2,256,256]{2,1,0:T(8,128)S(1)} %get-tuple-element.87), channel_id=1, source_target_pairs={{0,1},{1,0},{2,3},{3,2},{4,5},{5,4},{6,7},{7,6},{8,9},{9,8},{10,11... | collective-permute-start | bytes 1572872 | tf_op jit(solution)/shard_map/ppermute | solution.py:611
  86.3 12.7 %collective-permute-start.24 = (f32[128,1024]{1,0:T(8,128)S(1)}, f32[128,1024]{1,0:T(8,128)S(1)}, u32[]{:S(2)}, u32[]{:S(2)}) collective-permute-start(f32[128,1024]{1,0:T(8,128)S(1)} %late_second.1.a_ref), channel_id=1, source_target_pairs={{0,16},{16,0},{1,17},{17,1},{2,18},{18,2},{3,19},{19,3},{4,20},{20... | collective-permute-start | bytes 1572872 | tf_op jit(solution)/shard_map/ppermute | solution.py:611
  87.9 12.7 %collective-permute-start.20 = (f32[2,256,256]{2,1,0:T(8,128)S(1)}, f32[2,256,256]{2,1,0:T(8,128)S(1)}, u32[]{:S(2)}, u32[]{:S(2)}) collective-permute-start(f32[2,256,256]{2,1,0:T(8,128)S(1)} %copy-done.24), channel_id=1, source_target_pairs={{0,4},{4,0},{8,12},{12,8},{1,5},{5,1},{9,13},{13,9},{2,6},{6,2},{1... | collective-permute-start | bytes 1572872 | tf_op jit(solution)/shard_map/ppermute | solution.py:617
  87.9 14.8 %collective-permute-start.21 = (f32[2,256,256]{2,1,0:T(8,128)S(1)}, f32[2,256,256]{2,1,0:T(8,128)S(1)}, u32[]{:S(2)}, u32[]{:S(2)}) collective-permute-start(f32[2,256,256]{2,1,0:T(8,128)S(1)} %copy-done.23), channel_id=1, source_target_pairs={{0,8},{4,12},{8,0},{12,4},{1,9},{5,13},{9,1},{13,5},{2,10},{6,14},... | collective-permute-start | bytes 1572872 | tf_op jit(solution)/shard_map/ppermute | solution.py:617
  89.5 23.5 %collective-permute-start.22 = (f32[2,256,256]{2,1,0:T(8,128)S(1)}, f32[2,256,256]{2,1,0:T(8,128)S(1)}, u32[]{:S(2)}, u32[]{:S(2)}) collective-permute-start(f32[2,256,256]{2,1,0:T(8,128)S(1)} %copy-done.20), channel_id=1, source_target_pairs={{0,12},{4,8},{8,4},{12,0},{1,13},{5,9},{9,5},{13,1},{2,14},{6,10},... | collective-permute-start | bytes 1572872 | tf_op jit(solution)/shard_map/ppermute | solution.py:617
  97.6 23.1 %collective-permute-start.28 = (f32[2,128,256]{2,1,0:T(8,128)}, f32[2,128,256]{2,1,0:T(8,128)S(1)}, u32[]{:S(2)}, u32[]{:S(2)}) collective-permute-start(f32[2,128,256]{2,1,0:T(8,128)} %get-tuple-element.82), channel_id=1, source_target_pairs={{0,4},{4,0},{8,12},{12,8},{1,5},{5,1},{9,13},{13,9},{2,6},{6,2},{1... | collective-permute-start | bytes 786440 | tf_op jit(solution)/shard_map/ppermute | solution.py:617
  99.0 22.9 %collective-permute-start.29 = (f32[2,128,256]{2,1,0:T(8,128)S(1)}, f32[2,128,256]{2,1,0:T(8,128)S(1)}, u32[]{:S(2)}, u32[]{:S(2)}) collective-permute-start(f32[2,128,256]{2,1,0:T(8,128)S(1)} %copy-done.30), channel_id=1, source_target_pairs={{0,8},{4,12},{8,0},{12,4},{1,9},{5,13},{9,1},{13,5},{2,10},{6,14},... | collective-permute-start | bytes 786440 | tf_op jit(solution)/shard_map/ppermute | solution.py:617
  100.6 13.9 %copy-start.25 = (f32[2,256,256]{2,1,0:T(8,128)}, f32[2,256,256]{2,1,0:T(8,128)S(1)}, u32[]{:S(2)}) copy-start(f32[2,256,256]{2,1,0:T(8,128)S(1)} %collective-permute-done.20.refs_4_) | copy-start | bytes 1572868
  100.6 23.6 %collective-permute-start.30 = (f32[2,128,256]{2,1,0:T(8,128)S(1)}, f32[2,128,256]{2,1,0:T(8,128)S(1)}, u32[]{:S(2)}, u32[]{:S(2)}) collective-permute-start(f32[2,128,256]{2,1,0:T(8,128)S(1)} %copy-done.29), channel_id=1, source_target_pairs={{0,12},{4,8},{8,4},{12,0},{1,13},{5,9},{9,5},{13,1},{2,14},{6,10},... | collective-permute-start | bytes 786440 | tf_op jit(solution)/shard_map/ppermute | solution.py:617
  102.7 11.8 %copy-start.26 = (f32[2,256,256]{2,1,0:T(8,128)}, f32[2,256,256]{2,1,0:T(8,128)S(1)}, u32[]{:S(2)}) copy-start(f32[2,256,256]{2,1,0:T(8,128)S(1)} %collective-permute-done.21.refs_5_) | copy-start | bytes 1572868
  102.7 35.0 %collective-permute-start.25 = (f32[2,128,256]{2,1,0:T(8,128)}, f32[2,128,256]{2,1,0:T(8,128)}, u32[]{:S(2)}, u32[]{:S(2)}) collective-permute-start(f32[2,128,256]{2,1,0:T(8,128)} %get-tuple-element.78), channel_id=1, source_target_pairs={{0,4},{4,0},{8,12},{12,8},{1,5},{5,1},{9,13},{13,9},{2,6},{6,2},{1... | collective-permute-start | bytes 786440 | tf_op jit(solution)/shard_map/ppermute | solution.py:617
  113.0 32.5 %collective-permute-start.26 = (f32[2,128,256]{2,1,0:T(8,128)}, f32[2,128,256]{2,1,0:T(8,128)}, u32[]{:S(2)}, u32[]{:S(2)}) collective-permute-start(f32[2,128,256]{2,1,0:T(8,128)} %get-tuple-element.79), channel_id=1, source_target_pairs={{0,8},{4,12},{8,0},{12,4},{1,9},{5,13},{9,1},{13,5},{2,10},{6,14},... | collective-permute-start | bytes 786440 | tf_op jit(solution)/shard_map/ppermute | solution.py:617
  114.5 6.2 %copy-start.28 = (f32[2,128,256]{2,1,0:T(8,128)S(1)}, f32[2,128,256]{2,1,0:T(8,128)}, u32[]{:S(2)}) copy-start(f32[2,128,256]{2,1,0:T(8,128)} %get-tuple-element.80) | copy-start | bytes 786436
  120.7 3.6 %copy-start.32 = (f32[2,128,256]{2,1,0:T(8,128)}, f32[2,128,256]{2,1,0:T(8,128)S(1)}, u32[]{:S(2)}) copy-start(f32[2,128,256]{2,1,0:T(8,128)S(1)} %collective-permute-done.28.refs_4_) | copy-start | bytes 786436
  120.7 25.5 %collective-permute-start.27 = (f32[2,128,256]{2,1,0:T(8,128)S(1)}, f32[2,128,256]{2,1,0:T(8,128)S(1)}, u32[]{:S(2)}, u32[]{:S(2)}) collective-permute-start(f32[2,128,256]{2,1,0:T(8,128)S(1)} %copy-done.28), channel_id=1, source_target_pairs={{0,12},{4,8},{8,4},{12,0},{1,13},{5,9},{9,5},{13,1},{2,14},{6,10},... | collective-permute-start | bytes 786440 | tf_op jit(solution)/shard_map/ppermute | solution.py:617
  121.9 15.8 %collective-permute-start.32 = (f32[256,256]{1,0:T(8,128)S(1)}, f32[256,256]{1,0:T(8,128)S(1)}, u32[]{:S(2)}, u32[]{:S(2)}) collective-permute-start(f32[256,256]{1,0:T(8,128)S(1)} %get-tuple-element.89), channel_id=1, source_target_pairs={{0,2},{1,3},{2,0},{3,1},{4,6},{5,7},{6,4},{7,5},{8,10},{9,11},{10,... | collective-permute-start | bytes 786440 | tf_op jit(solution)/shard_map/ppermute | solution.py:611
  129.2 26.5 %collective-permute-start.34 = (f32[128,256]{1,0:T(8,128)S(1)}, f32[128,256]{1,0:T(8,128)S(1)}, u32[]{:S(2)}, u32[]{:S(2)}) collective-permute-start(f32[128,256]{1,0:T(8,128)S(1)} %get-tuple-element.92), channel_id=1, source_target_pairs={{0,3},{1,0},{2,1},{3,2},{4,7},{5,4},{6,5},{7,6},{8,11},{9,8},{10,9... | collective-permute-start | bytes 393224 | tf_op jit(solution)/shard_map/ppermute | solution.py:606
  137.7 18.4 %collective-permute-start.35 = (f32[128,256]{1,0:T(8,128)S(1)}, f32[128,256]{1,0:T(8,128)S(1)}, u32[]{:S(2)}, u32[]{:S(2)}) collective-permute-start(f32[128,256]{1,0:T(8,128)S(1)} %get-tuple-element.93), channel_id=1, source_target_pairs={{0,2},{1,3},{2,0},{3,1},{4,6},{5,7},{6,4},{7,5},{8,10},{9,11},{10,... | collective-permute-start | bytes 393224 | tf_op jit(solution)/shard_map/ppermute | solution.py:606
  137.7 8.5 %copy-start = (f32[256,256]{1,0:T(8,128)}, f32[256,256]{1,0:T(8,128)S(1)}, u32[]{:S(2)}) copy-start(f32[256,256]{1,0:T(8,128)S(1)} %first_image.1.refs_12_) | copy-start | bytes 786436
  137.7 20.3 %collective-permute-start.36 = (f32[128,256]{1,0:T(8,128)S(1)}, f32[128,256]{1,0:T(8,128)S(1)}, u32[]{:S(2)}, u32[]{:S(2)}) collective-permute-start(f32[128,256]{1,0:T(8,128)S(1)} %get-tuple-element.94), channel_id=1, source_target_pairs={{0,1},{1,2},{2,3},{3,0},{4,5},{5,6},{6,7},{7,4},{8,9},{9,10},{10,1... | collective-permute-start | bytes 393224 | tf_op jit(solution)/shard_map/ppermute | solution.py:606
  145.6 26.6 %collective-permute-start.33 = (f32[256,256]{1,0:T(8,128)S(1)}, f32[256,256]{1,0:T(8,128)S(1)}, u32[]{:S(2)}, u32[]{:S(2)}) collective-permute-start(f32[256,256]{1,0:T(8,128)S(1)} %first_image.1.refs_12_), channel_id=1, source_target_pairs={{0,0},{1,4},{2,8},{3,12},{4,5},{5,1},{6,13},{7,9},{8,10},{9,14},{1... | collective-permute-start | bytes 786440 | tf_op jit(solution)/shard_map/ppermute | solution.py:676
  151.2 8.4 %collective-permute-start.37 = (f32[128,256]{1,0:T(8,128)S(1)}, f32[128,256]{1,0:T(8,128)S(1)}, u32[]{:S(2)}, u32[]{:S(2)}) collective-permute-start(f32[128,256]{1,0:T(8,128)S(1)} %get-tuple-element.96), channel_id=1, source_target_pairs={{0,3},{1,0},{2,1},{3,2},{4,7},{5,4},{6,5},{7,6},{8,11},{9,8},{10,9... | collective-permute-start | bytes 393224 | tf_op jit(solution)/shard_map/ppermute | solution.py:606
  155.7 16.5 %collective-permute-start.38 = (f32[128,256]{1,0:T(8,128)S(1)}, f32[128,256]{1,0:T(8,128)S(1)}, u32[]{:S(2)}, u32[]{:S(2)}) collective-permute-start(f32[128,256]{1,0:T(8,128)S(1)} %get-tuple-element.97), channel_id=1, source_target_pairs={{0,2},{1,3},{2,0},{3,1},{4,6},{5,7},{6,4},{7,5},{8,10},{9,11},{10,... | collective-permute-start | bytes 393224 | tf_op jit(solution)/shard_map/ppermute | solution.py:606
  156.1 16.1 %collective-permute-start.39 = (f32[128,256]{1,0:T(8,128)S(1)}, f32[128,256]{1,0:T(8,128)S(1)}, u32[]{:S(2)}, u32[]{:S(2)}) collective-permute-start(f32[128,256]{1,0:T(8,128)S(1)} %get-tuple-element.98), channel_id=1, source_target_pairs={{0,1},{1,2},{2,3},{3,0},{4,5},{5,6},{6,7},{7,4},{8,9},{9,10},{10,1... | collective-permute-start | bytes 393224 | tf_op jit(solution)/shard_map/ppermute | solution.py:606
  (14 other events, 13.5 us)

commit v4 on v3

--- a/solution.py
+++ b/solution.py
@@ -328,7 +328,7 @@
     refs = refs[3:]
     if with_image:
         other_ref = refs[0]
-        out_ref, terms, line = refs[-(RADIX + 2)], refs[-(RADIX + 1) : -1], refs[-1]
+        out_ref, keep_ref, send_ref, line = refs[-4:]
     else:
         out_ref = refs[-1]
     block = fields[0].shape[2]
@@ -344,11 +344,10 @@
         out_ref[0, 0, :, at] = value[0]
         out_ref[1, 0, :, at] = value[1]
     if with_image:
-        count = len(terms)
-        part = line.shape[1] // count
-        for t in range(count):
-            at = pl.ds(pl.multiple_of(lax.rem(place_ref[0] + t, count) * part, part), part)
-            terms[t][...] = line[:, at]
+        mine = lax.bitwise_and(place_ref[0], 1)
+        for j in range(RADIX // 2):
+            for ref, first in ((keep_ref, mine), (send_ref, 1 - mine)):
+                ref[j] = line[:, pl.ds(pl.multiple_of((first + 2 * j) * block, block), block)]
 
 
 def last_stage(fields, slab, blocks, shift, slot, place, start, rows, other, held, after=()):
@@ -368,8 +367,9 @@
         args += far([other])
         specs.append(wide)
         cols = width // RADIX
-        outs += [jax.ShapeDtypeStruct((part, cols), F32)] * RADIX
-        out_specs += [whole((part, cols))] * RADIX
+        split = (RADIX // 2, part, cols)
+        outs += [jax.ShapeDtypeStruct(split, F32)] * 2
+        out_specs += [whole(split)] * 2
         scratch = [pltpu.VMEM((part, width), F32)]
     alias = {}
     if held is not None:
@@ -544,7 +544,7 @@
         out_shape=[jax.ShapeDtypeStruct(shape, F32)] * 2,
         compiler_params=params(),
         cost_estimate=BRIEF,
-        name="first_image_fold",
+        name="image_fold",
     )(place, a, b)
 
 
@@ -672,7 +672,8 @@
             r_last[c], late, blocks, shift, slot, place, c * (rows // CHUNKS), rows, source_out, receiver_out,
             [total] if c == CHUNKS - 1 else [],
         )
-        groups.append(swap_slots(terms, "freq"))
+        part_keep, part_send = fold_stage(terms[0], paired(terms[1], "freq", 1), place)
+        groups.append([part_keep, paired(part_send, "freq", 2)])
     first_image = lax.ppermute(total, ("row", "freq"), pairs)
     return (source_out, receiver_out, image_stage(first_image, groups))
 
@@ -712,7 +713,7 @@
     )
     term = jnp.stack([term[0][0], term[1][0], term[0][1], term[1][1]]).reshape(-1, term[0].shape[2])
     images = [lax.all_to_all(term, "row", split_axis=0, concat_axis=1, tiled=True)]
-    images.append(jnp.concatenate(terms, axis=1))
+    images.append(jnp.concatenate([terms[0][0], terms[1][0], terms[0][1], terms[1][1]], axis=1))
     parts = [lax.psum_scatter(t, "freq", scatter_dimension=1, tiled=True) for t in images]
     return (source_out, receiver_out, jnp.stack(parts))
 

time: 173 us -> 172 us (level)
  starting transfers between devices: 54 us -> 47.2 us
  waiting for transfers between devices: 64 us -> 68.1 us
    ppermute x5 -> x9, waiting for transfers between devices: 25.1 us -> 43.3 us  [paired(): lax.ppermute(value, axis, [(i, i ^ bits) for i in range(lax.axis_size(axi...]
    ppermute x9 -> x3, starting transfers between devices: 23.7 us -> 6.19 us  [swap_slots(): lax.ppermute(pieces[s], axis, [(i, (i + s) % count) for i in range(count)])]
    ppermute x9 -> x3, waiting for transfers between devices: 16.9 us -> 2.78 us  [swap_slots(): lax.ppermute(pieces[s], axis, [(i, (i + s) % count) for i in range(count)])]
    ppermute x5 -> x9, starting transfers between devices: 6.77 us -> 17.5 us  [paired(): lax.ppermute(value, axis, [(i, i ^ bits) for i in range(lax.axis_size(axi...]
    unnamed x76 -> x78, local copies, waits for them, and re-layouts: 7.49 us -> 8.21 us
  transfers between devices with their start and end apart: 40 -> 38, of which waited for: 14 -> 15; matrix products, arithmetic and copies ran while one was open for 0% -> 0% of each run, Pallas kernels for 25% -> 26%
where the time goes in v4:
time: 172 us; the launch traced here: 171 us
  waiting for transfers between devices  68.1 us (40%)
  starting transfers between devices  47.2 us (27%)
  Pallas kernels  45.9 us (27%)
  local copies, waits for them, and re-layouts  8.21 us (5%)
    ppermute x9, waiting for transfers between devices, paired(): lax.ppermute(value, axis, [(i, i ^ bits) for i in range(lax.axis_size(axi...  43.3 us
    ppermute x9, starting transfers between devices, paired(): lax.ppermute(value, axis, [(i, i ^ bits) for i in range(lax.axis_size(axi...  17.5 us
    ppermute x18, waiting for transfers between devices, swap_pairs(): lax.ppermute(pieces[s], axis, [(i, i ^ s) for i in range(count)])  15.9 us
    ppermute x18, starting transfers between devices, swap_pairs(): lax.ppermute(pieces[s], axis, [(i, i ^ s) for i in range(count)])  14.9 us
    pallas_call x3, Pallas kernels, last_stage(): pl.pallas_call(lambda *refs: last_kernel(with_image, *refs), grid_spec=pl...  14.6 us
    pallas_call x2, Pallas kernels, middle_stage(): pl.pallas_call(lambda *refs: middle_kernel(count, with_image, len(after),...  11.3 us
    unnamed x78, local copies, waits for them, and re-layouts  8.21 us
    pallas_call x2, Pallas kernels, first_stage(): pl.pallas_call(lambda *refs: first_kernel(form, len(after), *refs), grid_...  7.97 us
  transfers between devices with their start and end apart: 38, of which 15 were waited for; matrix products, arithmetic and copies ran while one was open for 0% of the time, Pallas kernels for 26%

profile of v4, /device:TPU:0, one launch (start us, length us, event | category | flops | bytes accessed | tf_op | source)
XLA Modules:
  0.0 171.2 jit_solution(11815721828276104001)
XLA Ops:
  0.6 1.2 copy-done.4
  1.9 0.7 copy-done.5
  2.5 1.4 cut_slab.1
  3.9 0.7 copy-done.13
  5.0 2.5 %collective-permute-start.4 = (f32[4,32,256]{2,1,0:T(8,128)S(1)}, f32[4,32,256]{2,1,0:T(8,128)S(1)}, u32[]{:S(2)}, u32[]{:S(2)}) collective-permute-start(f32[4,32,256]{2,1,0:T(8,128)S(1)} %get-tuple-element.59), channel_id=1, source_target_pairs={{0,8},{4,12},{8,0},{12,4},{1,9},{5,13},{9,1},{13,5},{2,10},{6,14},... | collective-permute-start | bytes 393224 | tf_op jit(solution)/shard_map/ppermute | solution.py:617
  7.7 2.8 %collective-permute-start.10 = (f32[128,1024]{1,0:T(8,128)}, f32[128,1024]{1,0:T(8,128)}, u32[]{:S(2)}, u32[]{:S(2)}) collective-permute-start(f32[128,1024]{1,0:T(8,128)} %get-tuple-element.67.a_ref), channel_id=1, source_target_pairs={{0,2},{1,3},{2,0},{3,1},{4,6},{5,7},{6,4},{7,5},{8,10},{9,11},{10,... | collective-permute-start | bytes 1572872 | tf_op jit(solution)/shard_map/ppermute | solution.py:611
  11.2 4.6 %along_y_first_s.1 = (f32[2,256,256]{2,1,0:T(8,128)}, f32[2,256,256]{2,1,0:T(8,128)}, f32[2,256,256]{2,1,0:T(8,128)}, f32[2,256,256]{2,1,0:T(8,128)}, bf16[4,512...) custom-call(s32[1]{0:T(128)} %bitcast.shift_ref.refs_0_, s32[1]{0:T(128)S(6)} %copy.11.refs_1_.slot_ref, ...), custom_call_target="tpu_custom_call" | custom-call | flops 99999997952 | bytes 10000000 | tf_op jit(solution)/shard_map/along_y_first_s/pallas_call | solution.py:225
  15.7 1.5 collective-permute-start.1
  17.3 0.6 copy-done.36
  18.0 3.4 %along_y_first_r.1 = (f32[2,256,256]{2,1,0:T(8,128)}, f32[2,256,256]{2,1,0:T(8,128)}, f32[2,256,256]{2,1,0:T(8,128)}, f32[2,256,256]{2,1,0:T(8,128)}) custom-call(s32[1]{0:T(128)} %bitcast.shift_ref.refs_0_, s32[1]{0:T(128)S(6)} %copy.11.refs_1_.slot_ref, f32[2,1,256,1024]{3,2,1,0:T(8,128)S(1)} %copy-done.3, f32[2,1,256,1024]{3,2,1,0:T(8,128)S(1)} %copy-done.3, ...), custom_call_target="tpu_custom_call" | custom-call | flops 99999997952 | bytes 10000000 | tf_op jit(solution)/shard_map/along_y_first_r/pallas_call | solution.py:225
  21.4 0.7 collective-permute-start.9
  22.1 1.0 copy-done.12
  23.2 1.2 regroup_slab.1
  24.4 1.5 collective-permute-start.6
  25.9 1.6 collective-permute-start.7
  27.5 10.2 %collective-permute-done.10.b_ref = f32[128,1024]{1,0:T(8,128)} collective-permute-done((f32[128,1024]{1,0:T(8,128)}, f32[128,1024]{1,0:T(8,128)}, u32[]{:S(2)}, u32[]{:S(2)}) %collective-permute-start.10) | collective-permute-done | bytes 524320 | tf_op jit(solution)/shard_map/ppermute | solution.py:611
  37.7 3.1 %collective-permute-start.8 = (f32[4,32,256]{2,1,0:T(8,128)S(1)}, f32[4,32,256]{2,1,0:T(8,128)S(1)}, u32[]{:S(2)}, u32[]{:S(2)}) collective-permute-start(f32[4,32,256]{2,1,0:T(8,128)S(1)} %get-tuple-element.65), channel_id=1, source_target_pairs={{0,1},{1,2},{2,3},{3,0},{4,5},{5,6},{6,7},{7,4},{8,9},{9,10},{10,1... | collective-permute-start | bytes 393224 | tf_op jit(solution)/shard_map/ppermute | solution.py:606
  40.8 2.1 %late_first.1.refs_6_.a_ref = f32[128,1024]{1,0:T(8,128)} custom-call(f32[128,1024]{1,0:T(8,128)} %get-tuple-element.67.a_ref, f32[128,1024]{1,0:T(8,128)} %collective-permute-done.10.b_ref), custom_call_target="tpu_custom_call" | custom-call | flops 1000 | bytes 1000 | tf_op jit(solution)/shard_map/late_first/pallas_call | solution.py:516
  42.9 1.6 collective-permute-start.2
  44.5 2.8 %collective-permute-done.8.refs_3_ = f32[4,32,256]{2,1,0:T(8,128)S(1)} collective-permute-done((f32[4,32,256]{2,1,0:T(8,128)S(1)}, f32[4,32,256]{2,1,0:T(8,128)S(1)}, u32[]{:S(2)}, u32[]{:S(2)}) %collective-permute-start.8) | collective-permute-done | bytes 131104 | tf_op jit(solution)/shard_map/ppermute | solution.py:606
  47.3 0.8 copy-done.14
  48.1 0.6 choose_slab.1.refs_0_
  48.7 1.9 %collective-permute-start.11 = (f32[4,32,256]{2,1,0:T(8,128)S(1)}, f32[4,32,256]{2,1,0:T(8,128)S(1)}, u32[]{:S(2)}, u32[]{:S(2)}) collective-permute-start(f32[4,32,256]{2,1,0:T(8,128)S(1)} %choose_slab.1.refs_0_), channel_id=1, source_target_pairs={{1,0},{2,1},{3,2},{0,3},{5,4},{6,5},{7,6},{4,7},{9,8},{10,9},{11,1... | collective-permute-start | bytes 393224 | tf_op jit(solution)/shard_map/ppermute | solution.py:601
  50.5 1.1 collective-permute-start.13
  51.7 1.5 collective-permute-start.14
  53.2 3.4 %collective-permute-done.2.refs_3_ = f32[2,256,256]{2,1,0:T(8,128)S(1)} collective-permute-done((f32[2,256,256]{2,1,0:T(8,128)S(1)}, f32[2,256,256]{2,1,0:T(8,128)S(1)}, u32[]{:S(2)}, u32[]{:S(2)}) %collective-permute-start.2) | collective-permute-done | bytes 524320 | tf_op jit(solution)/shard_map/ppermute | solution.py:617
  56.6 0.7 collective-permute-start.18
  57.3 1.2 collective-permute-start.19
  58.5 3.3 %collective-permute-done.12.refs_2_ = f32[4,32,256]{2,1,0:T(8,128)S(1)} collective-permute-done((f32[4,32,256]{2,1,0:T(8,128)S(1)}, f32[4,32,256]{2,1,0:T(8,128)S(1)}, u32[]{:S(2)}, u32[]{:S(2)}) %collective-permute-start.12) | collective-permute-done | bytes 131104 | tf_op jit(solution)/shard_map/ppermute | solution.py:601
  61.8 1.5 collective-permute-start.15
  63.8 1.5 collective-permute-start.17
  65.3 3.7 %along_x_s_first.1.refs_8_.refs_2_ = f32[4,2,256,256]{3,2,1,0:T(8,128)S(1)} custom-call(s32[1]{0:T(128)} %bitcast.shift_ref.refs_0_, f32[2,256,256]{2,1,0:T(8,128)} %get-tuple-element.52.refs_0_, f32[2,256,256]{2,1,0:T(8,128)} %copy-done.20, f32[2,256,256]{2,1,0:T(8,128)} %collective-permute-done.1.refs_2_.refs_4_, f32[2,256,256]{2,1,0:T(8,128)} %copy-done.23, ...), custom_call_target="tpu_custom_call" | custom-call | flops 99999997952 | bytes 10000000 | tf_op jit(solution)/shard_map/along_x_s_first/pallas_call | solution.py:252
  69.1 1.4 collective-permute-done.16.refs_6_
  70.5 1.4 collective-permute-done.17.refs_7_
  71.9 0.8 phases.1
  72.7 0.8 copy-done.19
  73.7 3.7 %along_x_s_second.1 = (f32[2,256,256]{2,1,0:T(8,128)}, f32[2,256,256]{2,1,0:T(8,128)}, f32[2,256,256]{2,1,0:T(8,128)}, f32[2,256,256]{2,1,0:T(8,128)}, f32[4,2,256,256]{3,2,1,0:T(8,128)S(1)}) custom-call(s32[1]{0:T(128)} %bitcast.shift_ref.refs_0_, s32[1]{0:T(128)} %bitcast.1.place_ref.refs_1_.refs_2_, ...), custom_call_target="tpu_custom_call" | custom-call | flops 99999997952 | bytes 10000000 | tf_op jit(solution)/shard_map/along_x_s_second/pallas_call | solution.py:307
  77.4 7.6 %along_x_r.1 = (f32[2,128,256]{2,1,0:T(8,128)}, f32[2,128,256]{2,1,0:T(8,128)}, f32[2,128,256]{2,1,0:T(8,128)}, f32[2,128,256]{2,1,0:T(8,128)}, f32[2,128,256]{2...) custom-call(s32[1]{0:T(128)} %bitcast.shift_ref.refs_0_, ...), custom_call_target="tpu_custom_call" | custom-call | flops 99999997952 | bytes 10000000 | tf_op jit(solution)/shard_map/along_x_r/pallas_call | solution.py:307
  85.0 1.3 late_second.1.a_ref
  86.3 1.6 collective-permute-start.24
  87.9 1.6 collective-permute-start.21
  89.8 7.8 %collective-permute-done.31.b_ref = f32[2,256,256]{2,1,0:T(8,128)S(1)} collective-permute-done((f32[2,256,256]{2,1,0:T(8,128)S(1)}, f32[2,256,256]{2,1,0:T(8,128)S(1)}, u32[]{:S(2)}, u32[]{:S(2)}) %collective-permute-start.31) | collective-permute-done | bytes 524320 | tf_op jit(solution)/shard_map/ppermute | solution.py:611
  97.7 1.3 collective-permute-done.24.b_ref
  99.0 1.5 collective-permute-start.29
  100.7 2.0 %collective-permute-done.21.refs_5_ = f32[2,256,256]{2,1,0:T(8,128)S(1)} collective-permute-done((f32[2,256,256]{2,1,0:T(8,128)S(1)}, f32[2,256,256]{2,1,0:T(8,128)S(1)}, u32[]{:S(2)}, u32[]{:S(2)}) %collective-permute-start.21) | collective-permute-done | bytes 524320 | tf_op jit(solution)/shard_map/ppermute | solution.py:617
  102.7 10.3 %collective-permute-done.22.refs_6_ = f32[2,256,256]{2,1,0:T(8,128)S(1)} collective-permute-done((f32[2,256,256]{2,1,0:T(8,128)S(1)}, f32[2,256,256]{2,1,0:T(8,128)S(1)}, u32[]{:S(2)}, u32[]{:S(2)}) %collective-permute-start.22) | collective-permute-done | bytes 524320 | tf_op jit(solution)/shard_map/ppermute | solution.py:617
  113.0 1.5 collective-permute-start.26
  114.5 6.2 %along_y_last_s.1.refs_10_ = f32[2,1,256,1024]{3,2,1,0:T(8,128)} custom-call(s32[1]{0:T(128)} %bitcast.shift_ref.refs_0_, s32[1]{0:T(128)S(6)} %copy.11.refs_1_.slot_ref, s32[1]{0:T(128)} %bitcast.1.place_ref.refs_1_.refs_2_, f32[2,256,256]{2,1,0:T(8,128)} %get-tuple-element.72.refs_3_, f32[2,256,256]{2,1,0:T(8,128)} %copy-done.26, ...), custom_call_target="tpu_custom_call" | custom-call | flops 99999997952 | bytes 10000000 | tf_op jit(solution)/shard_map/along_y_last_s/pallas_call | solution.py:381
  120.7 1.2 collective-permute-start.27
  121.9 2.2 %collective-permute-start.32 = (f32[256,256]{1,0:T(8,128)S(1)}, f32[256,256]{1,0:T(8,128)S(1)}, u32[]{:S(2)}, u32[]{:S(2)}) collective-permute-start(f32[256,256]{1,0:T(8,128)S(1)} %get-tuple-element.89), channel_id=1, source_target_pairs={{0,2},{1,3},{2,0},{3,1},{4,6},{5,7},{6,4},{7,5},{8,10},{9,11},{10,... | collective-permute-start | bytes 786440 | tf_op jit(solution)/shard_map/ppermute | solution.py:611
  124.3 0.7 copy-done.35
  125.0 4.2 %along_y_last_r.2 = (f32[2,1,256,1024]{3,2,1,0:T(8,128)}, f32[2,128,256]{2,1,0:T(8,128)S(1)}, f32[2,128,256]{2,1,0:T(8,128)S(1)}) custom-call(s32[1]{0:T(128)} %bitcast.shift_ref.refs_0_, s32[1]{0:T(128)S(6)} %copy.11.refs_1_.slot_ref, s32[1]{0:T(128)} %bitcast.1.place_ref.refs_1_.refs_2_, f32[2,128,256]{2,1,0:T(8,128)} %get-tuple-element.81.refs_3_, ...), custom_call_target="tpu_custom_call" | custom-call | flops 99999997952 | bytes 10000000 | tf_op jit(solution)/shard_map/along_y_last_r/pallas_call | solution.py:381
  129.2 2.0 %collective-permute-start.34 = (f32[2,128,256]{2,1,0:T(8,128)S(1)}, f32[2,128,256]{2,1,0:T(8,128)S(1)}, u32[]{:S(2)}, u32[]{:S(2)}) collective-permute-start(f32[2,128,256]{2,1,0:T(8,128)S(1)} %get-tuple-element.92), channel_id=1, source_target_pairs={{0,1},{1,0},{2,3},{3,2},{4,5},{5,4},{6,7},{7,6},{8,9},{9,8},{10,11... | collective-permute-start | bytes 786440 | tf_op jit(solution)/shard_map/ppermute | solution.py:611
  131.1 5.4 %collective-permute-done.32.b_ref = f32[256,256]{1,0:T(8,128)S(1)} collective-permute-done((f32[256,256]{1,0:T(8,128)S(1)}, f32[256,256]{1,0:T(8,128)S(1)}, u32[]{:S(2)}, u32[]{:S(2)}) %collective-permute-start.32) | collective-permute-done | bytes 262176 | tf_op jit(solution)/shard_map/ppermute | solution.py:611
  136.6 0.7 copy-done
  137.3 0.7 copy-done.34
  138.0 4.2 %along_y_last_r.3 = (f32[2,1,256,1024]{3,2,1,0:T(8,128)}, f32[2,128,256]{2,1,0:T(8,128)S(1)}, f32[2,128,256]{2,1,0:T(8,128)S(1)}) custom-call(s32[1]{0:T(128)} %bitcast.shift_ref.refs_0_, s32[1]{0:T(128)S(6)} %copy.11.refs_1_.slot_ref, s32[1]{0:T(128)} %bitcast.1.place_ref.refs_1_.refs_2_, ...), custom_call_target="tpu_custom_call", output_to_operand_aliasing={{0}: (11, {})} | custom-call | flops 99999997952 | bytes 10000000 | tf_op jit(solution)/shard_map/along_y_last_r/pallas_call | solution.py:381
  142.4 0.7 collective-permute-start.33
  143.1 5.2 %collective-permute-start.35 = (f32[128,256]{1,0:T(8,128)S(1)}, f32[128,256]{1,0:T(8,128)S(1)}, u32[]{:S(2)}, u32[]{:S(2)}) collective-permute-start(f32[128,256]{1,0:T(8,128)S(1)} %get-tuple-element.94), channel_id=1, source_target_pairs={{0,2},{1,3},{2,0},{3,1},{4,6},{5,7},{6,4},{7,5},{8,10},{9,11},{10,... | collective-permute-start | bytes 393224 | tf_op jit(solution)/shard_map/ppermute | solution.py:611
  148.3 1.2 collective-permute-done.36.b_ref
  149.5 3.4 %collective-permute-start.37 = (f32[128,256]{1,0:T(8,128)S(1)}, f32[128,256]{1,0:T(8,128)S(1)}, u32[]{:S(2)}, u32[]{:S(2)}) collective-permute-start(f32[128,256]{1,0:T(8,128)S(1)} %get-tuple-element.98), channel_id=1, source_target_pairs={{0,2},{1,3},{2,0},{3,1},{4,6},{5,7},{6,4},{7,5},{8,10},{9,11},{10,... | collective-permute-start | bytes 393224 | tf_op jit(solution)/shard_map/ppermute | solution.py:611
  152.9 16.0 %collective-permute-done.35.refs_2_ = f32[128,256]{1,0:T(8,128)S(1)} collective-permute-done((f32[128,256]{1,0:T(8,128)S(1)}, f32[128,256]{1,0:T(8,128)S(1)}, u32[]{:S(2)}, u32[]{:S(2)}) %collective-permute-start.35) | collective-permute-done | bytes 131104 | tf_op jit(solution)/shard_map/ppermute | solution.py:611
  168.9 1.4 collective-permute-done.37.refs_4_
  170.3 0.8 image_sum.1
  (110 shorter events, 2.6 us)
Async XLA Ops:
  2.5 8.6 %copy-start.2 = (f32[2,1,256,1024]{3,2,1,0:T(8,128)S(1)}, f32[2,1,256,1024]{3,2,1,0:T(8,128)}, u32[]{:S(2)}) copy-start(f32[2,1,256,1024]{3,2,1,0:T(8,128)} %refs_5_.2) | copy-start | bytes 6291460
  2.5 8.6 %copy-start.7 = (f32[512,1024]{1,0:T(8,128)S(1)}, f32[512,1024]{1,0:T(8,128)}, u32[]{:S(2)}) copy-start(f32[512,1024]{1,0:T(8,128)} %constant.15.clone.refs_7_) | copy-start | bytes 6291460
  4.6 12.7 %collective-permute-start.3 = (f32[4,32,256]{2,1,0:T(8,128)S(1)}, f32[4,32,256]{2,1,0:T(8,128)S(1)}, u32[]{:S(2)}, u32[]{:S(2)}) collective-permute-start(f32[4,32,256]{2,1,0:T(8,128)S(1)} %get-tuple-element.58), channel_id=1, source_target_pairs={{0,4},{4,0},{8,12},{12,8},{1,5},{5,1},{9,13},{13,9},{2,6},{6,2},{1... | collective-permute-start | bytes 393224 | tf_op jit(solution)/shard_map/ppermute | solution.py:617
  5.0 12.2 %collective-permute-start.4 = (f32[4,32,256]{2,1,0:T(8,128)S(1)}, f32[4,32,256]{2,1,0:T(8,128)S(1)}, u32[]{:S(2)}, u32[]{:S(2)}) collective-permute-start(f32[4,32,256]{2,1,0:T(8,128)S(1)} %get-tuple-element.59), channel_id=1, source_target_pairs={{0,8},{4,12},{8,0},{12,4},{1,9},{5,13},{9,1},{13,5},{2,10},{6,14},... | collective-permute-start | bytes 393224 | tf_op jit(solution)/shard_map/ppermute | solution.py:617
  7.5 9.7 %collective-permute-start.5 = (f32[4,32,256]{2,1,0:T(8,128)S(1)}, f32[4,32,256]{2,1,0:T(8,128)S(1)}, u32[]{:S(2)}, u32[]{:S(2)}) collective-permute-start(f32[4,32,256]{2,1,0:T(8,128)S(1)} %get-tuple-element.60), channel_id=1, source_target_pairs={{0,12},{4,8},{8,4},{12,0},{1,13},{5,9},{9,5},{13,1},{2,14},{6,10},... | collective-permute-start | bytes 393224 | tf_op jit(solution)/shard_map/ppermute | solution.py:617
  7.7 30.0 %collective-permute-start.10 = (f32[128,1024]{1,0:T(8,128)}, f32[128,1024]{1,0:T(8,128)}, u32[]{:S(2)}, u32[]{:S(2)}) collective-permute-start(f32[128,1024]{1,0:T(8,128)} %get-tuple-element.67.a_ref), channel_id=1, source_target_pairs={{0,2},{1,3},{2,0},{3,1},{4,6},{5,7},{6,4},{7,5},{8,10},{9,11},{10,... | collective-permute-start | bytes 1572872 | tf_op jit(solution)/shard_map/ppermute | solution.py:611
  11.2 6.8 %copy-start.3 = (f32[2,1,256,1024]{3,2,1,0:T(8,128)S(1)}, f32[2,1,256,1024]{3,2,1,0:T(8,128)}, u32[]{:S(2)}) copy-start(f32[2,1,256,1024]{3,2,1,0:T(8,128)} %refs_5_.3) | copy-start | bytes 6291460
  15.7 5.7 %copy-start.8 = (bf16[4,512,256]{2,1,0:T(8,128)(2,1)}, bf16[4,512,256]{2,1,0:T(8,128)(2,1)S(1)}, u32[]{:S(2)}) copy-start(bf16[4,512,256]{2,1,0:T(8,128)(2,1)S(1)} %get-tuple-element.56.refs_4_.refs_9_.refs_5_.refs_8_) | copy-start | bytes 3145732
  15.7 5.7 %copy-start.10 = (bf16[4,512,256]{2,1,0:T(8,128)(2,1)}, bf16[4,512,256]{2,1,0:T(8,128)(2,1)S(1)}, u32[]{:S(2)}) copy-start(bf16[4,512,256]{2,1,0:T(8,128)(2,1)S(1)} %get-tuple-element.57.refs_5_.refs_10_.refs_6_.refs_9_) | copy-start | bytes 3145732
  15.7 31.5 %collective-permute-start.1 = (f32[2,256,256]{2,1,0:T(8,128)}, f32[2,256,256]{2,1,0:T(8,128)}, u32[]{:S(2)}, u32[]{:S(2)}) collective-permute-start(f32[2,256,256]{2,1,0:T(8,128)} %get-tuple-element.54), channel_id=1, source_target_pairs={{0,8},{4,12},{8,0},{12,4},{1,9},{5,13},{9,1},{13,5},{2,10},{6,14},... | collective-permute-start | bytes 1572872 | tf_op jit(solution)/shard_map/ppermute | solution.py:617
  21.4 25.9 %collective-permute-start.9 = (f32[2,256,256]{2,1,0:T(8,128)}, f32[2,256,256]{2,1,0:T(8,128)S(1)}, u32[]{:S(2)}, u32[]{:S(2)}) collective-permute-start(f32[2,256,256]{2,1,0:T(8,128)} %get-tuple-element.66), channel_id=1, source_target_pairs={{0,8},{4,12},{8,0},{12,4},{1,9},{5,13},{9,1},{13,5},{2,10},{6,14},... | collective-permute-start | bytes 1572872 | tf_op jit(solution)/shard_map/ppermute | solution.py:617
  23.2 19.7 %copy-start.18 = (f32[2,256,256]{2,1,0:T(8,128)S(1)}, f32[2,256,256]{2,1,0:T(8,128)}, u32[]{:S(2)}) copy-start(f32[2,256,256]{2,1,0:T(8,128)} %get-tuple-element.53) | copy-start | bytes 1572868
  23.2 19.7 %copy-start.17 = (f32[2,256,256]{2,1,0:T(8,128)S(1)}, f32[2,256,256]{2,1,0:T(8,128)}, u32[]{:S(2)}) copy-start(f32[2,256,256]{2,1,0:T(8,128)} %get-tuple-element.55) | copy-start | bytes 1572868
  23.2 24.9 %copy-start.6 = (s32[4]{0:T(128)S(1)}, s32[4]{0:T(128)}, u32[]{:S(2)}) copy-start(s32[4]{0:T(128)} %owner_ref.3) | copy-start | bytes 52
  24.4 18.5 %collective-permute-start.6 = (f32[4,32,256]{2,1,0:T(8,128)S(1)}, f32[4,32,256]{2,1,0:T(8,128)S(1)}, u32[]{:S(2)}, u32[]{:S(2)}) collective-permute-start(f32[4,32,256]{2,1,0:T(8,128)S(1)} %get-tuple-element.63), channel_id=1, source_target_pairs={{0,3},{1,0},{2,1},{3,2},{4,7},{5,4},{6,5},{7,6},{8,11},{9,8},{10,9... | collective-permute-start | bytes 393224 | tf_op jit(solution)/shard_map/ppermute | solution.py:606
  25.9 17.0 %collective-permute-start.7 = (f32[4,32,256]{2,1,0:T(8,128)S(1)}, f32[4,32,256]{2,1,0:T(8,128)S(1)}, u32[]{:S(2)}, u32[]{:S(2)}) collective-permute-start(f32[4,32,256]{2,1,0:T(8,128)S(1)} %get-tuple-element.64), channel_id=1, source_target_pairs={{0,2},{1,3},{2,0},{3,1},{4,6},{5,7},{6,4},{7,5},{8,10},{9,11},{10,... | collective-permute-start | bytes 393224 | tf_op jit(solution)/shard_map/ppermute | solution.py:606
  37.7 9.6 %collective-permute-start.8 = (f32[4,32,256]{2,1,0:T(8,128)S(1)}, f32[4,32,256]{2,1,0:T(8,128)S(1)}, u32[]{:S(2)}, u32[]{:S(2)}) collective-permute-start(f32[4,32,256]{2,1,0:T(8,128)S(1)} %get-tuple-element.65), channel_id=1, source_target_pairs={{0,1},{1,2},{2,3},{3,0},{4,5},{5,6},{6,7},{7,4},{8,9},{9,10},{10,1... | collective-permute-start | bytes 393224 | tf_op jit(solution)/shard_map/ppermute | solution.py:606
  42.9 8.8 %collective-permute-start = (f32[2,256,256]{2,1,0:T(8,128)S(1)}, f32[2,256,256]{2,1,0:T(8,128)S(1)}, u32[]{:S(2)}, u32[]{:S(2)}) collective-permute-start(f32[2,256,256]{2,1,0:T(8,128)S(1)} %copy-done.18), channel_id=1, source_target_pairs={{0,4},{4,0},{8,12},{12,8},{1,5},{5,1},{9,13},{13,9},{2,6},{6,2},{1... | collective-permute-start | bytes 1572872 | tf_op jit(solution)/shard_map/ppermute | solution.py:617
  42.9 13.7 %collective-permute-start.2 = (f32[2,256,256]{2,1,0:T(8,128)S(1)}, f32[2,256,256]{2,1,0:T(8,128)S(1)}, u32[]{:S(2)}, u32[]{:S(2)}) collective-permute-start(f32[2,256,256]{2,1,0:T(8,128)S(1)} %copy-done.17), channel_id=1, source_target_pairs={{0,12},{4,8},{8,4},{12,0},{1,13},{5,9},{9,5},{13,1},{2,14},{6,10},... | collective-permute-start | bytes 1572872 | tf_op jit(solution)/shard_map/ppermute | solution.py:617
  48.1 8.5 %copy-start.16 = (f32[2,256,256]{2,1,0:T(8,128)S(1)}, f32[2,256,256]{2,1,0:T(8,128)}, u32[]{:S(2)}) copy-start(f32[2,256,256]{2,1,0:T(8,128)} %get-tuple-element.70) | copy-start | bytes 1572868
  48.1 9.2 %copy-start.15 = (f32[2,256,256]{2,1,0:T(8,128)S(1)}, f32[2,256,256]{2,1,0:T(8,128)}, u32[]{:S(2)}) copy-start(f32[2,256,256]{2,1,0:T(8,128)} %get-tuple-element.71) | copy-start | bytes 1572868
  48.1 17.3 %copy-start.9 = (bf16[4,512,256]{2,1,0:T(8,128)(2,1)S(1)}, bf16[4,512,256]{2,1,0:T(8,128)(2,1)}, u32[]{:S(2)}) copy-start(bf16[4,512,256]{2,1,0:T(8,128)(2,1)} %copy-done.8) | copy-start | bytes 3145732
  48.1 17.3 %copy-start.11 = (bf16[4,512,256]{2,1,0:T(8,128)(2,1)S(1)}, bf16[4,512,256]{2,1,0:T(8,128)(2,1)}, u32[]{:S(2)}) copy-start(bf16[4,512,256]{2,1,0:T(8,128)(2,1)} %copy-done.10) | copy-start | bytes 3145732
  48.7 8.6 %collective-permute-start.11 = (f32[4,32,256]{2,1,0:T(8,128)S(1)}, f32[4,32,256]{2,1,0:T(8,128)S(1)}, u32[]{:S(2)}, u32[]{:S(2)}) collective-permute-start(f32[4,32,256]{2,1,0:T(8,128)S(1)} %choose_slab.1.refs_0_), channel_id=1, source_target_pairs={{1,0},{2,1},{3,2},{0,3},{5,4},{6,5},{7,6},{4,7},{9,8},{10,9},{11,1... | collective-permute-start | bytes 393224 | tf_op jit(solution)/shard_map/ppermute | solution.py:601
  50.5 11.2 %collective-permute-start.12 = (f32[4,32,256]{2,1,0:T(8,128)S(1)}, f32[4,32,256]{2,1,0:T(8,128)S(1)}, u32[]{:S(2)}, u32[]{:S(2)}) collective-permute-start(f32[4,32,256]{2,1,0:T(8,128)S(1)} %choose_slab.1.refs_0_), channel_id=1, source_target_pairs={{2,0},{3,1},{0,2},{1,3},{6,4},{7,5},{4,6},{5,7},{10,8},{11,9},{8,1... | collective-permute-start | bytes 393224 | tf_op jit(solution)/shard_map/ppermute | solution.py:601
  50.5 12.8 %collective-permute-start.13 = (f32[4,32,256]{2,1,0:T(8,128)S(1)}, f32[4,32,256]{2,1,0:T(8,128)S(1)}, u32[]{:S(2)}, u32[]{:S(2)}) collective-permute-start(f32[4,32,256]{2,1,0:T(8,128)S(1)} %choose_slab.1.refs_0_), channel_id=1, source_target_pairs={{3,0},{0,1},{1,2},{2,3},{7,4},{4,5},{5,6},{6,7},{11,8},{8,9},{9,10... | collective-permute-start | bytes 393224 | tf_op jit(solution)/shard_map/ppermute | solution.py:601
  51.7 13.7 %copy-start.20 = (f32[2,256,256]{2,1,0:T(8,128)}, f32[2,256,256]{2,1,0:T(8,128)S(1)}, u32[]{:S(2)}) copy-start(f32[2,256,256]{2,1,0:T(8,128)S(1)} %collective-permute-done.refs_1_) | copy-start | bytes 1572868
  51.7 12.1 %collective-permute-start.14 = (f32[4,32,256]{2,1,0:T(8,128)S(1)}, f32[4,32,256]{2,1,0:T(8,128)S(1)}, u32[]{:S(2)}, u32[]{:S(2)}) collective-permute-start(f32[4,32,256]{2,1,0:T(8,128)S(1)} %choose_slab.1.refs_0_), channel_id=1, source_target_pairs={{0,16},{16,0},{1,17},{17,1},{2,18},{18,2},{3,19},{19,3},{4,20},{20... | collective-permute-start | bytes 393224 | tf_op jit(solution)/shard_map/ppermute | solution.py:651
  56.6 8.7 %copy-start.23 = (f32[2,256,256]{2,1,0:T(8,128)}, f32[2,256,256]{2,1,0:T(8,128)S(1)}, u32[]{:S(2)}) copy-start(f32[2,256,256]{2,1,0:T(8,128)S(1)} %collective-permute-done.2.refs_3_) | copy-start | bytes 1572868
  56.6 16.1 %collective-permute-start.18 = (f32[2,256,256]{2,1,0:T(8,128)S(1)}, f32[2,256,256]{2,1,0:T(8,128)S(1)}, u32[]{:S(2)}, u32[]{:S(2)}) collective-permute-start(f32[2,256,256]{2,1,0:T(8,128)S(1)} %copy-done.16), channel_id=1, source_target_pairs={{0,4},{4,0},{8,12},{12,8},{1,5},{5,1},{9,13},{13,9},{2,6},{6,2},{1... | collective-permute-start | bytes 1572872 | tf_op jit(solution)/shard_map/ppermute | solution.py:617
  57.3 15.4 %collective-permute-start.19 = (f32[2,256,256]{2,1,0:T(8,128)S(1)}, f32[2,256,256]{2,1,0:T(8,128)S(1)}, u32[]{:S(2)}, u32[]{:S(2)}) collective-permute-start(f32[2,256,256]{2,1,0:T(8,128)S(1)} %copy-done.15), channel_id=1, source_target_pairs={{0,12},{4,8},{8,4},{12,0},{1,13},{5,9},{9,5},{13,1},{2,14},{6,10},... | collective-permute-start | bytes 1572872 | tf_op jit(solution)/shard_map/ppermute | solution.py:617
  61.8 7.3 %collective-permute-start.15 = (f32[4,32,256]{2,1,0:T(8,128)S(1)}, f32[4,32,256]{2,1,0:T(8,128)S(1)}, u32[]{:S(2)}, u32[]{:S(2)}) collective-permute-start(f32[4,32,256]{2,1,0:T(8,128)S(1)} %collective-permute-done.11.refs_1_), channel_id=1, source_target_pairs={{0,16},{16,0},{1,17},{17,1},{2,18},{18,2},{3,19},{19,3},{4,20},{20... | collective-permute-start | bytes 393224 | tf_op jit(solution)/shard_map/ppermute | solution.py:651
  63.3 7.2 %collective-permute-start.16 = (f32[4,32,256]{2,1,0:T(8,128)S(1)}, f32[4,32,256]{2,1,0:T(8,128)S(1)}, u32[]{:S(2)}, u32[]{:S(2)}) collective-permute-start(f32[4,32,256]{2,1,0:T(8,128)S(1)} %collective-permute-done.12.refs_2_), channel_id=1, source_target_pairs={{0,16},{16,0},{1,17},{17,1},{2,18},{18,2},{3,19},{19,3},{4,20},{20... | collective-permute-start | bytes 393224 | tf_op jit(solution)/shard_map/ppermute | solution.py:651
  63.8 8.1 %collective-permute-start.17 = (f32[4,32,256]{2,1,0:T(8,128)S(1)}, f32[4,32,256]{2,1,0:T(8,128)S(1)}, u32[]{:S(2)}, u32[]{:S(2)}) collective-permute-start(f32[4,32,256]{2,1,0:T(8,128)S(1)} %collective-permute-done.13.refs_3_), channel_id=1, source_target_pairs={{0,16},{16,0},{1,17},{17,1},{2,18},{18,2},{3,19},{19,3},{4,20},{20... | collective-permute-start | bytes 393224 | tf_op jit(solution)/shard_map/ppermute | solution.py:651
  69.0 16.0 %collective-permute-start.23 = (f32[128,1024]{1,0:T(8,128)}, f32[128,1024]{1,0:T(8,128)}, u32[]{:S(2)}, u32[]{:S(2)}) collective-permute-start(f32[128,1024]{1,0:T(8,128)} %late_first.1.refs_6_.a_ref), channel_id=1, source_target_pairs={{0,1},{1,0},{2,3},{3,2},{4,5},{5,4},{6,7},{7,6},{8,9},{9,8},{10,11... | collective-permute-start | bytes 1572872 | tf_op jit(solution)/shard_map/ppermute | solution.py:611
  77.3 10.6 %copy-start.25 = (f32[2,256,256]{2,1,0:T(8,128)S(1)}, f32[2,256,256]{2,1,0:T(8,128)}, u32[]{:S(2)}) copy-start(f32[2,256,256]{2,1,0:T(8,128)} %get-tuple-element.73) | copy-start | bytes 1572868
  77.4 10.6 %copy-start.24 = (f32[2,256,256]{2,1,0:T(8,128)S(1)}, f32[2,256,256]{2,1,0:T(8,128)}, u32[]{:S(2)}) copy-start(f32[2,256,256]{2,1,0:T(8,128)} %get-tuple-element.74) | copy-start | bytes 1572868
  77.4 12.1 %copy-start.21 = (f32[2,256,256]{2,1,0:T(8,128)S(1)}, f32[2,256,256]{2,1,0:T(8,128)}, u32[]{:S(2)}) copy-start(f32[2,256,256]{2,1,0:T(8,128)} %get-tuple-element.75) | copy-start | bytes 1572868
  84.9 14.1 %copy-start.31 = (f32[2,128,256]{2,1,0:T(8,128)S(1)}, f32[2,128,256]{2,1,0:T(8,128)}, u32[]{:S(2)}) copy-start(f32[2,128,256]{2,1,0:T(8,128)} %get-tuple-element.83) | copy-start | bytes 786436
  84.9 15.7 %copy-start.30 = (f32[2,128,256]{2,1,0:T(8,128)S(1)}, f32[2,128,256]{2,1,0:T(8,128)}, u32[]{:S(2)}) copy-start(f32[2,128,256]{2,1,0:T(8,128)} %get-tuple-element.84) | copy-start | bytes 786436
  84.9 12.7 %collective-permute-start.31 = (f32[2,256,256]{2,1,0:T(8,128)S(1)}, f32[2,256,256]{2,1,0:T(8,128)S(1)}, u32[]{:S(2)}, u32[]{:S(2)}) collective-permute-start(f32[2,256,256]{2,1,0:T(8,128)S(1)} %get-tuple-element.87), channel_id=1, source_target_pairs={{0,1},{1,0},{2,3},{3,2},{4,5},{5,4},{6,7},{7,6},{8,9},{9,8},{10,11... | collective-permute-start | bytes 1572872 | tf_op jit(solution)/shard_map/ppermute | solution.py:611
  86.3 12.7 %collective-permute-start.24 = (f32[128,1024]{1,0:T(8,128)S(1)}, f32[128,1024]{1,0:T(8,128)S(1)}, u32[]{:S(2)}, u32[]{:S(2)}) collective-permute-start(f32[128,1024]{1,0:T(8,128)S(1)} %late_second.1.a_ref), channel_id=1, source_target_pairs={{0,16},{16,0},{1,17},{17,1},{2,18},{18,2},{3,19},{19,3},{4,20},{20... | collective-permute-start | bytes 1572872 | tf_op jit(solution)/shard_map/ppermute | solution.py:611
  87.9 12.7 %collective-permute-start.20 = (f32[2,256,256]{2,1,0:T(8,128)S(1)}, f32[2,256,256]{2,1,0:T(8,128)S(1)}, u32[]{:S(2)}, u32[]{:S(2)}) collective-permute-start(f32[2,256,256]{2,1,0:T(8,128)S(1)} %copy-done.25), channel_id=1, source_target_pairs={{0,4},{4,0},{8,12},{12,8},{1,5},{5,1},{9,13},{13,9},{2,6},{6,2},{1... | collective-permute-start | bytes 1572872 | tf_op jit(solution)/shard_map/ppermute | solution.py:617
  87.9 14.8 %collective-permute-start.21 = (f32[2,256,256]{2,1,0:T(8,128)S(1)}, f32[2,256,256]{2,1,0:T(8,128)S(1)}, u32[]{:S(2)}, u32[]{:S(2)}) collective-permute-start(f32[2,256,256]{2,1,0:T(8,128)S(1)} %copy-done.24), channel_id=1, source_target_pairs={{0,8},{4,12},{8,0},{12,4},{1,9},{5,13},{9,1},{13,5},{2,10},{6,14},... | collective-permute-start | bytes 1572872 | tf_op jit(solution)/shard_map/ppermute | solution.py:617
  89.5 23.5 %collective-permute-start.22 = (f32[2,256,256]{2,1,0:T(8,128)S(1)}, f32[2,256,256]{2,1,0:T(8,128)S(1)}, u32[]{:S(2)}, u32[]{:S(2)}) collective-permute-start(f32[2,256,256]{2,1,0:T(8,128)S(1)} %copy-done.21), channel_id=1, source_target_pairs={{0,12},{4,8},{8,4},{12,0},{1,13},{5,9},{9,5},{13,1},{2,14},{6,10},... | collective-permute-start | bytes 1572872 | tf_op jit(solution)/shard_map/ppermute | solution.py:617
  97.6 23.1 %collective-permute-start.28 = (f32[2,128,256]{2,1,0:T(8,128)}, f32[2,128,256]{2,1,0:T(8,128)S(1)}, u32[]{:S(2)}, u32[]{:S(2)}) collective-permute-start(f32[2,128,256]{2,1,0:T(8,128)} %get-tuple-element.82), channel_id=1, source_target_pairs={{0,4},{4,0},{8,12},{12,8},{1,5},{5,1},{9,13},{13,9},{2,6},{6,2},{1... | collective-permute-start | bytes 786440 | tf_op jit(solution)/shard_map/ppermute | solution.py:617
  99.0 22.9 %collective-permute-start.29 = (f32[2,128,256]{2,1,0:T(8,128)S(1)}, f32[2,128,256]{2,1,0:T(8,128)S(1)}, u32[]{:S(2)}, u32[]{:S(2)}) collective-permute-start(f32[2,128,256]{2,1,0:T(8,128)S(1)} %copy-done.31), channel_id=1, source_target_pairs={{0,8},{4,12},{8,0},{12,4},{1,9},{5,13},{9,1},{13,5},{2,10},{6,14},... | collective-permute-start | bytes 786440 | tf_op jit(solution)/shard_map/ppermute | solution.py:617
  100.6 13.9 %copy-start.26 = (f32[2,256,256]{2,1,0:T(8,128)}, f32[2,256,256]{2,1,0:T(8,128)S(1)}, u32[]{:S(2)}) copy-start(f32[2,256,256]{2,1,0:T(8,128)S(1)} %collective-permute-done.20.refs_4_) | copy-start | bytes 1572868
  100.6 23.7 %collective-permute-start.30 = (f32[2,128,256]{2,1,0:T(8,128)S(1)}, f32[2,128,256]{2,1,0:T(8,128)S(1)}, u32[]{:S(2)}, u32[]{:S(2)}) collective-permute-start(f32[2,128,256]{2,1,0:T(8,128)S(1)} %copy-done.30), channel_id=1, source_target_pairs={{0,12},{4,8},{8,4},{12,0},{1,13},{5,9},{9,5},{13,1},{2,14},{6,10},... | collective-permute-start | bytes 786440 | tf_op jit(solution)/shard_map/ppermute | solution.py:617
  102.7 11.8 %copy-start.27 = (f32[2,256,256]{2,1,0:T(8,128)}, f32[2,256,256]{2,1,0:T(8,128)S(1)}, u32[]{:S(2)}) copy-start(f32[2,256,256]{2,1,0:T(8,128)S(1)} %collective-permute-done.21.refs_5_) | copy-start | bytes 1572868
  102.7 34.5 %collective-permute-start.25 = (f32[2,128,256]{2,1,0:T(8,128)}, f32[2,128,256]{2,1,0:T(8,128)}, u32[]{:S(2)}, u32[]{:S(2)}) collective-permute-start(f32[2,128,256]{2,1,0:T(8,128)} %get-tuple-element.78), channel_id=1, source_target_pairs={{0,4},{4,0},{8,12},{12,8},{1,5},{5,1},{9,13},{13,9},{2,6},{6,2},{1... | collective-permute-start | bytes 786440 | tf_op jit(solution)/shard_map/ppermute | solution.py:617
  113.0 1.5 copy-start.28
  113.0 24.2 %collective-permute-start.26 = (f32[2,128,256]{2,1,0:T(8,128)}, f32[2,128,256]{2,1,0:T(8,128)}, u32[]{:S(2)}, u32[]{:S(2)}) collective-permute-start(f32[2,128,256]{2,1,0:T(8,128)} %get-tuple-element.79), channel_id=1, source_target_pairs={{0,8},{4,12},{8,0},{12,4},{1,9},{5,13},{9,1},{13,5},{2,10},{6,14},... | collective-permute-start | bytes 786440 | tf_op jit(solution)/shard_map/ppermute | solution.py:617
  114.5 6.2 %copy-start.29 = (f32[2,128,256]{2,1,0:T(8,128)S(1)}, f32[2,128,256]{2,1,0:T(8,128)}, u32[]{:S(2)}) copy-start(f32[2,128,256]{2,1,0:T(8,128)} %get-tuple-element.80) | copy-start | bytes 786436
  120.7 3.6 %copy-start.32 = (f32[2,128,256]{2,1,0:T(8,128)}, f32[2,128,256]{2,1,0:T(8,128)S(1)}, u32[]{:S(2)}) copy-start(f32[2,128,256]{2,1,0:T(8,128)S(1)} %collective-permute-done.28.refs_4_) | copy-start | bytes 786436
  120.7 16.5 %collective-permute-start.27 = (f32[2,128,256]{2,1,0:T(8,128)S(1)}, f32[2,128,256]{2,1,0:T(8,128)S(1)}, u32[]{:S(2)}, u32[]{:S(2)}) collective-permute-start(f32[2,128,256]{2,1,0:T(8,128)S(1)} %copy-done.29), channel_id=1, source_target_pairs={{0,12},{4,8},{8,4},{12,0},{1,13},{5,9},{9,5},{13,1},{2,14},{6,10},... | collective-permute-start | bytes 786440 | tf_op jit(solution)/shard_map/ppermute | solution.py:617
  121.9 2.4 %copy-start.33 = (f32[2,128,256]{2,1,0:T(8,128)}, f32[2,128,256]{2,1,0:T(8,128)S(1)}, u32[]{:S(2)}) copy-start(f32[2,128,256]{2,1,0:T(8,128)S(1)} %collective-permute-done.29.refs_5_) | copy-start | bytes 786436
  121.9 14.6 %collective-permute-start.32 = (f32[256,256]{1,0:T(8,128)S(1)}, f32[256,256]{1,0:T(8,128)S(1)}, u32[]{:S(2)}, u32[]{:S(2)}) collective-permute-start(f32[256,256]{1,0:T(8,128)S(1)} %get-tuple-element.89), channel_id=1, source_target_pairs={{0,2},{1,3},{2,0},{3,1},{4,6},{5,7},{6,4},{7,5},{8,10},{9,11},{10,... | collective-permute-start | bytes 786440 | tf_op jit(solution)/shard_map/ppermute | solution.py:611
  129.2 13.9 %collective-permute-start.34 = (f32[2,128,256]{2,1,0:T(8,128)S(1)}, f32[2,128,256]{2,1,0:T(8,128)S(1)}, u32[]{:S(2)}, u32[]{:S(2)}) collective-permute-start(f32[2,128,256]{2,1,0:T(8,128)S(1)} %get-tuple-element.92), channel_id=1, source_target_pairs={{0,1},{1,0},{2,3},{3,2},{4,5},{5,4},{6,7},{7,6},{8,9},{9,8},{10,11... | collective-permute-start | bytes 786440 | tf_op jit(solution)/shard_map/ppermute | solution.py:611
  138.0 4.4 %copy-start.1 = (f32[256,256]{1,0:T(8,128)S(1)}, f32[256,256]{1,0:T(8,128)}, u32[]{:S(2)}) copy-start(f32[256,256]{1,0:T(8,128)} %copy-done) | copy-start | bytes 786436
  142.2 7.2 %collective-permute-start.36 = (f32[2,128,256]{2,1,0:T(8,128)S(1)}, f32[2,128,256]{2,1,0:T(8,128)S(1)}, u32[]{:S(2)}, u32[]{:S(2)}) collective-permute-start(f32[2,128,256]{2,1,0:T(8,128)S(1)} %get-tuple-element.96), channel_id=1, source_target_pairs={{0,1},{1,0},{2,3},{3,2},{4,5},{5,4},{6,7},{7,6},{8,9},{9,8},{10,11... | collective-permute-start | bytes 786440 | tf_op jit(solution)/shard_map/ppermute | solution.py:611
  142.4 26.5 %collective-permute-start.33 = (f32[256,256]{1,0:T(8,128)S(1)}, f32[256,256]{1,0:T(8,128)S(1)}, u32[]{:S(2)}, u32[]{:S(2)}) collective-permute-start(f32[256,256]{1,0:T(8,128)S(1)} %copy-done.1), channel_id=1, source_target_pairs={{0,0},{1,4},{2,8},{3,12},{4,5},{5,1},{6,13},{7,9},{8,10},{9,14},{1... | collective-permute-start | bytes 786440 | tf_op jit(solution)/shard_map/ppermute | solution.py:677
  143.1 25.8 %collective-permute-start.35 = (f32[128,256]{1,0:T(8,128)S(1)}, f32[128,256]{1,0:T(8,128)S(1)}, u32[]{:S(2)}, u32[]{:S(2)}) collective-permute-start(f32[128,256]{1,0:T(8,128)S(1)} %get-tuple-element.94), channel_id=1, source_target_pairs={{0,2},{1,3},{2,0},{3,1},{4,6},{5,7},{6,4},{7,5},{8,10},{9,11},{10,... | collective-permute-start | bytes 393224 | tf_op jit(solution)/shard_map/ppermute | solution.py:611
  149.5 20.8 %collective-permute-start.37 = (f32[128,256]{1,0:T(8,128)S(1)}, f32[128,256]{1,0:T(8,128)S(1)}, u32[]{:S(2)}, u32[]{:S(2)}) collective-permute-start(f32[128,256]{1,0:T(8,128)S(1)} %get-tuple-element.98), channel_id=1, source_target_pairs={{0,2},{1,3},{2,0},{3,1},{4,6},{5,7},{6,4},{7,5},{8,10},{9,11},{10,... | collective-permute-start | bytes 393224 | tf_op jit(solution)/shard_map/ppermute | solution.py:611
  (13 other events, 10.3 us)
